TPU v7x, 32 devices: a whole 2x2x4 slice. The times are simulated.
32 devices in a mesh: seq: 8 (over z, y), head: 4 (over x, core).
Axes of the slice: x: 2, y: 2, z: 4, core: 2. Of those that a mesh axis runs over, the one named last changes fastest.
Arguments:
- query_rows: bfloat16 [6144, 2048], P('seq', 'head'), may hold values from -6 to 6
- key_rows: bfloat16 [6144, 2048], P('seq', 'head'), may hold values from -6 to 6
- value_rows: bfloat16 [6144, 2048], P('seq', 'head'), may hold values from -6 to 6
- output_rows: bfloat16 [6144, 2048], P('seq', 'head'), may hold values from -6 to 6
- output_grad: bfloat16 [6144, 2048], P('seq', 'head'), may hold values from -6 to 6
- projection: bfloat16 [3, 2048, 3072], P(None, 'head'), may hold values from -0.078125 to 0.078125
- neighbours: int32 [16, 4], replicated, may hold values from 0 to 15, as said below
- counts: int32 [16], replicated, may hold values from 3 to 4, as said below
Outputs:
- input_grad: bfloat16 [6144, 3072], P('seq', 'head')
Inputs may be any that keep to these rules, and one draw needn't show every extreme that they name: `neighbours`: row t lists 4 different tiles: first t itself, then t - 1, then t + 1 (modulo 16); the others lie among tiles (t // 2 - 1) * 2 to (t // 2 + 2) * 2 - 1, taken modulo 16. `counts`: every tile uses at least its first three listed tiles; some tile uses all 4.
All inputs are finite; a program needn't handle non-finite values.
Results may differ from a plain program's by a relative error of at most 0.015.
Values may be sent and summed in bfloat16 or wider, within the bound.
A program may use at most 128 MiB of HBM per device.

v0:
```python
import jax
import jax.numpy as jnp
from jax import lax
from jax.sharding import PartitionSpec as P

HD = 128
TILE = 384
NB = 4


def with_halo(cells, sides, width):
    for axis, dim in sides:
        count = lax.axis_size(axis)
        head = lax.slice_in_dim(cells, 0, width, axis=dim)
        tail = lax.slice_in_dim(cells, cells.shape[dim] - width, cells.shape[dim], axis=dim)
        cells = jnp.concatenate(
            [
                lax.ppermute(tail, axis, [(i, (i + 1) % count) for i in range(count)]),
                cells,
                lax.ppermute(head, axis, [((i + 1) % count, i) for i in range(count)]),
            ],
            axis=dim,
        )
    return cells


def passed_along(block, axis, distance):
    devices = range(lax.axis_size(axis))
    route = [((i - distance) % len(devices), i) for i in devices]
    return lax.ppermute(block, axis, route)


def head_split(rows, heads_dev):
    return rows.reshape(rows.shape[0] // TILE, TILE, heads_dev, HD)


def tile_scores(query_tile, near_keys, score_scale):
    return (
        jnp.einsum("ihd,jchd->hijc", query_tile, near_keys, preferred_element_type=jnp.float32)
        * score_scale
    )


def score_grads(softmax_weights, grad_tile, near_values, delta_tile, score_scale):
    prob_grad = jnp.einsum(
        "ihd,jchd->hijc", grad_tile, near_values, preferred_element_type=jnp.float32
    )
    return (
        softmax_weights.astype(jnp.float32)
        * (prob_grad - delta_tile[:, :, None, None])
        * score_scale
    ).astype(jnp.bfloat16)


def local(
    query_rows, key_rows, value_rows, output_rows, output_grad, projection, neighbours, counts
):
    seq_count = lax.axis_size("seq")
    place = lax.axis_index("seq")
    rows_dev = query_rows.shape[0]
    tiles_dev = rows_dev // TILE
    tiles_all = tiles_dev * seq_count
    heads_dev = query_rows.shape[1] // HD
    score_scale = HD ** (-0.5)
    first_tile = (place - 1) * tiles_dev
    window = with_halo(jnp.stack([key_rows, value_rows]), (("seq", 1),), rows_dev)
    key_window = window[0].reshape(3 * tiles_dev, TILE, heads_dev, HD)
    value_window = window[1].reshape(3 * tiles_dev, TILE, heads_dev, HD)
    queries = head_split(query_rows, heads_dev)
    grads_out = head_split(output_grad, heads_dev)
    outputs = head_split(output_rows, heads_dev)
    deltas = jnp.transpose(
        jnp.sum(grads_out.astype(jnp.float32) * outputs.astype(jnp.float32), axis=-1), (0, 2, 1)
    )
    slot_range = jnp.arange(NB)
    query_grads = []
    row_peaks = []
    row_totals = []
    key_acc = jnp.zeros((3 * tiles_dev, TILE, heads_dev, HD), jnp.float32)
    value_acc = jnp.zeros((3 * tiles_dev, TILE, heads_dev, HD), jnp.float32)
    for tile_at in range(tiles_dev):
        global_tile = place * tiles_dev + tile_at
        listed = neighbours[global_tile]
        is_live = slot_range < counts[global_tile]
        slots = (listed - first_tile) % tiles_all
        near_keys = key_window[slots]
        near_values = value_window[slots]
        live_mask = is_live[None, None, :, None]
        scores = jnp.where(
            live_mask, tile_scores(queries[tile_at], near_keys, score_scale), -jnp.inf
        )
        row_peak = jnp.max(scores, axis=(2, 3))
        raised = jnp.where(live_mask, jnp.exp(scores - row_peak[:, :, None, None]), 0.0)
        row_total = jnp.sum(raised, axis=(2, 3))
        softmax_weights = (raised / row_total[:, :, None, None]).astype(jnp.bfloat16)
        score_grad = score_grads(
            softmax_weights, grads_out[tile_at], near_values, deltas[tile_at], score_scale
        )
        query_grads.append(
            jnp.einsum(
                "hijc,jchd->ihd", score_grad, near_keys, preferred_element_type=jnp.float32
            ).astype(jnp.bfloat16)
        )
        row_peaks.append(row_peak)
        row_totals.append(row_total)
        key_acc = key_acc.at[slots].add(
            jnp.einsum(
                "hijc,ihd->jchd", score_grad, queries[tile_at], preferred_element_type=jnp.float32
            )
        )
        value_acc = value_acc.at[slots].add(
            jnp.einsum(
                "hijc,ihd->jchd",
                softmax_weights,
                grads_out[tile_at],
                preferred_element_type=jnp.float32,
            )
        )
    partials = jnp.stack([key_acc, value_acc])
    from_next = passed_along(partials[:, :tiles_dev].astype(jnp.bfloat16), "seq", -1).astype(
        jnp.float32
    )
    from_prev = passed_along(partials[:, 2 * tiles_dev :].astype(jnp.bfloat16), "seq", 1).astype(
        jnp.float32
    )
    owned = partials[:, tiles_dev : 2 * tiles_dev] + from_next + from_prev
    key_grads = owned[0].astype(jnp.bfloat16).reshape(rows_dev, heads_dev * HD)
    value_grads = owned[1].astype(jnp.bfloat16).reshape(rows_dev, heads_dev * HD)
    grad_stack = jnp.stack(
        [jnp.stack(query_grads).reshape(rows_dev, heads_dev * HD), key_grads, value_grads]
    )
    term = jnp.einsum("cik,ckm->im", grad_stack, projection, preferred_element_type=jnp.float32)
    return lax.psum_scatter(term.astype(jnp.bfloat16), "head", scatter_dimension=1, tiled=True)


def solution(mesh):
    in_specs = (
        P("seq", "head"),
        P("seq", "head"),
        P("seq", "head"),
        P("seq", "head"),
        P("seq", "head"),
        P(None, "head", None),
        P(),
        P(),
    )
    out_specs = P("seq", "head")
    return jax.shard_map(local, mesh=mesh, in_specs=in_specs, out_specs=out_specs, check_vma=False)
```

profile of v0, /device:TPU:0, one launch (start us, length us, event | category | flops | bytes accessed | tf_op | source)
XLA Modules:
  0.0 326.5 jit_solution(6907447338536314563)
XLA Ops:
  6.5 2.8 pad_maximum_fusion.2
  9.3 3.0 collective-permute-start
  12.3 3.0 collective-permute-start.1
  23.4 2.1 copy.141
  28.3 51.6 %collective-permute-done = bf16[2,768,512]{2,1,0:T(8,128)(2,1)} collective-permute-done((bf16[2,768,512]{2,1,0:T(8,128)(2,1)}, bf16[2,768,512]{2,1,0:T(8,128)(2,1)}, u32[]{:S(2)}, u32[]{:S(2)}) %collective-permute-start) | collective-permute-done | bytes 1572896 | tf_op jit(solution)/shard_map/ppermute | solution.py:18
  79.9 2.2 collective-permute-done.1
  82.1 2.5 pad_maximum_fusion.1
  86.4 2.1 reshape_squeeze.6
  88.5 2.2 copy.77
  90.7 5.3 %reshape_squeeze.7 = bf16[6,384,4,128]{3,2,1,0:T(4,128)(2,1)} reshape(bf16[1,2304,512]{2,1,0:T(8,128)(2,1)} %get-tuple-element.9) | data formatting | bytes 4718592 | tf_op jit(solution)/shard_map/reshape;squeeze | solution.py:68
  96.0 3.6 %copy.81 = bf16[6,384,4,128]{3,1,2,0:T(8,128)(2,1)} copy(bf16[6,384,4,128]{3,2,1,0:T(4,128)(2,1)} %reshape_squeeze.7) | data formatting | bytes 4718592 | tf_op jit(solution)/shard_map/reshape;squeeze | solution.py:68
  101.5 3.6 %gather_fusion.3 = bf16[4,384,4,128]{3,1,2,0:T(8,128)(2,1)} fusion(bf16[6,384,4,128]{3,1,2,0:T(8,128)(2,1)} %copy.81, s32[1024]{0:T(1024)S(1)} %pad_clamp_fusion), kind=kCustom, calls=%fused_computation.3 | custom fusion | bytes 3145744 | tf_op jit(solution)/shard_map/gather | solution.py:87
  105.1 2.0 gather_fusion
  107.0 3.6 %gather_fusion.1 = bf16[4,384,4,128]{3,1,2,0:T(8,128)(2,1)} fusion(bf16[6,384,4,128]{3,1,2,0:T(8,128)(2,1)} %copy.81, s32[1024]{0:T(1024)S(1)} %pad_clamp_fusion.1), kind=kCustom, calls=%fused_computation.1 | custom fusion | bytes 3145744 | tf_op jit(solution)/shard_map/gather | solution.py:87
  110.7 2.8 bitcast_reduce_fusion
  113.5 2.2 fusion.10
  115.7 2.6 divide_convert_fusion
  119.7 2.2 fusion.9
  122.0 2.8 divide_convert_fusion.1
  141.3 2.6 broadcast.160.clone.1
  143.9 7.6 %scatter_fusion.2 = f32[6,384,4,128]{3,1,2,0:T(8,128)} fusion(f32[6,384,4,128]{3,1,2,0:T(8,128)} %broadcast.160.clone.1, s32[4]{0:T(128)S(1)} %get-tuple-element.25, f32[4,384,4,128]{3,1,2,0:T(8,128)} %copy.105), kind=kCustom, calls=%fused_computation.6 | custom fusion | flops 786432 | bytes 9437200 | tf_op jit(solution)/shard_map/scatter-add | solution.py:111
  151.5 6.6 %scatter_fusion.3 = f32[6,384,4,128]{3,1,2,0:T(8,128)} fusion(f32[6,384,4,128]{3,1,2,0:T(8,128)} %scatter_fusion.2, s32[4]{0:T(128)S(1)} %get-tuple-element.26, f32[4,384,4,128]{3,1,2,0:T(8,128)S(1)} %copy.107), kind=kCustom, calls=%fused_computation.7 | custom fusion | flops 786432 | bytes 9437200 | tf_op jit(solution)/shard_map/scatter-add | solution.py:111
  158.1 2.8 broadcast.160.clone
  160.9 8.0 %scatter_fusion = f32[6,384,4,128]{3,1,2,0:T(8,128)} fusion(f32[6,384,4,128]{3,1,2,0:T(8,128)} %broadcast.160.clone, s32[4]{0:T(128)S(1)} %get-tuple-element.25, f32[4,384,4,128]{3,1,2,0:T(8,128)} %copy.101), kind=kCustom, calls=%fused_computation.4 | custom fusion | flops 786432 | bytes 9437200 | tf_op jit(solution)/shard_map/scatter-add | solution.py:106
  168.9 6.6 %scatter_fusion.1 = f32[6,384,4,128]{3,1,2,0:T(8,128)} fusion(f32[6,384,4,128]{3,1,2,0:T(8,128)} %scatter_fusion, s32[4]{0:T(128)S(1)} %get-tuple-element.26, f32[4,384,4,128]{3,1,2,0:T(8,128)S(1)} %copy-done), kind=kCustom, calls=%fused_computation.5 | custom fusion | flops 786432 | bytes 9437200 | tf_op jit(solution)/shard_map/scatter-add | solution.py:106
  175.4 4.7 %fusion = bf16[2,6,384,4,128]{4,2,3,1,0:T(8,128)(2,1)S(1)} fusion(f32[1,6,384,4,128]{4,2,3,1,0:T(8,128)} %bitcast.124, f32[1,6,384,4,128]{4,2,3,1,0:T(8,128)} %bitcast.122), kind=kLoop, calls=%fused_computation.11 | loop fusion | flops 2359296 | bytes 14155776 | tf_op jit(solution)/shard_map/convert.3
  182.0 3.4 %collective-permute-start.2 = (bf16[2,2,384,4,128]{4,2,3,1,0:T(8,128)(2,1)}, bf16[2,2,384,4,128]{4,2,3,1,0:T(8,128)(2,1)S(1)}, u32[]{:S(2)}, u32[]{:S(2)}) collective-permute-start(bf16[2,2,384,4,128]{4,2,3,1,0:T(8,128)(2,1)} %get-tuple-element.7), channel_id=1, source_target_pairs={{4,0},{8,4},{12,8},{16,12},{20,16},{24,20},{28,24},{0,28},{5,1},{9... | collective-permute-start | bytes 4718600 | tf_op jit(solution)/shard_map/ppermute | solution.py:30
  185.4 3.4 %fusion.45 = bf16[1,384,4,128]{1,3,2,0:T(8,128)(2,1)S(1)} fusion(bf16[4,384,4,128]{3,1,2,0:T(8,128)(2,1)S(1)} %copy-done.1, bf16[4,384,4,384]{1,3,2,0:T(8,128)(2,1)} %copy-done.4), kind=kOutput, calls=%fused_computation.64 | convolution fusion | flops 604176384 | bytes 6684672 | tf_op jit(solution)/shard_map/hijc,jchd->ihd/dot_general | solution.py:100
  191.8 59.1 %collective-permute-done.2 = bf16[2,2,384,4,128]{4,2,3,1,0:T(8,128)(2,1)S(1)} collective-permute-done((bf16[2,2,384,4,128]{4,2,3,1,0:T(8,128)(2,1)}, bf16[2,2,384,4,128]{4,2,3,1,0:T(8,128)(2,1)S(1)}, u32[]{:S(2)}, u32[]{:S(2)}) %collective-permute-start.2) | collective-permute-done | bytes 1572896 | tf_op jit(solution)/shard_map/ppermute | solution.py:30
  251.0 2.9 fusion.18
  255.9 12.7 %bitcast_convert_fusion = bf16[768,3072]{1,0:T(8,128)(2,1)} fusion(bf16[3,512,3072]{2,1,0:T(8,128)(2,1)} %param.13, bf16[1,768,512]{2,1,0:T(8,128)(2,1)S(1)} %convert_element_type.86, bf16[1,768,512]{2,1,0:T(8,128)(2,1)S(1)} %convert_element_type.85, bf16[1,768,512]{2,1,0:T(8,128)(2,1)S(1)} %copy-done.14), kind=kOutput, calls=%fused_computation.12 | convolution fusion | flops 7252475904 | bytes 16515072 | tf_op jit(solution)/shard_map/cik,ckm->im/dot_general | solution.py:132
  268.6 50.7 %reduce-scatter.2.cloned.1.call-done = bf16[768,768]{1,0:T(8,128)(2,1)} async-done(((bf16[768,3072]{1,0:T(8,128)(2,1)}), bf16[768,768]{1,0:T(8,128)(2,1)}) %reduce-scatter.2.cloned.1.call-update) | async-done | bytes 1179664 | tf_op jit(solution)/shard_map/reduce_scatter | solution.py:133
  (86 shorter events, 39.2 us)
Async XLA Ops:
  6.5 10.9 %copy-start.9 = (bf16[768,512]{1,0:T(8,128)(2,1)S(1)}, bf16[768,512]{1,0:T(8,128)(2,1)}, u32[]{:S(2)}) copy-start(bf16[768,512]{1,0:T(8,128)(2,1)} %param.12) | copy-start | bytes 2359300
  6.5 312.7 %reduce-scatter.2.cloned.1.call-start = ((), (), s32[]{:S(2)}) async-start(), calls=%async_computation.1 | async-start | bytes 5898240 | tf_op jit(solution)/shard_map/reduce_scatter | solution.py:133
  9.3 70.6 %collective-permute-start = (bf16[2,768,512]{2,1,0:T(8,128)(2,1)}, bf16[2,768,512]{2,1,0:T(8,128)(2,1)}, u32[]{:S(2)}, u32[]{:S(2)}) collective-permute-start(bf16[2,768,512]{2,1,0:T(8,128)(2,1)} %pad_maximum_fusion.2), channel_id=1, source_target_pairs={{0,4},{4,8},{8,12},{12,16},{16,20},{20,24},{24,28},{28,0},{1,5},{5... | collective-permute-start | bytes 4718600 | tf_op jit(solution)/shard_map/ppermute | solution.py:18
  12.3 69.9 %collective-permute-start.1 = (bf16[2,768,512]{2,1,0:T(8,128)(2,1)}, bf16[2,768,512]{2,1,0:T(8,128)(2,1)}, u32[]{:S(2)}, u32[]{:S(2)}) collective-permute-start(bf16[2,768,512]{2,1,0:T(8,128)(2,1)} %pad_maximum_fusion.2), channel_id=1, source_target_pairs={{4,0},{8,4},{12,8},{16,12},{20,16},{24,20},{28,24},{0,28},{5,1},{9... | collective-permute-start | bytes 4718600 | tf_op jit(solution)/shard_map/ppermute | solution.py:20
  20.6 5.6 %copy-start.17 = (s32[16]{0:T(128)S(1)}, s32[16]{0:T(128)}, u32[]{:S(2)}) copy-start(s32[16]{0:T(128)} %param.15) | copy-start | bytes 196
  20.6 6.2 %copy-start.15 = (s32[16,4]{0,1:T(4,128)S(1)}, s32[16,4]{0,1:T(4,128)}, u32[]{:S(2)}) copy-start(s32[16,4]{0,1:T(4,128)} %param.14) | copy-start | bytes 772
  21.1 61.0 %copy-start.8 = (bf16[768,512]{1,0:T(8,128)(2,1)S(1)}, bf16[768,512]{1,0:T(8,128)(2,1)}, u32[]{:S(2)}) copy-start(bf16[768,512]{1,0:T(8,128)(2,1)} %param.10) | copy-start | bytes 2359300
  23.4 94.9 %copy-start.6 = (bf16[384,512]{0,1:T(8,128)(2,1)}, bf16[384,512]{0,1:T(8,128)(2,1)S(1)}, u32[]{:S(2)}) copy-start(bf16[384,512]{0,1:T(8,128)(2,1)S(1)} %copy.140) | copy-start | bytes 1179652
  115.7 2.6 copy-start.2
  121.9 2.9 copy-start.10
  126.2 1.0 copy-start.11
  128.6 1.9 copy-start.13
  132.3 3.3 %copy-start.4 = (bf16[4,384,4,384]{1,3,2,0:T(8,128)(2,1)}, bf16[4,384,4,384]{1,3,2,0:T(8,128)(2,1)S(1)}, u32[]{:S(2)}) copy-start(bf16[4,384,4,384]{1,3,2,0:T(8,128)(2,1)S(1)} %fusion.2) | copy-start | bytes 14155780
  133.7 2.5 copy-start.12
  133.7 2.5 copy-start.16
  136.2 1.8 copy-start.7
  138.0 3.3 %copy-start.5 = (bf16[4,384,4,384]{1,3,2,0:T(8,128)(2,1)}, bf16[4,384,4,384]{1,3,2,0:T(8,128)(2,1)S(1)}, u32[]{:S(2)}) copy-start(bf16[4,384,4,384]{1,3,2,0:T(8,128)(2,1)S(1)} %fusion.6) | copy-start | bytes 14155780
  160.9 8.0 %copy-start = (f32[4,384,4,128]{3,1,2,0:T(8,128)S(1)}, f32[4,384,4,128]{3,1,2,0:T(8,128)}, u32[]{:S(2)}) copy-start(f32[4,384,4,128]{3,1,2,0:T(8,128)} %copy.103) | copy-start | bytes 9437188
  175.4 13.4 %slice-start = ((s8[4718592]{0:T(1024)(128)(4,1)}), s8[4194304]{0:T(1024)(128)(4,1)S(1)}, s32[]{:S(2)}) async-start(s8[4718592]{0:T(1024)(128)(4,1)} %bitcast.126), calls=%async_computation.2 | async-start | bytes 8388608
  175.4 13.4 %slice-start.1 = ((s8[4718592]{0:T(1024)(128)(4,1)}), s8[524288]{0:T(1024)(128)(4,1)S(1)}, s32[]{:S(2)}) async-start(s8[4718592]{0:T(1024)(128)(4,1)} %bitcast.126), calls=%async_computation.3 | async-start | bytes 1048576
  180.1 5.3 %copy-start.1 = (bf16[4,384,4,128]{3,1,2,0:T(8,128)(2,1)S(1)}, bf16[4,384,4,128]{3,1,2,0:T(8,128)(2,1)}, u32[]{:S(2)}) copy-start(bf16[4,384,4,128]{3,1,2,0:T(8,128)(2,1)} %gather_fusion.2) | copy-start | bytes 4718596
  182.0 6.8 %copy-start.3 = (bf16[4,384,4,128]{3,1,2,0:T(8,128)(2,1)S(1)}, bf16[4,384,4,128]{3,1,2,0:T(8,128)(2,1)}, u32[]{:S(2)}) copy-start(bf16[4,384,4,128]{3,1,2,0:T(8,128)(2,1)} %gather_fusion) | copy-start | bytes 4718596
  182.0 68.9 %collective-permute-start.2 = (bf16[2,2,384,4,128]{4,2,3,1,0:T(8,128)(2,1)}, bf16[2,2,384,4,128]{4,2,3,1,0:T(8,128)(2,1)S(1)}, u32[]{:S(2)}, u32[]{:S(2)}) collective-permute-start(bf16[2,2,384,4,128]{4,2,3,1,0:T(8,128)(2,1)} %get-tuple-element.7), channel_id=1, source_target_pairs={{4,0},{8,4},{12,8},{16,12},{20,16},{24,20},{28,24},{0,28},{5,1},{9... | collective-permute-start | bytes 4718600 | tf_op jit(solution)/shard_map/ppermute | solution.py:30
  185.4 65.5 %collective-permute-start.3 = (bf16[2,2,384,4,128]{4,2,3,1,0:T(8,128)(2,1)}, bf16[2,2,384,4,128]{4,2,3,1,0:T(8,128)(2,1)}, u32[]{:S(2)}, u32[]{:S(2)}) collective-permute-start(bf16[2,2,384,4,128]{4,2,3,1,0:T(8,128)(2,1)} %get-tuple-element.8), channel_id=1, source_target_pairs={{28,0},{0,4},{4,8},{8,12},{12,16},{16,20},{20,24},{24,28},{29,1},{... | collective-permute-start | bytes 4718600 | tf_op jit(solution)/shard_map/ppermute | solution.py:30
  253.9 2.0 copy-start.14
Sparse Core Ops, SparseCore 0:
  268.7 50.4 reduce-scatter.1
where the time goes:
time: 330 us; the launch traced here: 327 us
  waiting for transfers between devices  164 us (50%)
  other arithmetic  55.3 us (17%)
  local copies, waits for them, and re-layouts  53.5 us (16%)
  matrix products  30.4 us (9%)
  between operations  14.3 us (4%)
  starting transfers between devices  9.42 us (3%)
    ppermute x2, waiting for transfers between devices, passed_along(): return lax.ppermute(block, axis, route)  59.2 us
    ppermute x1, waiting for transfers between devices, with_halo(): lax.ppermute(tail, axis, [(i, (i + 1) % count) for i in range(count)])  51.6 us
    reduce_scatter x1, waiting for transfers between devices, local(): lax.psum_scatter(term.astype(jnp.bfloat16), 'head', scatter_dimension=1,...  50.7 us
    scatter-add x2, other arithmetic, local(): key_acc.at[slots]  14.6 us
    scatter-add x2, other arithmetic, local(): value_acc.at[slots]  14.2 us
    dot_general x1, matrix products, local(): jnp.einsum('cik,ckm->im', grad_stack, projection, preferred_element_type=...  12.7 us
    another operation x2, local copies, waits for them, and re-layouts, local(): value_window = window[1].reshape(3 * tiles_dev, TILE, heads_dev, HD)  8.91 us
    another operation x2, other arithmetic  7.55 us
  transfers between devices with their start and end apart: 5, of which 5 were waited for; matrix products, arithmetic and copies ran while one was open for 6% of the time, Pallas kernels for 0%

commit v1 on v0

v1 whole, which is shorter than its diff:
```python
import functools
import math

import jax
import jax.numpy as jnp
from jax import lax
from jax.experimental import pallas as pl
from jax.experimental.pallas import tpu as pltpu
from jax.sharding import PartitionSpec as P

HD = 128
TILE = 384
NB = 4
HALO = 2
F32 = jnp.float32
BF16 = jnp.bfloat16


def dot(a, b, dims):
    return lax.dot_general(a, b, ((dims[:1], dims[1:]), ((), ())), preferred_element_type=F32)


def attention_kernel(
    tiles, own_blocks, slots_ref, counts_ref, delta_ref, *refs
):
    qg_refs = refs[:own_blocks]
    kv_refs = refs[own_blocks : 2 * own_blocks + 2]
    query_grad_ref, prev_ref, own_ref, next_ref = refs[2 * own_blocks + 2 : 2 * own_blocks + 6]
    qg, kv, key_acc, value_acc, work = refs[2 * own_blocks + 6 :]
    rows_block = HALO * TILE
    for at, ref in enumerate(qg_refs):
        qg[at * rows_block : (at + 1) * rows_block, :] = ref[...]
    for at, ref in enumerate(kv_refs):
        kv[at * rows_block : (at + 1) * rows_block, :] = ref[...]
    key_acc[...] = jnp.zeros_like(key_acc)
    value_acc[...] = jnp.zeros_like(value_acc)
    scale = HD ** (-0.5)
    exponent = scale * math.log2(math.e)

    def tile_step(tile, slot_places):
        base = pl.multiple_of(tile * TILE, TILE)
        query = qg[pl.ds(base, TILE), :HD]
        grad = qg[pl.ds(base, TILE), HD:]
        delta = delta_ref[tile]
        starts = [pl.multiple_of(place * TILE, TILE) for place in slot_places]
        peak = None
        for j, start in enumerate(starts):
            scores = dot(kv[pl.ds(start, TILE), :HD], query, (1, 1))
            work[j] = scores
            top = jnp.max(scores, axis=0, keepdims=True)
            peak = top if peak is None else jnp.maximum(peak, top)
        total = jnp.zeros_like(peak)
        for j in range(len(starts)):
            raised = jnp.exp2((work[j] - peak) * exponent)
            work[j] = raised
            total = total + jnp.sum(raised, axis=0, keepdims=True)
        inverse = 1.0 / total
        query_grad = jnp.zeros((HD, TILE), F32)
        for j, start in enumerate(starts):
            keys = kv[pl.ds(start, TILE), :HD]
            weights = (work[j] * inverse).astype(BF16)
            prob_grad = dot(kv[pl.ds(start, TILE), HD:], grad, (1, 1))
            score_grad = (weights.astype(F32) * ((prob_grad - delta) * scale)).astype(BF16)
            value_acc[pl.ds(start, TILE), :] += dot(weights, grad, (1, 0))
            key_acc[pl.ds(start, TILE), :] += dot(score_grad, query, (1, 0))
            query_grad = query_grad + dot(keys, score_grad, (0, 0))
        query_grad_ref[pl.ds(base, TILE), :] = query_grad.T.astype(BF16)

    @pl.loop(0, tiles)
    def _(tile):
        near = [tile + HALO, tile + HALO - 1, tile + HALO + 1]

        @pl.when(counts_ref[tile] >= NB)
        def _():
            tile_step(tile, near + [slots_ref[tile * NB + NB - 1]])

        @pl.when(counts_ref[tile] < NB)
        def _():
            tile_step(tile, near)

    end = own_blocks + 1
    for half, acc in enumerate((key_acc, value_acc)):
        cols = slice(half * HD, (half + 1) * HD)
        prev_ref[:, cols] = acc[:rows_block, :].astype(BF16)
        own_ref[:, cols] = acc[rows_block : end * rows_block, :]
        next_ref[:, cols] = acc[end * rows_block :, :].astype(BF16)


def attention(slots, counts, delta, qg_blocks, kv_blocks):
    own_blocks = len(qg_blocks)
    tiles = own_blocks * HALO
    rows = tiles * TILE
    rows_block = HALO * TILE
    window = rows + 2 * rows_block
    vmem = pl.BlockSpec(memory_space=pltpu.VMEM)
    smem = pl.BlockSpec(memory_space=pltpu.SMEM)
    pair = jax.ShapeDtypeStruct((rows_block, 2 * HD), BF16)
    return pl.pallas_call(
        functools.partial(attention_kernel, tiles, own_blocks),
        out_shape=[
            jax.ShapeDtypeStruct((rows, HD), BF16),
            pair,
            jax.ShapeDtypeStruct((rows, 2 * HD), F32),
            pair,
        ],
        in_specs=[smem, smem] + [vmem] * (1 + len(qg_blocks) + len(kv_blocks)),
        out_specs=[vmem] * 4,
        scratch_shapes=[
            pltpu.VMEM((rows, 2 * HD), BF16),
            pltpu.VMEM((window, 2 * HD), BF16),
            pltpu.VMEM((window, HD), F32),
            pltpu.VMEM((window, HD), F32),
            pltpu.VMEM((NB, TILE, TILE), F32),
        ],
        compiler_params=pltpu.CompilerParams(vmem_limit_bytes=40 * 2**20),
        cost_estimate=pl.CostEstimate(
            flops=2 * 5 * rows * NB * TILE * HD * 2,
            bytes_accessed=rows * HD * 30,
            transcendentals=rows * NB * TILE,
        ),
    )(slots.reshape(-1), counts, delta.reshape(tiles, 1, TILE), *qg_blocks, *kv_blocks)


def shifted(block, axis, distance):
    count = lax.axis_size(axis)
    return lax.ppermute(block, axis, [(i, (i + distance) % count) for i in range(count)])


def swapped(block, axis, bit):
    count = lax.axis_size(axis)
    return lax.ppermute(block, axis, [(i, i ^ bit) for i in range(count)])


def head_cols(array, head):
    return lax.dynamic_slice_in_dim(array, head * HD, HD, 1)


def tables(neighbours, counts, first, tiles, tiles_all):
    ids = first + jnp.arange(tiles)
    slots = (neighbours[ids] - (first - HALO)) % tiles_all
    return slots.astype(jnp.int32), counts[ids].astype(jnp.int32)


def summed_over_heads(grads, projection):
    stack = jnp.stack(grads)
    count = lax.axis_size("head")
    if count != 4:
        term = jnp.einsum("cik,ckm->im", stack, projection, preferred_element_type=F32)
        return lax.psum_scatter(term.astype(BF16), "head", scatter_dimension=1, tiled=True)
    place = lax.axis_index("head")
    chip, core = place // 2, place % 2
    width = projection.shape[2] // count

    def chip_sum(target):
        weights = lax.dynamic_slice_in_dim(projection, target * 2 * width, 2 * width, 2)
        term = jnp.einsum("cik,ckm->im", stack, weights, preferred_element_type=F32).astype(BF16)
        sent = lax.dynamic_slice_in_dim(term, (1 - core) * width, width, 1)
        kept = lax.dynamic_slice_in_dim(term, core * width, width, 1)
        return kept.astype(F32) + swapped(sent, "head", 1).astype(F32)

    far = swapped(chip_sum(1 - chip).astype(BF16), "head", 2)
    return (chip_sum(chip) + far.astype(F32)).astype(BF16)


def local(
    query_rows, key_rows, value_rows, output_rows, output_grad, projection, neighbours, counts
):
    seq_count = lax.axis_size("seq")
    place = lax.axis_index("seq")
    rows_dev = query_rows.shape[0]
    tiles_dev = rows_dev // TILE
    tiles_all = tiles_dev * seq_count
    heads_dev = query_rows.shape[1] // HD
    deltas = jnp.sum(
        (output_grad.astype(F32) * output_rows.astype(F32)).reshape(rows_dev, heads_dev, HD), axis=-1
    ).T
    grads = ([], [], [])
    if heads_dev % 2 or seq_count % 2:
        slots, live = tables(neighbours, counts, place * tiles_dev, tiles_dev, tiles_all)
        for head in range(heads_dev):
            qg = jnp.concatenate([head_cols(query_rows, head), head_cols(output_grad, head)], 1)
            kv = jnp.concatenate([head_cols(key_rows, head), head_cols(value_rows, head)], 1)
            window = [shifted(kv, "seq", 1), kv, shifted(kv, "seq", -1)]
            query_grad, to_prev, own, to_next = attention(slots, live, deltas[head], [qg], window)
            own = (
                own + shifted(to_prev, "seq", -1).astype(F32) + shifted(to_next, "seq", 1).astype(F32)
            ).astype(BF16)
            for into, block in zip(grads, (query_grad, own[:, :HD], own[:, HD:])):
                into.append(block)
        return summed_over_heads([jnp.concatenate(blocks, 1) for blocks in grads], projection)

    odd = place % 2
    half = heads_dev // 2
    first = (place - odd) * tiles_dev
    slots, live = tables(neighbours, counts, first, 2 * tiles_dev, tiles_all)

    def in_order(mine, other):
        return jnp.where(odd == 0, mine, other), jnp.where(odd == 0, other, mine)

    delta_mine = lax.dynamic_slice_in_dim(deltas, odd * half, half, 0)
    delta_sent = lax.dynamic_slice_in_dim(deltas, (1 - odd) * half, half, 0)
    delta_pair = jnp.concatenate(in_order(delta_mine, swapped(delta_sent, "seq", 1)), 1)

    def exchanged(left, right, step):
        def both(head):
            return jnp.concatenate([head_cols(left, head), head_cols(right, head)], 1)

        return in_order(
            both(odd * half + step), swapped(both((1 - odd) * half + step), "seq", 1)
        )

    mine, other = [], []
    kv_pairs = [exchanged(key_rows, value_rows, step) for step in range(half)]
    qg_pairs = [exchanged(query_rows, output_grad, step) for step in range(half)]
    for step in range(half):
        low, high = kv_pairs[step]
        window = [shifted(high, "seq", 2), low, high, shifted(low, "seq", -2)]
        query_grad, to_prev, own, to_next = attention(
            slots, live, delta_pair[step], list(qg_pairs[step]), window
        )
        from_next = shifted(to_prev, "seq", -2)
        from_prev = shifted(to_next, "seq", 2)
        low = own[:rows_dev] + from_prev.astype(F32)
        high = own[rows_dev:] + from_next.astype(F32)
        low = jnp.concatenate([query_grad[:rows_dev], low.astype(BF16)], 1)
        high = jnp.concatenate([query_grad[rows_dev:], high.astype(BF16)], 1)
        mine.append(jnp.where(odd == 0, low, high))
        other.append(swapped(jnp.where(odd == 0, high, low), "seq", 1))
    parts = []
    for which in range(3):
        cols = slice(which * HD, (which + 1) * HD)
        first_half, second_half = in_order(
            jnp.concatenate([block[:, cols] for block in mine], 1),
            jnp.concatenate([block[:, cols] for block in other], 1),
        )
        parts.append(jnp.concatenate([first_half, second_half], 1))
    return summed_over_heads(parts, projection)


def solution(mesh):
    in_specs = (
        P("seq", "head"),
        P("seq", "head"),
        P("seq", "head"),
        P("seq", "head"),
        P("seq", "head"),
        P(None, "head", None),
        P(),
        P(),
    )
    out_specs = P("seq", "head")
    return jax.shard_map(local, mesh=mesh, in_specs=in_specs, out_specs=out_specs, check_vma=False)
```

time: 330 us -> 165 us (0.50)
  waiting for transfers between devices: 164 us -> 85.2 us
  local copies, waits for them, and re-layouts: 53.5 us -> 5.09 us
  other arithmetic: 55.3 us -> 16.2 us
  matrix products: 30.4 us -> 11 us
  starting transfers between devices: 9.42 us -> 27.8 us
  Pallas kernels: 0 us -> 18.3 us
  between operations: 14.3 us -> 0.51 us
    reduce_scatter x1 -> x0, waiting for transfers between devices: 50.7 us -> none  [local(): lax.psum_scatter(term.astype(jnp.bfloat16), 'head', scatter_dimension=1,...]
    scatter-add x4 -> x0, other arithmetic: 28.7 us -> none  [the longest x2 14.6 us: local(): key_acc.at[slots]]
    ppermute x4 -> x18, waiting for transfers between devices: 113 us -> 85.2 us  [the longest x10 65.8 us: swapped(): return lax.ppermute(block, axis, [(i, i ^ bit) for i in range(count)])]
    another operation x8 -> x0, local copies, waits for them, and re-layouts: 20.4 us -> none  [the longest x2 8.91 us: local(): value_window = window[1].reshape(3 * tiles_dev, TILE, heads_dev, HD)]
    dot_general x11 -> x2, matrix products: 30.4 us -> 11 us  [chip_sum(): jnp.einsum('cik,ckm->im', stack, weights, preferred_element_type=F32)]
    ppermute x4 -> x18, starting transfers between devices: 9.42 us -> 27.8 us  [the longest x8 16 us: shifted(): lax.ppermute(block, axis, [(i, (i + distance) % count) for i in range(cou...]
    pallas_call x0 -> x2, Pallas kernels: none -> 18.3 us  [attention(): pl.pallas_call(functools.partial(attention_kernel, tiles, own_blocks), ou...]
    another operation x4 -> x3, other arithmetic: 10.4 us -> 0.17 us  [summed_over_heads(): stack = jnp.stack(grads)]
  transfers between devices with their start and end apart: 5 -> 18, of which waited for: 5 -> 8; matrix products, arithmetic and copies ran while one was open for 6% -> 13% of each run, Pallas kernels for 0% -> 11%
where the time goes in v1:
time: 165 us; the launch traced here: 164 us
  waiting for transfers between devices  85.2 us (52%)
  starting transfers between devices  27.8 us (17%)
  Pallas kernels  18.3 us (11%)
  other arithmetic  16.2 us (10%)
  matrix products  11 us (7%)
  local copies, waits for them, and re-layouts  5.09 us (3%)
    ppermute x10, waiting for transfers between devices, swapped(): return lax.ppermute(block, axis, [(i, i ^ bit) for i in range(count)])  65.8 us
    ppermute x8, waiting for transfers between devices, shifted(): lax.ppermute(block, axis, [(i, (i + distance) % count) for i in range(cou...  19.4 us
    pallas_call x2, Pallas kernels, attention(): pl.pallas_call(functools.partial(attention_kernel, tiles, own_blocks), ou...  18.3 us
    ppermute x8, starting transfers between devices, shifted(): lax.ppermute(block, axis, [(i, (i + distance) % count) for i in range(cou...  16 us
    ppermute x10, starting transfers between devices, swapped(): return lax.ppermute(block, axis, [(i, i ^ bit) for i in range(count)])  11.8 us
    dot_general x2, matrix products, chip_sum(): jnp.einsum('cik,ckm->im', stack, weights, preferred_element_type=F32)  11 us
    select_n x7, other arithmetic, in_order(): return (jnp.where(odd == 0, mine, other), jnp.where(odd == 0, other, mine))  6.33 us
  transfers between devices with their start and end apart: 18, of which 8 were waited for; matrix products, arithmetic and copies ran while one was open for 13% of the time, Pallas kernels for 11%

profile of v1, /device:TPU:0, one launch (start us, length us, event | category | flops | bytes accessed | tf_op | source)
XLA Modules:
  0.0 164.1 jit_solution(18157480944336990654)
XLA Ops:
  0.0 1.6 convert_multiply_fusion
  3.1 0.9 dynamic-slice_bitcast_fusion
  4.0 3.0 %collective-permute-start = (f32[2,768]{0,1:T(8,128)}, f32[2,768]{0,1:T(8,128)}, u32[]{:S(2)}, u32[]{:S(2)}) collective-permute-start(f32[2,768]{0,1:T(8,128)} %dynamic-slice_bitcast_fusion), channel_id=1, source_target_pairs={{0,4},{4,0},{8,12},{12,8},{16,20},{20,16},{24,28},{28,24},{1,5},{5... | collective-permute-start | bytes 18440 | tf_op jit(solution)/shard_map/ppermute | solution.py:131
  9.7 1.6 collective-permute-start.8
  13.3 1.6 collective-permute-start.2
  17.2 1.2 bitcast_select_fusion.1
  18.7 15.3 %collective-permute-done.8 = bf16[768,256]{1,0:T(8,128)(2,1)} collective-permute-done((bf16[768,256]{1,0:T(8,128)(2,1)}, bf16[768,256]{1,0:T(8,128)(2,1)}, u32[]{:S(2)}, u32[]{:S(2)}) %collective-permute-start.8) | collective-permute-done | bytes 393248 | tf_op jit(solution)/shard_map/ppermute | solution.py:131
  34.1 1.2 broadcast_select_fusion.10
  35.3 2.2 %collective-permute-start.9 = (bf16[768,256]{1,0:T(8,128)(2,1)S(1)}, bf16[768,256]{1,0:T(8,128)(2,1)S(1)}, u32[]{:S(2)}, u32[]{:S(2)}) collective-permute-start(bf16[768,256]{1,0:T(8,128)(2,1)S(1)} %get-tuple-element.56.refs_4_), channel_id=1, source_target_pairs={{0,8},{4,12},{8,16},{12,20},{16,24},{20,28},{24,0},{28,4},{1,9},{5... | collective-permute-start | bytes 1179656 | tf_op jit(solution)/shard_map/ppermute | solution.py:126
  37.4 2.1 %collective-permute-start.10 = (bf16[768,256]{1,0:T(8,128)(2,1)S(1)}, bf16[768,256]{1,0:T(8,128)(2,1)S(1)}, u32[]{:S(2)}, u32[]{:S(2)}) collective-permute-start(bf16[768,256]{1,0:T(8,128)(2,1)S(1)} %get-tuple-element.55.refs_3_), channel_id=1, source_target_pairs={{0,24},{4,28},{8,0},{12,4},{16,8},{20,12},{24,16},{28,20},{1,25},{... | collective-permute-start | bytes 1179656 | tf_op jit(solution)/shard_map/ppermute | solution.py:126
  39.5 10.6 %collective-permute-done.2 = bf16[768,256]{1,0:T(8,128)(2,1)} collective-permute-done((bf16[768,256]{1,0:T(8,128)(2,1)}, bf16[768,256]{1,0:T(8,128)(2,1)}, u32[]{:S(2)}, u32[]{:S(2)}) %collective-permute-start.2) | collective-permute-done | bytes 393248 | tf_op jit(solution)/shard_map/ppermute | solution.py:131
  50.1 1.2 broadcast_select_fusion.14
  51.3 1.9 %collective-permute-start.3 = (bf16[768,256]{1,0:T(8,128)(2,1)S(1)}, bf16[768,256]{1,0:T(8,128)(2,1)S(1)}, u32[]{:S(2)}, u32[]{:S(2)}) collective-permute-start(bf16[768,256]{1,0:T(8,128)(2,1)S(1)} %get-tuple-element.36.refs_4_), channel_id=1, source_target_pairs={{0,8},{4,12},{8,16},{12,20},{16,24},{20,28},{24,0},{28,4},{1,9},{5... | collective-permute-start | bytes 1179656 | tf_op jit(solution)/shard_map/ppermute | solution.py:126
  53.1 2.1 %collective-permute-start.4 = (bf16[768,256]{1,0:T(8,128)(2,1)S(1)}, bf16[768,256]{1,0:T(8,128)(2,1)S(1)}, u32[]{:S(2)}, u32[]{:S(2)}) collective-permute-start(bf16[768,256]{1,0:T(8,128)(2,1)S(1)} %get-tuple-element.35.refs_3_), channel_id=1, source_target_pairs={{0,24},{4,28},{8,0},{12,4},{16,8},{20,12},{24,16},{28,20},{1,25},{... | collective-permute-start | bytes 1179656 | tf_op jit(solution)/shard_map/ppermute | solution.py:126
  55.2 1.2 broadcast_select_fusion.12
  56.4 1.2 broadcast_select_fusion.16
  57.6 9.2 %shard_map.83 = (bf16[1536,128]{1,0:T(8,128)(2,1)S(1)}, bf16[768,256]{1,0:T(8,128)(2,1)S(1)}, f32[1536,256]{1,0:T(8,128)S(1)}, bf16[768,256]{1,0:T(8,128)(2,1)S(1)}) custom-call(s32[16]{0:T(128)S(1)} %and_select_fusion.slots_ref, s32[4]{0:T(128)S(1)} %gather_fusion.1, f32[4,1,384]{2,1,0:T(1,128)S(1)} %bitcast.20, ...), custom_call_target="tpu_custom_call" | custom-call | flops 6039797760 | bytes 5898240 | tf_op jit(solution)/shard_map/pallas_call | solution.py:98
  66.8 3.8 %collective-permute-start.12 = (bf16[768,256]{1,0:T(8,128)(2,1)S(1)}, bf16[768,256]{1,0:T(8,128)(2,1)S(1)}, u32[]{:S(2)}, u32[]{:S(2)}) collective-permute-start(bf16[768,256]{1,0:T(8,128)(2,1)S(1)} %get-tuple-element.20), channel_id=1, source_target_pairs={{0,24},{4,28},{8,0},{12,4},{16,8},{20,12},{24,16},{28,20},{1,25},{... | collective-permute-start | bytes 1179656 | tf_op jit(solution)/shard_map/ppermute | solution.py:126
  70.6 8.3 %collective-permute-done.4.refs_5_ = bf16[768,256]{1,0:T(8,128)(2,1)S(1)} collective-permute-done((bf16[768,256]{1,0:T(8,128)(2,1)S(1)}, bf16[768,256]{1,0:T(8,128)(2,1)S(1)}, u32[]{:S(2)}, u32[]{:S(2)}) %collective-permute-start.4) | collective-permute-done | bytes 393248 | tf_op jit(solution)/shard_map/ppermute | solution.py:126
  78.9 9.2 %shard_map.82 = (bf16[1536,128]{1,0:T(8,128)(2,1)S(1)}, bf16[768,256]{1,0:T(8,128)(2,1)S(1)}, f32[1536,256]{1,0:T(8,128)S(1)}, bf16[768,256]{1,0:T(8,128)(2,1)S(1)}) custom-call(s32[16]{0:T(128)S(1)} %and_select_fusion.slots_ref, s32[4]{0:T(128)S(1)} %gather_fusion.1, f32[4,1,384]{2,1,0:T(1,128)S(1)} %bitcast.19, ...), custom_call_target="tpu_custom_call" | custom-call | flops 6039797760 | bytes 5898240 | tf_op jit(solution)/shard_map/pallas_call | solution.py:98
  88.2 3.8 %collective-permute-start.6 = (bf16[768,256]{1,0:T(8,128)(2,1)S(1)}, bf16[768,256]{1,0:T(8,128)(2,1)S(1)}, u32[]{:S(2)}, u32[]{:S(2)}) collective-permute-start(bf16[768,256]{1,0:T(8,128)(2,1)S(1)} %get-tuple-element.16), channel_id=1, source_target_pairs={{0,24},{4,28},{8,0},{12,4},{16,8},{20,12},{24,16},{28,20},{1,25},{... | collective-permute-start | bytes 1179656 | tf_op jit(solution)/shard_map/ppermute | solution.py:126
  92.5 1.3 collective-permute-start.14
  93.8 7.7 %collective-permute-done.5 = bf16[768,256]{1,0:T(8,128)(2,1)S(1)} collective-permute-done((bf16[768,256]{1,0:T(8,128)(2,1)S(1)}, bf16[768,256]{1,0:T(8,128)(2,1)S(1)}, u32[]{:S(2)}, u32[]{:S(2)}) %collective-permute-start.5) | collective-permute-done | bytes 393248 | tf_op jit(solution)/shard_map/ppermute | solution.py:126
  101.6 3.4 %collective-permute-done.6 = bf16[768,256]{1,0:T(8,128)(2,1)S(1)} collective-permute-done((bf16[768,256]{1,0:T(8,128)(2,1)S(1)}, bf16[768,256]{1,0:T(8,128)(2,1)S(1)}, u32[]{:S(2)}, u32[]{:S(2)}) %collective-permute-start.6) | collective-permute-done | bytes 393248 | tf_op jit(solution)/shard_map/ppermute | solution.py:126
  105.4 1.6 collective-permute-start.13
  107.4 12.6 %collective-permute-done.13 = bf16[768,384]{1,0:T(8,128)(2,1)S(1)} collective-permute-done((bf16[768,384]{1,0:T(8,128)(2,1)S(1)}, bf16[768,384]{1,0:T(8,128)(2,1)S(1)}, u32[]{:S(2)}, u32[]{:S(2)}) %collective-permute-start.13) | collective-permute-done | bytes 589856 | tf_op jit(solution)/shard_map/ppermute | solution.py:131
  121.3 4.1 %bitcast_convert_fusion = bf16[768,1536]{1,0:T(8,128)(2,1)S(1)} fusion(bf16[3,512,3072]{2,1,0:T(8,128)(2,1)S(1)} %bitcast.22, s32[]{:T(128)S(6)} %select_n.206, bf16[1,768,512]{2,1,0:T(8,128)(2,1)S(1)} %maximum_bitcast_fusion.2, bf16[1,768,512]{2,1,0:T(8,128)(2,1)S(1)} %maximum_bitcast_fusion.1, bf16[1,768,512]{2,1,0:T(8,128)(2,1)S(1)} %maximum_bitcast_fusion), kind=kOutput, calls=%fused_computation.2 | convolution fusion | flops 3627417600 | bytes 9437188 | tf_op jit(solution)/shard_map/cik,ckm->im/dot_general | solution.py:156
  125.6 6.9 %bitcast_convert_fusion.1 = bf16[768,1536]{1,0:T(8,128)(2,1)S(1)} fusion(bf16[3,512,3072]{2,1,0:T(8,128)(2,1)} %param.13, s32[]{:T(128)S(6)} %select_n.202, bf16[1,768,512]{2,1,0:T(8,128)(2,1)} %copy-done.5, bf16[1,768,512]{2,1,0:T(8,128)(2,1)} %copy-done.6, bf16[1,768,512]{2,1,0:T(8,128)(2,1)} %copy-done.7), kind=kOutput, calls=%fused_computation.3 | convolution fusion | flops 3627417600 | bytes 9437188 | tf_op jit(solution)/shard_map/cik,ckm->im/dot_general | solution.py:156
  133.1 1.6 add_convert_fusion.1
  134.7 1.6 collective-permute-start.17
  136.2 26.4 %collective-permute-done.17 = bf16[768,768]{1,0:T(8,128)(2,1)S(1)} collective-permute-done((bf16[768,768]{1,0:T(8,128)(2,1)S(1)}, bf16[768,768]{1,0:T(8,128)(2,1)S(1)}, u32[]{:S(2)}, u32[]{:S(2)}) %collective-permute-start.17) | collective-permute-done | bytes 1179680 | tf_op jit(solution)/shard_map/ppermute | solution.py:131
  162.6 1.5 add_convert_fusion
  (80 shorter events, 12.1 us)
Async XLA Ops:
  0.0 15.7 %copy-start = (s32[16]{0:T(128)S(1)}, s32[16]{0:T(128)}, u32[]{:S(2)}) copy-start(s32[16]{0:T(128)} %param.15) | copy-start | bytes 196
  2.2 4.8 %copy-start.1 = (bf16[768,512]{1,0:T(8,128)(2,1)S(1)}, bf16[768,512]{1,0:T(8,128)(2,1)}, u32[]{:S(2)}) copy-start(bf16[768,512]{1,0:T(8,128)(2,1)} %param.12) | copy-start | bytes 2359300
  3.1 4.0 %copy-start.2 = (bf16[768,512]{1,0:T(8,128)(2,1)S(1)}, bf16[768,512]{1,0:T(8,128)(2,1)}, u32[]{:S(2)}) copy-start(bf16[768,512]{1,0:T(8,128)(2,1)} %param.8) | copy-start | bytes 2359300
  4.0 13.2 %collective-permute-start = (f32[2,768]{0,1:T(8,128)}, f32[2,768]{0,1:T(8,128)}, u32[]{:S(2)}, u32[]{:S(2)}) collective-permute-start(f32[2,768]{0,1:T(8,128)} %dynamic-slice_bitcast_fusion), channel_id=1, source_target_pairs={{0,4},{4,0},{8,12},{12,8},{16,20},{20,16},{24,28},{28,24},{1,5},{5... | collective-permute-start | bytes 18440 | tf_op jit(solution)/shard_map/ppermute | solution.py:131
  7.1 1.1 copy-start.3
  7.3 1.4 copy-start.4
  8.1 45.0 %collective-permute-start.7 = (bf16[768,256]{1,0:T(8,128)(2,1)}, bf16[768,256]{1,0:T(8,128)(2,1)}, u32[]{:S(2)}, u32[]{:S(2)}) collective-permute-start(bf16[768,256]{1,0:T(8,128)(2,1)} %pad_maximum_fusion.12), channel_id=1, source_target_pairs={{0,4},{4,0},{8,12},{12,8},{16,20},{20,16},{24,28},{28,24},{1,5},{5... | collective-permute-start | bytes 1179656 | tf_op jit(solution)/shard_map/ppermute | solution.py:131
  8.8 6.1 %copy-start.8 = (s32[16,4]{0,1:T(4,128)S(1)}, s32[16,4]{0,1:T(4,128)}, u32[]{:S(2)}) copy-start(s32[16,4]{0,1:T(4,128)} %param.14) | copy-start | bytes 772
  9.7 24.4 %collective-permute-start.8 = (bf16[768,256]{1,0:T(8,128)(2,1)}, bf16[768,256]{1,0:T(8,128)(2,1)}, u32[]{:S(2)}, u32[]{:S(2)}) collective-permute-start(bf16[768,256]{1,0:T(8,128)(2,1)} %pad_maximum_fusion.13), channel_id=1, source_target_pairs={{0,4},{4,0},{8,12},{12,8},{16,20},{20,16},{24,28},{28,24},{1,5},{5... | collective-permute-start | bytes 1179656 | tf_op jit(solution)/shard_map/ppermute | solution.py:131
  12.1 44.3 %collective-permute-start.1 = (bf16[768,256]{1,0:T(8,128)(2,1)}, bf16[768,256]{1,0:T(8,128)(2,1)}, u32[]{:S(2)}, u32[]{:S(2)}) collective-permute-start(bf16[768,256]{1,0:T(8,128)(2,1)} %pad_maximum_fusion.8), channel_id=1, source_target_pairs={{0,4},{4,0},{8,12},{12,8},{16,20},{20,16},{24,28},{28,24},{1,5},{5... | collective-permute-start | bytes 1179656 | tf_op jit(solution)/shard_map/ppermute | solution.py:131
  13.3 36.8 %collective-permute-start.2 = (bf16[768,256]{1,0:T(8,128)(2,1)}, bf16[768,256]{1,0:T(8,128)(2,1)}, u32[]{:S(2)}, u32[]{:S(2)}) collective-permute-start(bf16[768,256]{1,0:T(8,128)(2,1)} %pad_maximum_fusion.9), channel_id=1, source_target_pairs={{0,4},{4,0},{8,12},{12,8},{16,20},{20,16},{24,28},{28,24},{1,5},{5... | collective-permute-start | bytes 1179656 | tf_op jit(solution)/shard_map/ppermute | solution.py:131
  35.3 22.3 %collective-permute-start.9 = (bf16[768,256]{1,0:T(8,128)(2,1)S(1)}, bf16[768,256]{1,0:T(8,128)(2,1)S(1)}, u32[]{:S(2)}, u32[]{:S(2)}) collective-permute-start(bf16[768,256]{1,0:T(8,128)(2,1)S(1)} %get-tuple-element.56.refs_4_), channel_id=1, source_target_pairs={{0,8},{4,12},{8,16},{12,20},{16,24},{20,28},{24,0},{28,4},{1,9},{5... | collective-permute-start | bytes 1179656 | tf_op jit(solution)/shard_map/ppermute | solution.py:126
  37.4 20.2 %collective-permute-start.10 = (bf16[768,256]{1,0:T(8,128)(2,1)S(1)}, bf16[768,256]{1,0:T(8,128)(2,1)S(1)}, u32[]{:S(2)}, u32[]{:S(2)}) collective-permute-start(bf16[768,256]{1,0:T(8,128)(2,1)S(1)} %get-tuple-element.55.refs_3_), channel_id=1, source_target_pairs={{0,24},{4,28},{8,0},{12,4},{16,8},{20,12},{24,16},{28,20},{1,25},{... | collective-permute-start | bytes 1179656 | tf_op jit(solution)/shard_map/ppermute | solution.py:126
  51.3 19.4 %collective-permute-start.3 = (bf16[768,256]{1,0:T(8,128)(2,1)S(1)}, bf16[768,256]{1,0:T(8,128)(2,1)S(1)}, u32[]{:S(2)}, u32[]{:S(2)}) collective-permute-start(bf16[768,256]{1,0:T(8,128)(2,1)S(1)} %get-tuple-element.36.refs_4_), channel_id=1, source_target_pairs={{0,8},{4,12},{8,16},{12,20},{16,24},{20,28},{24,0},{28,4},{1,9},{5... | collective-permute-start | bytes 1179656 | tf_op jit(solution)/shard_map/ppermute | solution.py:126
  53.1 25.8 %collective-permute-start.4 = (bf16[768,256]{1,0:T(8,128)(2,1)S(1)}, bf16[768,256]{1,0:T(8,128)(2,1)S(1)}, u32[]{:S(2)}, u32[]{:S(2)}) collective-permute-start(bf16[768,256]{1,0:T(8,128)(2,1)S(1)} %get-tuple-element.35.refs_3_), channel_id=1, source_target_pairs={{0,24},{4,28},{8,0},{12,4},{16,8},{20,12},{24,16},{28,20},{1,25},{... | collective-permute-start | bytes 1179656 | tf_op jit(solution)/shard_map/ppermute | solution.py:126
  66.8 25.3 %collective-permute-start.11 = (bf16[768,256]{1,0:T(8,128)(2,1)S(1)}, bf16[768,256]{1,0:T(8,128)(2,1)S(1)}, u32[]{:S(2)}, u32[]{:S(2)}) collective-permute-start(bf16[768,256]{1,0:T(8,128)(2,1)S(1)} %get-tuple-element.19), channel_id=1, source_target_pairs={{0,8},{4,12},{8,16},{12,20},{16,24},{20,28},{24,0},{28,4},{1,9},{5... | collective-permute-start | bytes 1179656 | tf_op jit(solution)/shard_map/ppermute | solution.py:126
  66.8 25.2 %collective-permute-start.12 = (bf16[768,256]{1,0:T(8,128)(2,1)S(1)}, bf16[768,256]{1,0:T(8,128)(2,1)S(1)}, u32[]{:S(2)}, u32[]{:S(2)}) collective-permute-start(bf16[768,256]{1,0:T(8,128)(2,1)S(1)} %get-tuple-element.20), channel_id=1, source_target_pairs={{0,24},{4,28},{8,0},{12,4},{16,8},{20,12},{24,16},{28,20},{1,25},{... | collective-permute-start | bytes 1179656 | tf_op jit(solution)/shard_map/ppermute | solution.py:126
  88.1 13.5 %collective-permute-start.5 = (bf16[768,256]{1,0:T(8,128)(2,1)S(1)}, bf16[768,256]{1,0:T(8,128)(2,1)S(1)}, u32[]{:S(2)}, u32[]{:S(2)}) collective-permute-start(bf16[768,256]{1,0:T(8,128)(2,1)S(1)} %get-tuple-element.15), channel_id=1, source_target_pairs={{0,8},{4,12},{8,16},{12,20},{16,24},{20,28},{24,0},{28,4},{1,9},{5... | collective-permute-start | bytes 1179656 | tf_op jit(solution)/shard_map/ppermute | solution.py:126
  88.2 16.8 %collective-permute-start.6 = (bf16[768,256]{1,0:T(8,128)(2,1)S(1)}, bf16[768,256]{1,0:T(8,128)(2,1)S(1)}, u32[]{:S(2)}, u32[]{:S(2)}) collective-permute-start(bf16[768,256]{1,0:T(8,128)(2,1)S(1)} %get-tuple-element.16), channel_id=1, source_target_pairs={{0,24},{4,28},{8,0},{12,4},{16,8},{20,12},{24,16},{28,20},{1,25},{... | collective-permute-start | bytes 1179656 | tf_op jit(solution)/shard_map/ppermute | solution.py:126
  92.3 28.5 %slice-start = ((s8[9437184]{0:T(1024)(128)(4,1)}), s8[4194304]{0:T(1024)(128)(4,1)S(1)}, s32[]{:S(2)}) async-start(s8[9437184]{0:T(1024)(128)(4,1)} %bitcast.21), calls=%async_computation | async-start | bytes 8388608
  92.5 14.7 %collective-permute-start.14 = (bf16[768,384]{1,0:T(8,128)(2,1)S(1)}, bf16[768,384]{1,0:T(8,128)(2,1)S(1)}, u32[]{:S(2)}, u32[]{:S(2)}) collective-permute-start(bf16[768,384]{1,0:T(8,128)(2,1)S(1)} %get-tuple-element.28), channel_id=1, source_target_pairs={{0,4},{4,0},{8,12},{12,8},{16,20},{20,16},{24,28},{28,24},{1,5},{5... | collective-permute-start | bytes 1769480 | tf_op jit(solution)/shard_map/ppermute | solution.py:131
  105.2 15.6 %slice-start.1 = ((s8[9437184]{0:T(1024)(128)(4,1)}), s8[4194304]{0:T(1024)(128)(4,1)S(1)}, s32[]{:S(2)}) async-start(s8[9437184]{0:T(1024)(128)(4,1)} %bitcast.21), calls=%async_computation.1 | async-start | bytes 8388608
  105.4 14.5 %collective-permute-start.13 = (bf16[768,384]{1,0:T(8,128)(2,1)S(1)}, bf16[768,384]{1,0:T(8,128)(2,1)S(1)}, u32[]{:S(2)}, u32[]{:S(2)}) collective-permute-start(bf16[768,384]{1,0:T(8,128)(2,1)S(1)} %get-tuple-element.26), channel_id=1, source_target_pairs={{0,4},{4,0},{8,12},{12,8},{16,20},{20,16},{24,28},{28,24},{1,5},{5... | collective-permute-start | bytes 1769480 | tf_op jit(solution)/shard_map/ppermute | solution.py:131
  120.0 1.2 slice-start.2
  120.5 4.9 %copy-start.5 = (bf16[1,768,512]{2,1,0:T(8,128)(2,1)}, bf16[1,768,512]{2,1,0:T(8,128)(2,1)S(1)}, u32[]{:S(2)}) copy-start(bf16[1,768,512]{2,1,0:T(8,128)(2,1)S(1)} %maximum_bitcast_fusion.2) | copy-start | bytes 2359300
  120.5 4.8 %copy-start.6 = (bf16[1,768,512]{2,1,0:T(8,128)(2,1)}, bf16[1,768,512]{2,1,0:T(8,128)(2,1)S(1)}, u32[]{:S(2)}) copy-start(bf16[1,768,512]{2,1,0:T(8,128)(2,1)S(1)} %maximum_bitcast_fusion.1) | copy-start | bytes 2359300
  121.3 4.1 %copy-start.7 = (bf16[1,768,512]{2,1,0:T(8,128)(2,1)}, bf16[1,768,512]{2,1,0:T(8,128)(2,1)S(1)}, u32[]{:S(2)}) copy-start(bf16[1,768,512]{2,1,0:T(8,128)(2,1)S(1)} %maximum_bitcast_fusion) | copy-start | bytes 2359300
  125.5 7.6 %collective-permute-start.16 = (bf16[768,768]{1,0:T(8,128)(2,1)S(1)}, bf16[768,768]{1,0:T(8,128)(2,1)}, u32[]{:S(2)}, u32[]{:S(2)}) collective-permute-start(bf16[768,768]{1,0:T(8,128)(2,1)S(1)} %constant_dynamic-slice_fusion), channel_id=1, source_target_pairs={{0,1},{1,0},{2,3},{3,2},{4,5},{5,4},{6,7},{7,6},{8,9},{9,8},{10,11... | collective-permute-start | bytes 3538952 | tf_op jit(solution)/shard_map/ppermute | solution.py:131
  132.6 3.7 %collective-permute-start.15 = (bf16[768,768]{1,0:T(8,128)(2,1)S(1)}, bf16[768,768]{1,0:T(8,128)(2,1)S(1)}, u32[]{:S(2)}, u32[]{:S(2)}) collective-permute-start(bf16[768,768]{1,0:T(8,128)(2,1)S(1)} %constant_dynamic-slice_fusion.1), channel_id=1, source_target_pairs={{0,1},{1,0},{2,3},{3,2},{4,5},{5,4},{6,7},{7,6},{8,9},{9,8},{10,11... | collective-permute-start | bytes 3538952 | tf_op jit(solution)/shard_map/ppermute | solution.py:131
  134.7 28.0 %collective-permute-start.17 = (bf16[768,768]{1,0:T(8,128)(2,1)S(1)}, bf16[768,768]{1,0:T(8,128)(2,1)S(1)}, u32[]{:S(2)}, u32[]{:S(2)}) collective-permute-start(bf16[768,768]{1,0:T(8,128)(2,1)S(1)} %add_convert_fusion.1), channel_id=1, source_target_pairs={{0,2},{1,3},{2,0},{3,1},{4,6},{5,7},{6,4},{7,5},{8,10},{9,11},{10,... | collective-permute-start | bytes 3538952 | tf_op jit(solution)/shard_map/ppermute | solution.py:131

commit v2 on v1

--- a/solution.py
+++ b/solution.py
@@ -81,9 +81,12 @@
     end = own_blocks + 1
     for half, acc in enumerate((key_acc, value_acc)):
         cols = slice(half * HD, (half + 1) * HD)
-        prev_ref[:, cols] = acc[:rows_block, :].astype(BF16)
         own_ref[:, cols] = acc[rows_block : end * rows_block, :]
-        next_ref[:, cols] = acc[end * rows_block :, :].astype(BF16)
+        for at in range(HALO):
+            before = (HALO - 1 - at) * TILE
+            after = end * rows_block + at * TILE
+            prev_ref[at, :, cols] = acc[before : before + TILE, :].astype(BF16)
+            next_ref[at, :, cols] = acc[after : after + TILE, :].astype(BF16)
 
 
 def attention(slots, counts, delta, qg_blocks, kv_blocks):
@@ -94,7 +97,7 @@
     window = rows + 2 * rows_block
     vmem = pl.BlockSpec(memory_space=pltpu.VMEM)
     smem = pl.BlockSpec(memory_space=pltpu.SMEM)
-    pair = jax.ShapeDtypeStruct((rows_block, 2 * HD), BF16)
+    pair = jax.ShapeDtypeStruct((HALO, TILE, 2 * HD), BF16)
     return pl.pallas_call(
         functools.partial(attention_kernel, tiles, own_blocks),
         out_shape=[
@@ -141,12 +144,8 @@
     return slots.astype(jnp.int32), counts[ids].astype(jnp.int32)
 
 
-def summed_over_heads(grads, projection):
-    stack = jnp.stack(grads)
+def owner_terms(stack, projection):
     count = lax.axis_size("head")
-    if count != 4:
-        term = jnp.einsum("cik,ckm->im", stack, projection, preferred_element_type=F32)
-        return lax.psum_scatter(term.astype(BF16), "head", scatter_dimension=1, tiled=True)
     place = lax.axis_index("head")
     chip, core = place // 2, place % 2
     width = projection.shape[2] // count
@@ -159,7 +158,20 @@
         return kept.astype(F32) + swapped(sent, "head", 1).astype(F32)
 
     far = swapped(chip_sum(1 - chip).astype(BF16), "head", 2)
-    return (chip_sum(chip) + far.astype(F32)).astype(BF16)
+    return chip_sum(chip), far
+
+
+def scattered_over_heads(stack, projection):
+    term = jnp.einsum("cik,ckm->im", stack, projection, preferred_element_type=F32)
+    return lax.psum_scatter(term.astype(BF16), "head", scatter_dimension=1, tiled=True)
+
+
+def after(arrays, awaited):
+    return lax.optimization_barrier((tuple(arrays), tuple(awaited)))[0]
+
+
+def tile_of(array, at):
+    return lax.slice_in_dim(array, at * TILE, (at + 1) * TILE, axis=0)
 
 
 def local(
@@ -174,67 +186,124 @@
     deltas = jnp.sum(
         (output_grad.astype(F32) * output_rows.astype(F32)).reshape(rows_dev, heads_dev, HD), axis=-1
     ).T
-    grads = ([], [], [])
-    if heads_dev % 2 or seq_count % 2:
+    if heads_dev % 2 or seq_count % 2 or tiles_dev != HALO:
+        grads = ([], [], [])
         slots, live = tables(neighbours, counts, place * tiles_dev, tiles_dev, tiles_all)
         for head in range(heads_dev):
             qg = jnp.concatenate([head_cols(query_rows, head), head_cols(output_grad, head)], 1)
             kv = jnp.concatenate([head_cols(key_rows, head), head_cols(value_rows, head)], 1)
             window = [shifted(kv, "seq", 1), kv, shifted(kv, "seq", -1)]
             query_grad, to_prev, own, to_next = attention(slots, live, deltas[head], [qg], window)
-            own = (
-                own + shifted(to_prev, "seq", -1).astype(F32) + shifted(to_next, "seq", 1).astype(F32)
-            ).astype(BF16)
+            from_next = shifted(to_prev, "seq", -1)[::-1].reshape(rows_dev, 2 * HD)
+            from_prev = shifted(to_next, "seq", 1).reshape(rows_dev, 2 * HD)
+            own = (own + from_next.astype(F32) + from_prev.astype(F32)).astype(BF16)
             for into, block in zip(grads, (query_grad, own[:, :HD], own[:, HD:])):
                 into.append(block)
-        return summed_over_heads([jnp.concatenate(blocks, 1) for blocks in grads], projection)
+        stack = jnp.stack([jnp.concatenate(blocks, 1) for blocks in grads])
+        return scattered_over_heads(stack, projection)
 
     odd = place % 2
+    even = odd == 0
     half = heads_dev // 2
     first = (place - odd) * tiles_dev
     slots, live = tables(neighbours, counts, first, 2 * tiles_dev, tiles_all)
 
     def in_order(mine, other):
-        return jnp.where(odd == 0, mine, other), jnp.where(odd == 0, other, mine)
-
-    delta_mine = lax.dynamic_slice_in_dim(deltas, odd * half, half, 0)
-    delta_sent = lax.dynamic_slice_in_dim(deltas, (1 - odd) * half, half, 0)
-    delta_pair = jnp.concatenate(in_order(delta_mine, swapped(delta_sent, "seq", 1)), 1)
-
-    def exchanged(left, right, step):
-        def both(head):
-            return jnp.concatenate([head_cols(left, head), head_cols(right, head)], 1)
-
-        return in_order(
-            both(odd * half + step), swapped(both((1 - odd) * half + step), "seq", 1)
-        )
-
-    mine, other = [], []
-    kv_pairs = [exchanged(key_rows, value_rows, step) for step in range(half)]
-    qg_pairs = [exchanged(query_rows, output_grad, step) for step in range(half)]
+        return jnp.where(even, mine, other), jnp.where(even, other, mine)
+
+    def both(left, right, head):
+        return jnp.concatenate([head_cols(left, head), head_cols(right, head)], 1)
+
+    kept, sent = odd * half, (1 - odd) * half
+    kv_kept = [both(key_rows, value_rows, kept + step) for step in range(half)]
+    kv_sent = [both(key_rows, value_rows, sent + step) for step in range(half)]
+    qg_kept = [both(query_rows, output_grad, kept + step) for step in range(half)]
+    qg_sent = [both(query_rows, output_grad, sent + step) for step in range(half)]
+
+    kv_got = [swapped(kv_sent[0], "seq", 1)]
+    delta_sent = lax.dynamic_slice_in_dim(deltas, sent, half, 0)
+    qg_got = []
+    for step in range(half):
+        awaited = kv_got[step]
+        wave = [qg_sent[step]] + kv_sent[step + 1 : step + 2]
+        if step == 0:
+            wave.append(delta_sent)
+        wave = [swapped(block, "seq", 1) for block in after(wave, [awaited])]
+        qg_got.append(wave[0])
+        if step + 1 < half:
+            kv_got.append(wave[1])
+        if step == 0:
+            delta_got = wave[-1]
+    delta_kept = lax.dynamic_slice_in_dim(deltas, kept, half, 0)
+    delta_pair = jnp.concatenate(in_order(delta_kept, delta_got), 1)
+
+    kv_pairs = [in_order(kv_kept[step], kv_got[step]) for step in range(half)]
+    halos = []
+    for step in range(half):
+        ends = kv_pairs[step] if step == 0 else after(kv_pairs[step], halos[-1])
+        halos.append((shifted(ends[1], "seq", 2), shifted(ends[0], "seq", -2)))
+
+    def of_owner(tiles_low_high):
+        low, high = tiles_low_high
+        return jnp.where(even, low, high), jnp.where(even, high, low)
+
+    places = ((0, 3), (1, 2))
+    query_grads, kv_mine, kv_other = [], [], []
+    arrived = None
     for step in range(half):
         low, high = kv_pairs[step]
-        window = [shifted(high, "seq", 2), low, high, shifted(low, "seq", -2)]
+        window = [halos[step][0], low, high, halos[step][1]]
+        qg_blocks = list(in_order(qg_kept[step], qg_got[step]))
         query_grad, to_prev, own, to_next = attention(
-            slots, live, delta_pair[step], list(qg_pairs[step]), window
+            slots, live, delta_pair[step], qg_blocks, window
         )
-        from_next = shifted(to_prev, "seq", -2)
-        from_prev = shifted(to_next, "seq", 2)
-        low = own[:rows_dev] + from_prev.astype(F32)
-        high = own[rows_dev:] + from_next.astype(F32)
-        low = jnp.concatenate([query_grad[:rows_dev], low.astype(BF16)], 1)
-        high = jnp.concatenate([query_grad[rows_dev:], high.astype(BF16)], 1)
-        mine.append(jnp.where(odd == 0, low, high))
-        other.append(swapped(jnp.where(odd == 0, high, low), "seq", 1))
-    parts = []
-    for which in range(3):
-        cols = slice(which * HD, (which + 1) * HD)
-        first_half, second_half = in_order(
-            jnp.concatenate([block[:, cols] for block in mine], 1),
-            jnp.concatenate([block[:, cols] for block in other], 1),
-        )
-        parts.append(jnp.concatenate([first_half, second_half], 1))
-    return summed_over_heads(parts, projection)
+        query_grads.append(query_grad)
+        if step + 1 < half:
+            to_prev, to_next = after((to_prev, to_next), halos[step + 1])
+            back = shifted(to_prev, "seq", -2), shifted(to_next, "seq", 2)
+            from_next, from_prev = [[block[at] for at in range(HALO)] for block in back]
+        else:
+            ends = [(to_prev[at], to_next[at]) for at in range(HALO)]
+            from_next, from_prev = [], []
+            for at in range(HALO):
+                block = after(ends[at], arrived) if arrived else ends[at]
+                arrived = shifted(block[0], "seq", -2), shifted(block[1], "seq", 2)
+                from_next.append(arrived[0])
+                from_prev.append(arrived[1])
+        if step + 1 < half:
+            arrived = back
+        sums = []
+        for at, (at_low, at_high) in enumerate(places):
+            low = tile_of(own, at_low) + from_prev[at].astype(F32)
+            high = tile_of(own, at_high) + from_next[at].astype(F32)
+            sums.append(of_owner((low.astype(BF16), high.astype(BF16))))
+        kv_mine.append([mine for mine, _ in sums])
+        if step + 1 < half:
+            got = swapped(jnp.concatenate([other for _, other in sums], 0), "seq", 1)
+            kv_other.append([tile_of(got, at) for at in range(HALO)])
+        else:
+            kv_other.append([swapped(other, "seq", 1) for _, other in sums])
+    query_all = jnp.concatenate(query_grads, 1)
+    query_sums = [of_owner((tile_of(query_all, low), tile_of(query_all, high))) for low, high in places]
+    query_got = swapped(jnp.concatenate([other for _, other in query_sums], 0), "seq", 1)
+
+    results = []
+    for at in range(HALO):
+        parts = [in_order(query_sums[at][0], tile_of(query_got, at))]
+        for cols in (slice(0, HD), slice(HD, 2 * HD)):
+            parts.append(
+                in_order(
+                    jnp.concatenate([blocks[at][:, cols] for blocks in kv_mine], 1),
+                    jnp.concatenate([blocks[at][:, cols] for blocks in kv_other], 1),
+                )
+            )
+        stack = jnp.stack([jnp.concatenate(part, 1) for part in parts])
+        if lax.axis_size("head") == 4:
+            near, far = owner_terms(stack, projection)
+            results.append((near + far.astype(F32)).astype(BF16))
+        else:
+            results.append(scattered_over_heads(stack, projection))
+    return jnp.concatenate(in_order(results[0], results[1]), 0)
 
 
 def solution(mesh):

time: 165 us -> 165 us (level)
  starting transfers between devices: 27.8 us -> 35.4 us
  other arithmetic: 16.2 us -> 11.4 us
  waiting for transfers between devices: 85.2 us -> 80.9 us
  local copies, waits for them, and re-layouts: 5.09 us -> 9.05 us
  matrix products: 11 us -> 8.21 us
    ppermute x10 -> x15, waiting for transfers between devices: 65.8 us -> 50.1 us  [swapped(): return lax.ppermute(block, axis, [(i, i ^ bit) for i in range(count)])]
    ppermute x8 -> x10, waiting for transfers between devices: 19.4 us -> 30.8 us  [shifted(): lax.ppermute(block, axis, [(i, (i + distance) % count) for i in range(cou...]
    dynamic_slice x4, local copies, waits for them, and re-layouts: 0.56 us -> 5.28 us  [head_cols(): return lax.dynamic_slice_in_dim(array, head * HD, HD, 1)]
    ppermute x10 -> x15, starting transfers between devices: 11.8 us -> 16.1 us  [swapped(): return lax.ppermute(block, axis, [(i, i ^ bit) for i in range(count)])]
    ppermute x8 -> x10, starting transfers between devices: 16 us -> 19.3 us  [shifted(): lax.ppermute(block, axis, [(i, (i + distance) % count) for i in range(cou...]
    convert_element_type x4 -> x2, other arithmetic: 3.49 us -> 0.31 us  [owner_terms(): far = swapped(chip_sum(1 - chip).astype(BF16), 'head', 2)]
    dot_general x2 -> x4, matrix products: 11 us -> 8.21 us  [chip_sum(): jnp.einsum('cik,ckm->im', stack, weights, preferred_element_type=F32)]
    select_n x9 -> x13, other arithmetic: 6.77 us -> 5.35 us  [the longest x10 4.86 us: in_order(): return (jnp.where(even, mine, other), jnp.where(even, other, mine))]
  transfers between devices with their start and end apart: 18 -> 25, of which waited for: 8 -> 13; matrix products, arithmetic and copies ran while one was open for 13% -> 14% of each run, Pallas kernels for 11% -> 6%
where the time goes in v2:
time: 165 us
  waiting for transfers between devices  80.9 us (49%)
  starting transfers between devices  35.4 us (21%)
  Pallas kernels  19.4 us (12%)
  other arithmetic  11.4 us (7%)
  local copies, waits for them, and re-layouts  9.05 us (5%)
  matrix products  8.21 us (5%)
    ppermute x15, waiting for transfers between devices, swapped(): return lax.ppermute(block, axis, [(i, i ^ bit) for i in range(count)])  50.1 us
    ppermute x10, waiting for transfers between devices, shifted(): lax.ppermute(block, axis, [(i, (i + distance) % count) for i in range(cou...  30.8 us
    pallas_call x2, Pallas kernels, attention(): pl.pallas_call(functools.partial(attention_kernel, tiles, own_blocks), ou...  19.4 us
    ppermute x10, starting transfers between devices, shifted(): lax.ppermute(block, axis, [(i, (i + distance) % count) for i in range(cou...  19.3 us
    ppermute x15, starting transfers between devices, swapped(): return lax.ppermute(block, axis, [(i, i ^ bit) for i in range(count)])  16.1 us
    dot_general x4, matrix products, chip_sum(): jnp.einsum('cik,ckm->im', stack, weights, preferred_element_type=F32)  8.21 us
    dynamic_slice x4, local copies, waits for them, and re-layouts, head_cols(): return lax.dynamic_slice_in_dim(array, head * HD, HD, 1)  5.28 us
    select_n x10, other arithmetic, in_order(): return (jnp.where(even, mine, other), jnp.where(even, other, mine))  4.86 us
  transfers between devices with their start and end apart: 25, of which 13 were waited for; matrix products, arithmetic and copies ran while one was open for 14% of the time, Pallas kernels for 6%

profile of v2, /device:TPU:0, one launch (start us, length us, event | category | flops | bytes accessed | tf_op | source)
XLA Modules:
  0.0 164.9 jit_solution(16061482401438682878)
XLA Ops:
  0.0 2.1 %constant_dynamic-slice_fusion.11 = (bf16[768,128]{1,0:T(8,128)(2,1)}, bf16[768,128]{1,0:T(8,128)(2,1)S(1)}, bf16[768,128]{1,0:T(8,128)(2,1)}, bf16[768,128]{1,0:T(8,128)(2,1)}) fusion(bf16[768,512]{1,0:T(8,128)(2,1)} %param.9, s32[]{:T(128)S(6)} %select_n.259, s32[]{:T(128)S(6)} %select_n.253, s32[]{:T(128)S(6)} %select_n.254, s32[]{:T(128)S(6)} %select_n.264), kind=kLoop, calls=%fused_computation.124 | loop fusion | bytes 1572880 | tf_op jit(solution)/shard_map/dynamic_slice | solution.py:138
  3.9 3.0 %collective-permute-start = (bf16[768,256]{1,0:T(8,128)(2,1)}, bf16[768,256]{1,0:T(8,128)(2,1)}, u32[]{:S(2)}, u32[]{:S(2)}) collective-permute-start(bf16[768,256]{1,0:T(8,128)(2,1)} %pad_maximum_fusion.9), channel_id=1, source_target_pairs={{0,4},{4,0},{8,12},{12,8},{16,20},{20,16},{24,28},{28,24},{1,5},{5... | collective-permute-start | bytes 1179656 | tf_op jit(solution)/shard_map/ppermute | solution.py:134
  16.3 1.7 %collective-permute-start.2 = (bf16[768,256]{1,0:T(8,128)(2,1)}, bf16[768,256]{1,0:T(8,128)(2,1)}, u32[]{:S(2)}, u32[]{:S(2)}) collective-permute-start(bf16[768,256]{1,0:T(8,128)(2,1)} %pad_maximum_fusion.7), channel_id=1, source_target_pairs={{0,4},{4,0},{8,12},{12,8},{16,20},{20,16},{24,28},{28,24},{1,5},{5... | collective-permute-start | bytes 1179656 | tf_op jit(solution)/shard_map/ppermute | solution.py:134
  19.5 1.9 %collective-permute-start.3 = (bf16[768,256]{1,0:T(8,128)(2,1)S(1)}, bf16[768,256]{1,0:T(8,128)(2,1)S(1)}, u32[]{:S(2)}, u32[]{:S(2)}) collective-permute-start(bf16[768,256]{1,0:T(8,128)(2,1)S(1)} %get-tuple-element.75.refs_4_), channel_id=1, source_target_pairs={{0,8},{4,12},{8,16},{12,20},{16,24},{20,28},{24,0},{28,4},{1,9},{5... | collective-permute-start | bytes 1179656 | tf_op jit(solution)/shard_map/ppermute | solution.py:129
  21.3 2.1 %collective-permute-start.4 = (bf16[768,256]{1,0:T(8,128)(2,1)S(1)}, bf16[768,256]{1,0:T(8,128)(2,1)S(1)}, u32[]{:S(2)}, u32[]{:S(2)}) collective-permute-start(bf16[768,256]{1,0:T(8,128)(2,1)S(1)} %get-tuple-element.74.refs_3_), channel_id=1, source_target_pairs={{0,24},{4,28},{8,0},{12,4},{16,8},{20,12},{24,16},{28,20},{1,25},{... | collective-permute-start | bytes 1179656 | tf_op jit(solution)/shard_map/ppermute | solution.py:129
  23.4 1.7 %collective-permute-start.5 = (bf16[768,256]{1,0:T(8,128)(2,1)}, bf16[768,256]{1,0:T(8,128)(2,1)}, u32[]{:S(2)}, u32[]{:S(2)}) collective-permute-start(bf16[768,256]{1,0:T(8,128)(2,1)} %pad_maximum_fusion.8), channel_id=1, source_target_pairs={{0,4},{4,0},{8,12},{12,8},{16,20},{20,16},{24,28},{28,24},{1,5},{5... | collective-permute-start | bytes 1179656 | tf_op jit(solution)/shard_map/ppermute | solution.py:134
  25.1 11.9 %collective-permute-done.1 = f32[2,768]{0,1:T(8,128)S(1)} collective-permute-done((f32[2,768]{0,1:T(8,128)}, f32[2,768]{0,1:T(8,128)S(1)}, u32[]{:S(2)}, u32[]{:S(2)}) %collective-permute-start.1) | collective-permute-done | bytes 6176 | tf_op jit(solution)/shard_map/ppermute | solution.py:134
  37.5 6.3 %collective-permute-done.5 = bf16[768,256]{1,0:T(8,128)(2,1)} collective-permute-done((bf16[768,256]{1,0:T(8,128)(2,1)}, bf16[768,256]{1,0:T(8,128)(2,1)}, u32[]{:S(2)}, u32[]{:S(2)}) %collective-permute-start.5) | collective-permute-done | bytes 393248 | tf_op jit(solution)/shard_map/ppermute | solution.py:134
  44.9 1.5 collective-permute-start.7
  46.5 2.3 %collective-permute-start.8 = (bf16[768,256]{1,0:T(8,128)(2,1)S(1)}, bf16[768,256]{1,0:T(8,128)(2,1)S(1)}, u32[]{:S(2)}, u32[]{:S(2)}) collective-permute-start(bf16[768,256]{1,0:T(8,128)(2,1)S(1)} %get-tuple-element.31.refs_3_), channel_id=1, source_target_pairs={{0,24},{4,28},{8,0},{12,4},{16,8},{20,12},{24,16},{28,20},{1,25},{... | collective-permute-start | bytes 1179656 | tf_op jit(solution)/shard_map/ppermute | solution.py:129
  48.8 1.4 collective-permute-start.6
  51.4 9.7 %shard_map.82 = (bf16[1536,128]{1,0:T(8,128)(2,1)S(1)}, bf16[2,384,256]{2,1,0:T(8,128)(2,1)S(1)}, f32[1536,256]{1,0:T(8,128)S(1)}, bf16[2,384,256]{2,1,0:T(8,128)(2,1)S(1)}) custom-call(s32[16]{0:T(128)S(1)} %and_select_fusion.slots_ref, s32[4]{0:T(128)S(1)} %gather_fusion.1, f32[4,1,384]{2,1,0:T(1,128)S(1)} %bitcast.82, ...), custom_call_target="tpu_custom_call" | custom-call | flops 6039797760 | bytes 5898240 | tf_op jit(solution)/shard_map/pallas_call | solution.py:101
  61.4 2.3 %collective-permute-done.8.refs_5_ = bf16[768,256]{1,0:T(8,128)(2,1)S(1)} collective-permute-done((bf16[768,256]{1,0:T(8,128)(2,1)S(1)}, bf16[768,256]{1,0:T(8,128)(2,1)S(1)}, u32[]{:S(2)}, u32[]{:S(2)}) %collective-permute-start.8) | collective-permute-done | bytes 393248 | tf_op jit(solution)/shard_map/ppermute | solution.py:129
  63.7 9.7 %shard_map.83 = (bf16[1536,128]{1,0:T(8,128)(2,1)S(1)}, bf16[2,384,256]{2,1,0:T(8,128)(2,1)S(1)}, f32[1536,256]{1,0:T(8,128)S(1)}, bf16[2,384,256]{2,1,0:T(8,128)(2,1)S(1)}) custom-call(s32[16]{0:T(128)S(1)} %and_select_fusion.slots_ref, s32[4]{0:T(128)S(1)} %gather_fusion.1, f32[4,1,384]{2,1,0:T(1,128)S(1)} %bitcast.81, ...), custom_call_target="tpu_custom_call" | custom-call | flops 6039797760 | bytes 5898240 | tf_op jit(solution)/shard_map/pallas_call | solution.py:101
  73.6 1.6 collective-permute-start.9
  75.8 3.2 %collective-permute-start.11 = (bf16[2,384,256]{2,1,0:T(8,128)(2,1)S(1)}, bf16[2,384,256]{2,1,0:T(8,128)(2,1)S(1)}, u32[]{:S(2)}, u32[]{:S(2)}) collective-permute-start(bf16[2,384,256]{2,1,0:T(8,128)(2,1)S(1)} %get-tuple-element.37), channel_id=1, source_target_pairs={{0,24},{4,28},{8,0},{12,4},{16,8},{20,12},{24,16},{28,20},{1,25},{... | collective-permute-start | bytes 1179656 | tf_op jit(solution)/shard_map/ppermute | solution.py:129
  79.0 10.0 %collective-permute-done.10 = bf16[2,384,256]{2,1,0:T(8,128)(2,1)S(1)} collective-permute-done((bf16[2,384,256]{2,1,0:T(8,128)(2,1)S(1)}, bf16[2,384,256]{2,1,0:T(8,128)(2,1)S(1)}, u32[]{:S(2)}, u32[]{:S(2)}) %collective-permute-start.10) | collective-permute-done | bytes 393248 | tf_op jit(solution)/shard_map/ppermute | solution.py:129
  89.0 5.6 %collective-permute-done.11 = bf16[2,384,256]{2,1,0:T(8,128)(2,1)S(1)} collective-permute-done((bf16[2,384,256]{2,1,0:T(8,128)(2,1)S(1)}, bf16[2,384,256]{2,1,0:T(8,128)(2,1)S(1)}, u32[]{:S(2)}, u32[]{:S(2)}) %collective-permute-start.11) | collective-permute-done | bytes 393248 | tf_op jit(solution)/shard_map/ppermute | solution.py:129
  96.1 3.5 %collective-permute-start.13 = (bf16[384,256]{1,0:T(8,128)(2,1)S(1)}, bf16[384,256]{1,0:T(8,128)(2,1)S(1)}, u32[]{:S(2)}, u32[]{:S(2)}) collective-permute-start(bf16[384,256]{1,0:T(8,128)(2,1)S(1)} %get-tuple-element.42), channel_id=1, source_target_pairs={{0,24},{4,28},{8,0},{12,4},{16,8},{20,12},{24,16},{28,20},{1,25},{... | collective-permute-start | bytes 589832 | tf_op jit(solution)/shard_map/ppermute | solution.py:129
  99.8 5.6 %collective-permute-done.12 = bf16[384,256]{1,0:T(8,128)(2,1)S(1)} collective-permute-done((bf16[384,256]{1,0:T(8,128)(2,1)S(1)}, bf16[384,256]{1,0:T(8,128)(2,1)S(1)}, u32[]{:S(2)}, u32[]{:S(2)}) %collective-permute-start.12) | collective-permute-done | bytes 196640 | tf_op jit(solution)/shard_map/ppermute | solution.py:129
  106.6 3.4 %collective-permute-start.20 = (bf16[384,256]{1,0:T(8,128)(2,1)S(1)}, bf16[384,256]{1,0:T(8,128)(2,1)S(1)}, u32[]{:S(2)}, u32[]{:S(2)}) collective-permute-start(bf16[384,256]{1,0:T(8,128)(2,1)S(1)} %get-tuple-element.44), channel_id=1, source_target_pairs={{0,24},{4,28},{8,0},{12,4},{16,8},{20,12},{24,16},{28,20},{1,25},{... | collective-permute-start | bytes 589832 | tf_op jit(solution)/shard_map/ppermute | solution.py:129
  110.1 4.6 %collective-permute-done.19 = bf16[384,256]{1,0:T(8,128)(2,1)S(1)} collective-permute-done((bf16[384,256]{1,0:T(8,128)(2,1)S(1)}, bf16[384,256]{1,0:T(8,128)(2,1)S(1)}, u32[]{:S(2)}, u32[]{:S(2)}) %collective-permute-start.19) | collective-permute-done | bytes 196640 | tf_op jit(solution)/shard_map/ppermute | solution.py:129
  114.7 1.9 %collective-permute-done.20 = bf16[384,256]{1,0:T(8,128)(2,1)S(1)} collective-permute-done((bf16[384,256]{1,0:T(8,128)(2,1)S(1)}, bf16[384,256]{1,0:T(8,128)(2,1)S(1)}, u32[]{:S(2)}, u32[]{:S(2)}) %collective-permute-start.20) | collective-permute-done | bytes 196640 | tf_op jit(solution)/shard_map/ppermute | solution.py:129
  117.0 1.9 %collective-permute-start.15 = (bf16[384,256]{1,0:T(8,128)(2,1)S(1)}, bf16[384,256]{1,0:T(8,128)(2,1)S(1)}, u32[]{:S(2)}, u32[]{:S(2)}) collective-permute-start(bf16[384,256]{1,0:T(8,128)(2,1)S(1)} %get-tuple-element.56), channel_id=1, source_target_pairs={{0,4},{4,0},{8,12},{12,8},{16,20},{20,16},{24,28},{28,24},{1,5},{5... | collective-permute-start | bytes 589832 | tf_op jit(solution)/shard_map/ppermute | solution.py:134
  119.1 5.7 %collective-permute-done.21 = bf16[384,256]{1,0:T(8,128)(2,1)S(1)} collective-permute-done((bf16[384,256]{1,0:T(8,128)(2,1)S(1)}, bf16[384,256]{1,0:T(8,128)(2,1)S(1)}, u32[]{:S(2)}, u32[]{:S(2)}) %collective-permute-start.21) | collective-permute-done | bytes 196640 | tf_op jit(solution)/shard_map/ppermute | solution.py:134
  125.1 2.0 %fusion.26 = bf16[384,1536]{1,0:T(8,128)(2,1)S(1)} fusion(bf16[3,512,3072]{2,1,0:T(8,128)(2,1)S(1)} %bitcast.84, s32[]{:T(128)S(6)} %select_n.284, bf16[1,384,512]{2,1,0:T(8,128)(2,1)S(1)} %maximum_bitcast_fusion.5, bf16[1,384,512]{2,1,0:T(8,128)(2,1)S(1)} %maximum_bitcast_fusion.4, bf16[1,384,512]{2,1,0:T(8,128)(2,1)S(1)} %maximum_bitcast_fusion.3), kind=kOutput, calls=%fused_computation.16 | convolution fusion | flops 1813708800 | bytes 7077892 | tf_op jit(solution)/shard_map/cik,ckm->im/dot_general | solution.py:155
  127.3 2.1 %fusion.20 = bf16[384,1536]{1,0:T(8,128)(2,1)S(1)} fusion(bf16[3,512,3072]{2,1,0:T(8,128)(2,1)S(1)} %bitcast.84, s32[]{:T(128)S(6)} %select_n.288, bf16[1,384,512]{2,1,0:T(8,128)(2,1)S(1)} %maximum_bitcast_fusion.5, bf16[1,384,512]{2,1,0:T(8,128)(2,1)S(1)} %maximum_bitcast_fusion.4, bf16[1,384,512]{2,1,0:T(8,128)(2,1)S(1)} %maximum_bitcast_fusion.3), kind=kOutput, calls=%fused_computation.14 | convolution fusion | flops 1813708800 | bytes 7077892 | tf_op jit(solution)/shard_map/cik,ckm->im/dot_general | solution.py:155
  130.2 2.1 %fusion.23 = bf16[384,1536]{1,0:T(8,128)(2,1)S(1)} fusion(bf16[3,512,3072]{2,1,0:T(8,128)(2,1)S(1)} %bitcast.84, s32[]{:T(128)S(6)} %select_n.288, bf16[1,384,512]{2,1,0:T(8,128)(2,1)S(1)} %maximum_bitcast_fusion.2, bf16[1,384,512]{2,1,0:T(8,128)(2,1)S(1)} %maximum_bitcast_fusion.1, bf16[1,384,512]{2,1,0:T(8,128)(2,1)S(1)} %maximum_bitcast_fusion), kind=kOutput, calls=%fused_computation.15 | convolution fusion | flops 1813708800 | bytes 7077892 | tf_op jit(solution)/shard_map/cik,ckm->im/dot_general | solution.py:155
  132.4 2.0 %fusion.29 = bf16[384,1536]{1,0:T(8,128)(2,1)S(1)} fusion(bf16[3,512,3072]{2,1,0:T(8,128)(2,1)S(1)} %bitcast.84, s32[]{:T(128)S(6)} %select_n.284, bf16[1,384,512]{2,1,0:T(8,128)(2,1)S(1)} %maximum_bitcast_fusion.2, bf16[1,384,512]{2,1,0:T(8,128)(2,1)S(1)} %maximum_bitcast_fusion.1, bf16[1,384,512]{2,1,0:T(8,128)(2,1)S(1)} %maximum_bitcast_fusion), kind=kOutput, calls=%fused_computation.17 | convolution fusion | flops 1813708800 | bytes 7077892 | tf_op jit(solution)/shard_map/cik,ckm->im/dot_general | solution.py:155
  135.6 1.9 %collective-permute-start.18 = (bf16[384,768]{1,0:T(8,128)(2,1)S(1)}, bf16[384,768]{1,0:T(8,128)(2,1)S(1)}, u32[]{:S(2)}, u32[]{:S(2)}) collective-permute-start(bf16[384,768]{1,0:T(8,128)(2,1)S(1)} %add_convert_fusion.3), channel_id=1, source_target_pairs={{0,2},{1,3},{2,0},{3,1},{4,6},{5,7},{6,4},{7,5},{8,10},{9,11},{10,... | collective-permute-start | bytes 1769480 | tf_op jit(solution)/shard_map/ppermute | solution.py:134
  137.6 13.9 %collective-permute-done.24 = bf16[384,768]{1,0:T(8,128)(2,1)S(1)} collective-permute-done((bf16[384,768]{1,0:T(8,128)(2,1)S(1)}, bf16[384,768]{1,0:T(8,128)(2,1)S(1)}, u32[]{:S(2)}, u32[]{:S(2)}) %collective-permute-start.24) | collective-permute-done | bytes 589856 | tf_op jit(solution)/shard_map/ppermute | solution.py:134
  151.5 11.7 %collective-permute-done.18 = bf16[384,768]{1,0:T(8,128)(2,1)S(1)} collective-permute-done((bf16[384,768]{1,0:T(8,128)(2,1)S(1)}, bf16[384,768]{1,0:T(8,128)(2,1)S(1)}, u32[]{:S(2)}, u32[]{:S(2)}) %collective-permute-start.18) | collective-permute-done | bytes 589856 | tf_op jit(solution)/shard_map/ppermute | solution.py:134
  (125 shorter events, 23.9 us)
Async XLA Ops:
  0.0 14.1 %copy-start = (s32[16]{0:T(128)S(1)}, s32[16]{0:T(128)}, u32[]{:S(2)}) copy-start(s32[16]{0:T(128)} %param.15) | copy-start | bytes 196
  3.9 12.4 %collective-permute-start = (bf16[768,256]{1,0:T(8,128)(2,1)}, bf16[768,256]{1,0:T(8,128)(2,1)}, u32[]{:S(2)}, u32[]{:S(2)}) collective-permute-start(bf16[768,256]{1,0:T(8,128)(2,1)} %pad_maximum_fusion.9), channel_id=1, source_target_pairs={{0,4},{4,0},{8,12},{12,8},{16,20},{20,16},{24,28},{28,24},{1,5},{5... | collective-permute-start | bytes 1179656 | tf_op jit(solution)/shard_map/ppermute | solution.py:134
  16.3 34.0 %collective-permute-start.2 = (bf16[768,256]{1,0:T(8,128)(2,1)}, bf16[768,256]{1,0:T(8,128)(2,1)}, u32[]{:S(2)}, u32[]{:S(2)}) collective-permute-start(bf16[768,256]{1,0:T(8,128)(2,1)} %pad_maximum_fusion.7), channel_id=1, source_target_pairs={{0,4},{4,0},{8,12},{12,8},{16,20},{20,16},{24,28},{28,24},{1,5},{5... | collective-permute-start | bytes 1179656 | tf_op jit(solution)/shard_map/ppermute | solution.py:134
  18.0 18.9 %collective-permute-start.1 = (f32[2,768]{0,1:T(8,128)}, f32[2,768]{0,1:T(8,128)S(1)}, u32[]{:S(2)}, u32[]{:S(2)}) collective-permute-start(f32[2,768]{0,1:T(8,128)} %dynamic-slice_bitcast_fusion), channel_id=1, source_target_pairs={{0,4},{4,0},{8,12},{12,8},{16,20},{20,16},{24,28},{28,24},{1,5},{5... | collective-permute-start | bytes 18440 | tf_op jit(solution)/shard_map/ppermute | solution.py:134
  19.5 25.4 %collective-permute-start.3 = (bf16[768,256]{1,0:T(8,128)(2,1)S(1)}, bf16[768,256]{1,0:T(8,128)(2,1)S(1)}, u32[]{:S(2)}, u32[]{:S(2)}) collective-permute-start(bf16[768,256]{1,0:T(8,128)(2,1)S(1)} %get-tuple-element.75.refs_4_), channel_id=1, source_target_pairs={{0,8},{4,12},{8,16},{12,20},{16,24},{20,28},{24,0},{28,4},{1,9},{5... | collective-permute-start | bytes 1179656 | tf_op jit(solution)/shard_map/ppermute | solution.py:129
  21.3 22.4 %copy-start.10 = (bf16[768,128]{1,0:T(8,128)(2,1)S(1)}, bf16[768,128]{1,0:T(8,128)(2,1)}, u32[]{:S(2)}) copy-start(bf16[768,128]{1,0:T(8,128)(2,1)} %get-tuple-element.79) | copy-start | bytes 589828
  21.3 22.4 %copy-start.11 = (bf16[768,128]{1,0:T(8,128)(2,1)S(1)}, bf16[768,128]{1,0:T(8,128)(2,1)}, u32[]{:S(2)}) copy-start(bf16[768,128]{1,0:T(8,128)(2,1)} %get-tuple-element.83) | copy-start | bytes 589828
  21.3 23.6 %collective-permute-start.4 = (bf16[768,256]{1,0:T(8,128)(2,1)S(1)}, bf16[768,256]{1,0:T(8,128)(2,1)S(1)}, u32[]{:S(2)}, u32[]{:S(2)}) collective-permute-start(bf16[768,256]{1,0:T(8,128)(2,1)S(1)} %get-tuple-element.74.refs_3_), channel_id=1, source_target_pairs={{0,24},{4,28},{8,0},{12,4},{16,8},{20,12},{24,16},{28,20},{1,25},{... | collective-permute-start | bytes 1179656 | tf_op jit(solution)/shard_map/ppermute | solution.py:129
  23.4 20.3 %collective-permute-start.5 = (bf16[768,256]{1,0:T(8,128)(2,1)}, bf16[768,256]{1,0:T(8,128)(2,1)}, u32[]{:S(2)}, u32[]{:S(2)}) collective-permute-start(bf16[768,256]{1,0:T(8,128)(2,1)} %pad_maximum_fusion.8), channel_id=1, source_target_pairs={{0,4},{4,0},{8,12},{12,8},{16,20},{20,16},{24,28},{28,24},{1,5},{5... | collective-permute-start | bytes 1179656 | tf_op jit(solution)/shard_map/ppermute | solution.py:134
  37.1 13.1 %copy-start.9 = (bf16[768,128]{1,0:T(8,128)(2,1)S(1)}, bf16[768,128]{1,0:T(8,128)(2,1)}, u32[]{:S(2)}) copy-start(bf16[768,128]{1,0:T(8,128)(2,1)} %get-tuple-element.70) | copy-start | bytes 589828
  44.9 16.5 %collective-permute-start.7 = (bf16[768,256]{1,0:T(8,128)(2,1)S(1)}, bf16[768,256]{1,0:T(8,128)(2,1)S(1)}, u32[]{:S(2)}, u32[]{:S(2)}) collective-permute-start(bf16[768,256]{1,0:T(8,128)(2,1)S(1)} %get-tuple-element.30.refs_4_), channel_id=1, source_target_pairs={{0,8},{4,12},{8,16},{12,20},{16,24},{20,28},{24,0},{28,4},{1,9},{5... | collective-permute-start | bytes 1179656 | tf_op jit(solution)/shard_map/ppermute | solution.py:129
  46.5 17.2 %collective-permute-start.8 = (bf16[768,256]{1,0:T(8,128)(2,1)S(1)}, bf16[768,256]{1,0:T(8,128)(2,1)S(1)}, u32[]{:S(2)}, u32[]{:S(2)}) collective-permute-start(bf16[768,256]{1,0:T(8,128)(2,1)S(1)} %get-tuple-element.31.refs_3_), channel_id=1, source_target_pairs={{0,24},{4,28},{8,0},{12,4},{16,8},{20,12},{24,16},{28,20},{1,25},{... | collective-permute-start | bytes 1179656 | tf_op jit(solution)/shard_map/ppermute | solution.py:129
  48.8 12.4 %collective-permute-start.6 = (bf16[768,256]{1,0:T(8,128)(2,1)S(1)}, bf16[768,256]{1,0:T(8,128)(2,1)S(1)}, u32[]{:S(2)}, u32[]{:S(2)}) collective-permute-start(bf16[768,256]{1,0:T(8,128)(2,1)S(1)} %copy-done.14), channel_id=1, source_target_pairs={{0,4},{4,0},{8,12},{12,8},{16,20},{20,16},{24,28},{28,24},{1,5},{5... | collective-permute-start | bytes 1179656 | tf_op jit(solution)/shard_map/ppermute | solution.py:134
  63.7 61.4 %slice-start = ((s8[9437184]{0:T(1024)(128)(4,1)}), s8[1048576]{0:T(1024)(128)(4,1)S(1)}, s32[]{:S(2)}) async-start(s8[9437184]{0:T(1024)(128)(4,1)} %bitcast.83), calls=%async_computation | async-start | bytes 2097152
  63.7 61.4 %slice-start.1 = ((s8[9437184]{0:T(1024)(128)(4,1)}), s8[4194304]{0:T(1024)(128)(4,1)S(1)}, s32[]{:S(2)}) async-start(s8[9437184]{0:T(1024)(128)(4,1)} %bitcast.83), calls=%async_computation.1 | async-start | bytes 8388608
  73.6 26.1 %collective-permute-start.9 = (bf16[768,256]{1,0:T(8,128)(2,1)S(1)}, bf16[768,256]{1,0:T(8,128)(2,1)S(1)}, u32[]{:S(2)}, u32[]{:S(2)}) collective-permute-start(bf16[768,256]{1,0:T(8,128)(2,1)S(1)} %pad_maximum_fusion.15), channel_id=1, source_target_pairs={{0,4},{4,0},{8,12},{12,8},{16,20},{20,16},{24,28},{28,24},{1,5},{5... | collective-permute-start | bytes 1179656 | tf_op jit(solution)/shard_map/ppermute | solution.py:134
  75.1 13.9 %collective-permute-start.10 = (bf16[2,384,256]{2,1,0:T(8,128)(2,1)S(1)}, bf16[2,384,256]{2,1,0:T(8,128)(2,1)S(1)}, u32[]{:S(2)}, u32[]{:S(2)}) collective-permute-start(bf16[2,384,256]{2,1,0:T(8,128)(2,1)S(1)} %get-tuple-element.36), channel_id=1, source_target_pairs={{0,8},{4,12},{8,16},{12,20},{16,24},{20,28},{24,0},{28,4},{1,9},{5... | collective-permute-start | bytes 1179656 | tf_op jit(solution)/shard_map/ppermute | solution.py:129
  75.8 18.9 %collective-permute-start.11 = (bf16[2,384,256]{2,1,0:T(8,128)(2,1)S(1)}, bf16[2,384,256]{2,1,0:T(8,128)(2,1)S(1)}, u32[]{:S(2)}, u32[]{:S(2)}) collective-permute-start(bf16[2,384,256]{2,1,0:T(8,128)(2,1)S(1)} %get-tuple-element.37), channel_id=1, source_target_pairs={{0,24},{4,28},{8,0},{12,4},{16,8},{20,12},{24,16},{28,20},{1,25},{... | collective-permute-start | bytes 1179656 | tf_op jit(solution)/shard_map/ppermute | solution.py:129
  94.6 30.4 %slice-start.2 = ((s8[9437184]{0:T(1024)(128)(4,1)}), s8[4194304]{0:T(1024)(128)(4,1)S(1)}, s32[]{:S(2)}) async-start(s8[9437184]{0:T(1024)(128)(4,1)} %bitcast.83), calls=%async_computation.2 | async-start | bytes 8388608
  94.9 24.1 %collective-permute-start.14 = (bf16[768,256]{1,0:T(8,128)(2,1)S(1)}, bf16[768,256]{1,0:T(8,128)(2,1)S(1)}, u32[]{:S(2)}, u32[]{:S(2)}) collective-permute-start(bf16[768,256]{1,0:T(8,128)(2,1)S(1)} %pad_maximum_fusion.16), channel_id=1, source_target_pairs={{0,4},{4,0},{8,12},{12,8},{16,20},{20,16},{24,28},{28,24},{1,5},{5... | collective-permute-start | bytes 1179656 | tf_op jit(solution)/shard_map/ppermute | solution.py:134
  95.9 9.6 %collective-permute-start.12 = (bf16[384,256]{1,0:T(8,128)(2,1)S(1)}, bf16[384,256]{1,0:T(8,128)(2,1)S(1)}, u32[]{:S(2)}, u32[]{:S(2)}) collective-permute-start(bf16[384,256]{1,0:T(8,128)(2,1)S(1)} %get-tuple-element.41), channel_id=1, source_target_pairs={{0,8},{4,12},{8,16},{12,20},{16,24},{20,28},{24,0},{28,4},{1,9},{5... | collective-permute-start | bytes 589832 | tf_op jit(solution)/shard_map/ppermute | solution.py:129
  96.1 10.1 %collective-permute-start.13 = (bf16[384,256]{1,0:T(8,128)(2,1)S(1)}, bf16[384,256]{1,0:T(8,128)(2,1)S(1)}, u32[]{:S(2)}, u32[]{:S(2)}) collective-permute-start(bf16[384,256]{1,0:T(8,128)(2,1)S(1)} %get-tuple-element.42), channel_id=1, source_target_pairs={{0,24},{4,28},{8,0},{12,4},{16,8},{20,12},{24,16},{28,20},{1,25},{... | collective-permute-start | bytes 589832 | tf_op jit(solution)/shard_map/ppermute | solution.py:129
  106.2 8.5 %collective-permute-start.19 = (bf16[384,256]{1,0:T(8,128)(2,1)S(1)}, bf16[384,256]{1,0:T(8,128)(2,1)S(1)}, u32[]{:S(2)}, u32[]{:S(2)}) collective-permute-start(bf16[384,256]{1,0:T(8,128)(2,1)S(1)} %get-tuple-element.43), channel_id=1, source_target_pairs={{0,8},{4,12},{8,16},{12,20},{16,24},{20,28},{24,0},{28,4},{1,9},{5... | collective-permute-start | bytes 589832 | tf_op jit(solution)/shard_map/ppermute | solution.py:129
  106.6 10.0 %collective-permute-start.20 = (bf16[384,256]{1,0:T(8,128)(2,1)S(1)}, bf16[384,256]{1,0:T(8,128)(2,1)S(1)}, u32[]{:S(2)}, u32[]{:S(2)}) collective-permute-start(bf16[384,256]{1,0:T(8,128)(2,1)S(1)} %get-tuple-element.44), channel_id=1, source_target_pairs={{0,24},{4,28},{8,0},{12,4},{16,8},{20,12},{24,16},{28,20},{1,25},{... | collective-permute-start | bytes 589832 | tf_op jit(solution)/shard_map/ppermute | solution.py:129
  116.9 7.9 %collective-permute-start.21 = (bf16[384,256]{1,0:T(8,128)(2,1)S(1)}, bf16[384,256]{1,0:T(8,128)(2,1)S(1)}, u32[]{:S(2)}, u32[]{:S(2)}) collective-permute-start(bf16[384,256]{1,0:T(8,128)(2,1)S(1)} %get-tuple-element.53), channel_id=1, source_target_pairs={{0,4},{4,0},{8,12},{12,8},{16,20},{20,16},{24,28},{28,24},{1,5},{5... | collective-permute-start | bytes 589832 | tf_op jit(solution)/shard_map/ppermute | solution.py:134
  117.0 12.9 %collective-permute-start.15 = (bf16[384,256]{1,0:T(8,128)(2,1)S(1)}, bf16[384,256]{1,0:T(8,128)(2,1)S(1)}, u32[]{:S(2)}, u32[]{:S(2)}) collective-permute-start(bf16[384,256]{1,0:T(8,128)(2,1)S(1)} %get-tuple-element.56), channel_id=1, source_target_pairs={{0,4},{4,0},{8,12},{12,8},{16,20},{20,16},{24,28},{28,24},{1,5},{5... | collective-permute-start | bytes 589832 | tf_op jit(solution)/shard_map/ppermute | solution.py:134
  127.2 10.4 %collective-permute-start.22 = (bf16[384,768]{1,0:T(8,128)(2,1)S(1)}, bf16[384,768]{1,0:T(8,128)(2,1)S(1)}, u32[]{:S(2)}, u32[]{:S(2)}) collective-permute-start(bf16[384,768]{1,0:T(8,128)(2,1)S(1)} %constant_dynamic-slice_fusion.1), channel_id=1, source_target_pairs={{0,1},{1,0},{2,3},{3,2},{4,5},{5,4},{6,7},{7,6},{8,9},{9,8},{10,11... | collective-permute-start | bytes 1769480 | tf_op jit(solution)/shard_map/ppermute | solution.py:134
  129.4 5.7 %collective-permute-start.23 = (bf16[384,768]{1,0:T(8,128)(2,1)S(1)}, bf16[384,768]{1,0:T(8,128)(2,1)S(1)}, u32[]{:S(2)}, u32[]{:S(2)}) collective-permute-start(bf16[384,768]{1,0:T(8,128)(2,1)S(1)} %constant_dynamic-slice_fusion), channel_id=1, source_target_pairs={{0,1},{1,0},{2,3},{3,2},{4,5},{5,4},{6,7},{7,6},{8,9},{9,8},{10,11... | collective-permute-start | bytes 1769480 | tf_op jit(solution)/shard_map/ppermute | solution.py:134
  132.3 3.1 %collective-permute-start.17 = (bf16[384,768]{1,0:T(8,128)(2,1)S(1)}, bf16[384,768]{1,0:T(8,128)(2,1)S(1)}, u32[]{:S(2)}, u32[]{:S(2)}) collective-permute-start(bf16[384,768]{1,0:T(8,128)(2,1)S(1)} %constant_dynamic-slice_fusion.2), channel_id=1, source_target_pairs={{0,1},{1,0},{2,3},{3,2},{4,5},{5,4},{6,7},{7,6},{8,9},{9,8},{10,11... | collective-permute-start | bytes 1769480 | tf_op jit(solution)/shard_map/ppermute | solution.py:134
  134.5 3.0 %collective-permute-start.16 = (bf16[384,768]{1,0:T(8,128)(2,1)S(1)}, bf16[384,768]{1,0:T(8,128)(2,1)S(1)}, u32[]{:S(2)}, u32[]{:S(2)}) collective-permute-start(bf16[384,768]{1,0:T(8,128)(2,1)S(1)} %constant_dynamic-slice_fusion.3), channel_id=1, source_target_pairs={{0,1},{1,0},{2,3},{3,2},{4,5},{5,4},{6,7},{7,6},{8,9},{9,8},{10,11... | collective-permute-start | bytes 1769480 | tf_op jit(solution)/shard_map/ppermute | solution.py:134
  135.3 16.3 %collective-permute-start.24 = (bf16[384,768]{1,0:T(8,128)(2,1)S(1)}, bf16[384,768]{1,0:T(8,128)(2,1)S(1)}, u32[]{:S(2)}, u32[]{:S(2)}) collective-permute-start(bf16[384,768]{1,0:T(8,128)(2,1)S(1)} %add_convert_fusion.1), channel_id=1, source_target_pairs={{0,2},{1,3},{2,0},{3,1},{4,6},{5,7},{6,4},{7,5},{8,10},{9,11},{10,... | collective-permute-start | bytes 1769480 | tf_op jit(solution)/shard_map/ppermute | solution.py:134
  135.6 27.6 %collective-permute-start.18 = (bf16[384,768]{1,0:T(8,128)(2,1)S(1)}, bf16[384,768]{1,0:T(8,128)(2,1)S(1)}, u32[]{:S(2)}, u32[]{:S(2)}) collective-permute-start(bf16[384,768]{1,0:T(8,128)(2,1)S(1)} %add_convert_fusion.3), channel_id=1, source_target_pairs={{0,2},{1,3},{2,0},{3,1},{4,6},{5,7},{6,4},{7,5},{8,10},{9,11},{10,... | collective-permute-start | bytes 1769480 | tf_op jit(solution)/shard_map/ppermute | solution.py:134
  (12 other events, 54.4 us)

commit v3 on v2

v3 whole, which is shorter than its diff:
```python
import functools
import math

import jax
import jax.numpy as jnp
from jax import lax
from jax.experimental import pallas as pl
from jax.experimental.pallas import tpu as pltpu
from jax.sharding import PartitionSpec as P

HD = 128
TILE = 384
NB = 4
HALO = 2
F32 = jnp.float32
BF16 = jnp.bfloat16


def dot(a, b, dims):
    return lax.dot_general(a, b, ((dims[:1], dims[1:]), ((), ())), preferred_element_type=F32)


def attention_kernel(own_blocks, slots_ref, counts_ref, odd_ref, delta_ref, *refs):
    n = own_blocks
    tiles = n * HALO
    qg_refs, kv_refs, refs = refs[:n], refs[n : 2 * n + 2], refs[2 * n + 2 :]
    query_grad_refs, kv_grad_refs, refs = refs[:n], refs[n : 2 * n + 2], refs[2 * n + 2 :]
    qg, kv, query_acc, key_acc, value_acc, work = refs
    rows_block = HALO * TILE
    if n == 2:
        odd = odd_ref[0]
        places = [1 + odd, 2 - odd, 3 * (1 - odd), 3 * odd]
        flips = [odd, 1 - odd, odd, 1 - odd]
    else:
        places, flips = [1, 0, 2], [0, 0, 0]

    def tile_rows(place, flip, at):
        in_block = flip if at == 0 else 1 - flip
        return pl.ds(pl.multiple_of((place * HALO + in_block) * TILE, TILE), TILE)

    for place, ref in zip(places, qg_refs):
        qg[pl.ds(pl.multiple_of((place - 1) * rows_block, TILE), rows_block), :] = ref[...]
    for place, ref in zip(places, kv_refs):
        kv[pl.ds(pl.multiple_of(place * rows_block, TILE), rows_block), :] = ref[...]
    key_acc[...] = jnp.zeros_like(key_acc)
    value_acc[...] = jnp.zeros_like(value_acc)
    scale = HD ** (-0.5)
    exponent = scale * math.log2(math.e)

    def tile_step(tile, slot_places):
        base = pl.multiple_of(tile * TILE, TILE)
        query = qg[pl.ds(base, TILE), :HD]
        grad = qg[pl.ds(base, TILE), HD:]
        delta = delta_ref[tile]
        starts = [pl.multiple_of(place * TILE, TILE) for place in slot_places]
        peak = None
        for j, start in enumerate(starts):
            scores = dot(kv[pl.ds(start, TILE), :HD], query, (1, 1))
            work[j] = scores
            top = jnp.max(scores, axis=0, keepdims=True)
            peak = top if peak is None else jnp.maximum(peak, top)
        total = jnp.zeros_like(peak)
        for j in range(len(starts)):
            raised = jnp.exp2((work[j] - peak) * exponent)
            work[j] = raised
            total = total + jnp.sum(raised, axis=0, keepdims=True)
        inverse = 1.0 / total
        query_grad = jnp.zeros((HD, TILE), F32)
        for j, start in enumerate(starts):
            keys = kv[pl.ds(start, TILE), :HD]
            weights = (work[j] * inverse).astype(BF16)
            prob_grad = dot(kv[pl.ds(start, TILE), HD:], grad, (1, 1))
            score_grad = (weights.astype(F32) * ((prob_grad - delta) * scale)).astype(BF16)
            value_acc[pl.ds(start, TILE), :] += dot(weights, grad, (1, 0))
            key_acc[pl.ds(start, TILE), :] += dot(score_grad, query, (1, 0))
            query_grad = query_grad + dot(keys, score_grad, (0, 0))
        query_acc[pl.ds(base, TILE), :] = query_grad.T.astype(BF16)

    @pl.loop(0, tiles)
    def _(tile):
        near = [tile + HALO, tile + HALO - 1, tile + HALO + 1]

        @pl.when(counts_ref[tile] >= NB)
        def _():
            tile_step(tile, near + [slots_ref[tile * NB + NB - 1]])

        @pl.when(counts_ref[tile] < NB)
        def _():
            tile_step(tile, near)

    for at in range(HALO):
        for place, flip, ref in zip(places, flips, query_grad_refs):
            ref[at] = query_acc[tile_rows(place - 1, flip, at), :]
        for place, flip, ref in zip(places, flips, kv_grad_refs):
            rows = tile_rows(place, flip, at)
            ref[at, :, :HD] = key_acc[rows, :].astype(ref.dtype)
            ref[at, :, HD:] = value_acc[rows, :].astype(ref.dtype)


def attention(slots, counts, odd, delta, qg_blocks, kv_blocks):
    n = len(qg_blocks)
    tiles = n * HALO
    rows = tiles * TILE
    window = rows + 2 * HALO * TILE
    vmem = pl.BlockSpec(memory_space=pltpu.VMEM)
    smem = pl.BlockSpec(memory_space=pltpu.SMEM)

    def blocks(count, width, dtype):
        return [jax.ShapeDtypeStruct((HALO, TILE, width), dtype)] * count

    out = pl.pallas_call(
        functools.partial(attention_kernel, n),
        out_shape=blocks(n, HD, BF16) + blocks(n, 2 * HD, F32) + blocks(2, 2 * HD, BF16),
        in_specs=[smem] * 3 + [vmem] * (1 + len(qg_blocks) + len(kv_blocks)),
        out_specs=[vmem] * (2 * n + 2),
        scratch_shapes=[
            pltpu.VMEM((rows, 2 * HD), BF16),
            pltpu.VMEM((window, 2 * HD), BF16),
            pltpu.VMEM((rows, HD), BF16),
            pltpu.VMEM((window, HD), F32),
            pltpu.VMEM((window, HD), F32),
            pltpu.VMEM((NB, TILE, TILE), F32),
        ],
        compiler_params=pltpu.CompilerParams(vmem_limit_bytes=40 * 2**20),
        cost_estimate=pl.CostEstimate(
            flops=2 * 5 * rows * NB * TILE * HD * 2,
            bytes_accessed=rows * HD * 30,
            transcendentals=rows * NB * TILE,
        ),
    )(slots.reshape(-1), counts, odd, delta.reshape(tiles, 1, TILE), *qg_blocks, *kv_blocks)
    return out[:n], out[n : 2 * n], out[2 * n :]


def shifted(block, axis, distance):
    count = lax.axis_size(axis)
    return lax.ppermute(block, axis, [(i, (i + distance) % count) for i in range(count)])


def swapped(block, axis, bit):
    count = lax.axis_size(axis)
    return lax.ppermute(block, axis, [(i, i ^ bit) for i in range(count)])


def head_cols(array, head):
    return lax.dynamic_slice_in_dim(array, head * HD, HD, 1)


def tables(neighbours, counts, first, tiles, tiles_all):
    ids = first + jnp.arange(tiles)
    slots = (neighbours[ids] - (first - HALO)) % tiles_all
    return slots.astype(jnp.int32), counts[ids].astype(jnp.int32)


def chip_sum(stack, projection, target):
    core = lax.axis_index("head") % 2
    width = projection.shape[2] // 4
    weights = lax.dynamic_slice_in_dim(projection, target * 2 * width, 2 * width, 2)
    term = jnp.einsum("cik,ckm->im", stack, weights, preferred_element_type=F32).astype(BF16)
    sent = lax.dynamic_slice_in_dim(term, (1 - core) * width, width, 1)
    kept = lax.dynamic_slice_in_dim(term, core * width, width, 1)
    return kept.astype(F32) + swapped(sent, "head", 1).astype(F32)


def scattered_over_heads(stack, projection):
    term = jnp.einsum("cik,ckm->im", stack, projection, preferred_element_type=F32)
    return lax.psum_scatter(term.astype(BF16), "head", scatter_dimension=1, tiled=True)


def after(arrays, awaited):
    return lax.optimization_barrier((tuple(arrays), tuple(awaited)))[0]


def local(
    query_rows, key_rows, value_rows, output_rows, output_grad, projection, neighbours, counts
):
    seq_count = lax.axis_size("seq")
    place = lax.axis_index("seq")
    rows_dev = query_rows.shape[0]
    tiles_dev = rows_dev // TILE
    tiles_all = tiles_dev * seq_count
    heads_dev = query_rows.shape[1] // HD
    deltas = jnp.sum(
        (output_grad.astype(F32) * output_rows.astype(F32)).reshape(rows_dev, heads_dev, HD), axis=-1
    ).T
    if heads_dev % 2 or seq_count % 2 or tiles_dev != HALO:
        grads = ([], [], [])
        slots, live = tables(neighbours, counts, place * tiles_dev, tiles_dev, tiles_all)
        for head in range(heads_dev):
            qg = jnp.concatenate([head_cols(query_rows, head), head_cols(output_grad, head)], 1)
            kv = jnp.concatenate([head_cols(key_rows, head), head_cols(value_rows, head)], 1)
            window = [kv, shifted(kv, "seq", 1), shifted(kv, "seq", -1)]
            (query_grad,), (own,), (to_prev, to_next) = attention(
                slots, live, jnp.zeros((1,), jnp.int32), deltas[head], [qg], window
            )
            own = own + shifted(to_prev, "seq", -1).astype(F32) + shifted(to_next, "seq", 1).astype(F32)
            own = own.astype(BF16).reshape(rows_dev, 2 * HD)
            query_grad = query_grad.reshape(rows_dev, HD)
            for into, block in zip(grads, (query_grad, own[:, :HD], own[:, HD:])):
                into.append(block)
        stack = jnp.stack([jnp.concatenate(blocks, 1) for blocks in grads])
        return scattered_over_heads(stack, projection)

    odd = place % 2
    even = odd == 0
    half = heads_dev // 2
    first = (place - odd) * tiles_dev
    slots, live = tables(neighbours, counts, first, 2 * tiles_dev, tiles_all)

    def in_order(mine, other):
        return jnp.where(even, mine, other), jnp.where(even, other, mine)

    def both(left, right, head):
        return jnp.concatenate([head_cols(left, head), head_cols(right, head)], 1)

    kept, sent = odd * half, (1 - odd) * half
    kv_kept = [both(key_rows, value_rows, kept + step) for step in range(half)]
    kv_sent = [both(key_rows, value_rows, sent + step) for step in range(half)]
    qg_kept = [both(query_rows, output_grad, kept + step) for step in range(half)]
    qg_sent = [both(query_rows, output_grad, sent + step) for step in range(half)]

    def outward(block, sign):
        route = [(i, (i + 2 * sign * (2 * (i % 2) - 1)) % seq_count) for i in range(seq_count)]
        return lax.ppermute(block, "seq", route)

    kv_got = [swapped(kv_sent[0], "seq", 1)]
    halos = [(outward(kv_kept[0], 1), outward(kv_got[0], -1))]
    delta_sent = lax.dynamic_slice_in_dim(deltas, sent, half, 0)
    qg_got = []
    for step in range(half):
        wave = [qg_sent[step]] + kv_sent[step + 1 : step + 2]
        if step == 0:
            wave.append(delta_sent)
        wave = [swapped(block, "seq", 1) for block in after(wave, [kv_got[step]])]
        qg_got.append(wave[0])
        if step == 0:
            delta_got = wave[-1]
        if step + 1 < half:
            kv_got.append(wave[1])
            (own_block,) = after([kv_kept[step + 1]], [halos[step][0]])
            (got_block,) = after([kv_got[step + 1]], [halos[step][1]])
            halos.append((outward(own_block, 1), outward(got_block, -1)))
    delta_kept = lax.dynamic_slice_in_dim(deltas, kept, half, 0)
    delta_pair = jnp.concatenate(in_order(delta_kept, delta_got), 1)
    odd_ref = odd.astype(jnp.int32).reshape(1)

    query_mine, query_sent, kv_mine, kv_other = [], [], [], []
    for step in range(half):
        window = [kv_kept[step], kv_got[step], *halos[step]]
        query_grad, (own, other), (back_own, back_other) = attention(
            slots, live, odd_ref, delta_pair[step], [qg_kept[step], qg_got[step]], window
        )
        query_mine.append(query_grad[0])
        query_sent.append(query_grad[1])
        if step + 1 < half:
            back_other, back_own = outward(back_other, 1), outward(back_own, -1)
            kv_mine.append((own + back_own.astype(F32)).astype(BF16))
            kv_other.append(swapped((other + back_other.astype(F32)).astype(BF16), "seq", 1))
        else:
            mine, others = [], []
            near = None
            for at in range(HALO):
                pair = back_other[at], back_own[at]
                if near is not None:
                    pair = [after([block], [before])[0] for block, before in zip(pair, near)]
                near = outward(pair[0], 1), outward(pair[1], -1)
                others.append(swapped((other[at] + near[0].astype(F32)).astype(BF16), "seq", 1))
                mine.append((own[at] + near[1].astype(F32)).astype(BF16))
            kv_mine.append(mine)
            kv_other.append(others)
    query_got = swapped(jnp.concatenate(query_sent, 2), "seq", 1)

    chip = lax.axis_index("head") // 2
    results = []
    sent_sum = None
    for at in range(HALO):
        parts = [in_order(jnp.concatenate([block[at] for block in query_mine], 1), query_got[at])]
        for cols in (slice(0, HD), slice(HD, 2 * HD)):
            parts.append(
                in_order(
                    jnp.concatenate([blocks[at][:, cols] for blocks in kv_mine], 1),
                    jnp.concatenate([blocks[at][:, cols] for blocks in kv_other], 1),
                )
            )
        if lax.axis_size("head") != 4:
            stack = jnp.stack([jnp.concatenate(part, 1) for part in parts])
            results.append(scattered_over_heads(stack, projection))
            continue
        if sent_sum is not None:
            parts = [after(part, [sent_sum]) for part in parts]
        stack = jnp.stack([jnp.concatenate(part, 1) for part in parts])
        sent_sum = chip_sum(stack, projection, 1 - chip).astype(BF16)
        far = swapped(sent_sum, "head", 2)
        results.append((stack, far))
    if lax.axis_size("head") == 4:
        results = [
            (chip_sum(stack, projection, chip) + far.astype(F32)).astype(BF16)
            for stack, far in results
        ]
    return jnp.concatenate(in_order(results[0], results[1]), 0)


def solution(mesh):
    in_specs = (
        P("seq", "head"),
        P("seq", "head"),
        P("seq", "head"),
        P("seq", "head"),
        P("seq", "head"),
        P(None, "head", None),
        P(),
        P(),
    )
    out_specs = P("seq", "head")
    return jax.shard_map(local, mesh=mesh, in_specs=in_specs, out_specs=out_specs, check_vma=False)
```

time: 165 us -> 140 us (0.85)
  waiting for transfers between devices: 80.9 us -> 58.3 us
  starting transfers between devices: 35.4 us -> 26.5 us
  other arithmetic: 11.4 us -> 15.5 us
  local copies, waits for them, and re-layouts: 9.05 us -> 11.5 us
    ppermute x10, waiting for transfers between devices: 30.8 us -> 16.1 us  [outward(): return lax.ppermute(block, 'seq', route)]
    ppermute x15, waiting for transfers between devices: 50.1 us -> 42.2 us  [swapped(): return lax.ppermute(block, axis, [(i, i ^ bit) for i in range(count)])]
    ppermute x10, starting transfers between devices: 19.3 us -> 14.2 us  [outward(): return lax.ppermute(block, 'seq', route)]
    ppermute x15, starting transfers between devices: 16.1 us -> 12.3 us  [swapped(): return lax.ppermute(block, axis, [(i, i ^ bit) for i in range(count)])]
    select_n x2, local copies, waits for them, and re-layouts: 0.3 us -> 3.48 us  [in_order(): return (jnp.where(even, mine, other), jnp.where(even, other, mine))]
    concatenate x4 -> x8, other arithmetic: 3.25 us -> 6.37 us  [both(): return jnp.concatenate([head_cols(left, head), head_cols(right, head)], 1)]
    dynamic_slice x4 -> x2, local copies, waits for them, and re-layouts: 5.28 us -> 2.81 us  [head_cols(): return lax.dynamic_slice_in_dim(array, head * HD, HD, 1)]
    select_n x10 -> x8, other arithmetic: 4.86 us -> 3.35 us  [in_order(): return (jnp.where(even, mine, other), jnp.where(even, other, mine))]
  transfers between devices with their start and end apart: 25 -> 25, of which waited for: 13 -> 13; matrix products, arithmetic and copies ran while one was open for 14% -> 20% of each run, Pallas kernels for 6% -> 14%
where the time goes in v3:
time: 140 us; the launch traced here: 139 us
  waiting for transfers between devices  58.3 us (42%)
  starting transfers between devices  26.5 us (19%)
  Pallas kernels  18.8 us (13%)
  other arithmetic  15.5 us (11%)
  local copies, waits for them, and re-layouts  11.5 us (8%)
  matrix products  8.1 us (6%)
    ppermute x15, waiting for transfers between devices, swapped(): return lax.ppermute(block, axis, [(i, i ^ bit) for i in range(count)])  42.2 us
    pallas_call x2, Pallas kernels, attention(): pl.pallas_call(functools.partial(attention_kernel, n), out_shape=blocks(n...  18.8 us
    ppermute x10, waiting for transfers between devices, outward(): return lax.ppermute(block, 'seq', route)  16.1 us
    ppermute x10, starting transfers between devices, outward(): return lax.ppermute(block, 'seq', route)  14.2 us
    ppermute x15, starting transfers between devices, swapped(): return lax.ppermute(block, axis, [(i, i ^ bit) for i in range(count)])  12.3 us
    dot_general x4, matrix products, chip_sum(): jnp.einsum('cik,ckm->im', stack, weights, preferred_element_type=F32)  8.1 us
    concatenate x8, other arithmetic, both(): return jnp.concatenate([head_cols(left, head), head_cols(right, head)], 1)  6.37 us
    select_n x2, local copies, waits for them, and re-layouts, in_order(): return (jnp.where(even, mine, other), jnp.where(even, other, mine))  3.48 us
  transfers between devices with their start and end apart: 25, of which 13 were waited for; matrix products, arithmetic and copies ran while one was open for 20% of the time, Pallas kernels for 14%

profile of v3, /device:TPU:0, one launch (start us, length us, event | category | flops | bytes accessed | tf_op | source)
XLA Modules:
  0.0 139.4 jit_solution(14108750029621003964)
XLA Ops:
  0.0 1.6 %constant_dynamic-slice_fusion.10 = (bf16[768,128]{1,0:T(8,128)(2,1)S(1)}, bf16[768,128]{1,0:T(8,128)(2,1)S(1)}, bf16[768,128]{1,0:T(8,128)(2,1)S(1)}, bf16[768,...) fusion(bf16[768,512]{1,0:T(8,128)(2,1)} %param.10, ...), kind=kLoop, calls=%fused_computation.108 | loop fusion | bytes 3145744 | tf_op jit(solution)/shard_map/dynamic_slice | solution.py:145
  2.5 3.0 %collective-permute-start = (bf16[768,256]{1,0:T(8,128)(2,1)}, bf16[768,256]{1,0:T(8,128)(2,1)S(1)}, u32[]{:S(2)}, u32[]{:S(2)}) collective-permute-start(bf16[768,256]{1,0:T(8,128)(2,1)} %pad_maximum_fusion.9), channel_id=1, source_target_pairs={{0,4},{4,0},{8,12},{12,8},{16,20},{20,16},{24,28},{28,24},{1,5},{5... | collective-permute-start | bytes 1179656 | tf_op jit(solution)/shard_map/ppermute | solution.py:141
  5.5 3.7 %collective-permute-start.3 = (bf16[768,256]{1,0:T(8,128)(2,1)S(1)}, bf16[768,256]{1,0:T(8,128)(2,1)S(1)}, u32[]{:S(2)}, u32[]{:S(2)}) collective-permute-start(bf16[768,256]{1,0:T(8,128)(2,1)S(1)} %pad_maximum_fusion.11.refs_2_), channel_id=1, source_target_pairs={{0,24},{4,12},{8,0},{12,20},{16,8},{20,28},{24,16},{28,4},{1,25},{... | collective-permute-start | bytes 1179656 | tf_op jit(solution)/shard_map/ppermute | solution.py:223
  12.8 1.8 %reshape.28 = f32[768,4,128]{2,1,0:T(4,128)S(1)} reshape(f32[768,512]{1,0:T(8,128)} %convert_multiply_fusion) | data formatting | bytes 3145728 | tf_op jit(solution)/shard_map/reshape | solution.py:183
  15.3 1.8 %pad_maximum_fusion.7 = bf16[768,256]{1,0:T(8,128)(2,1)} fusion(bf16[768,128]{1,0:T(8,128)(2,1)} %get-tuple-element.69, bf16[768,128]{1,0:T(8,128)(2,1)} %get-tuple-element.132), kind=kLoop, calls=%fused_computation.30 | loop fusion | flops 786432 | bytes 786432 | tf_op jit(solution)/shard_map/concatenate | solution.py:213
  23.7 2.0 %collective-permute-start.5 = (bf16[768,256]{1,0:T(8,128)(2,1)}, bf16[768,256]{1,0:T(8,128)(2,1)S(1)}, u32[]{:S(2)}, u32[]{:S(2)}) collective-permute-start(bf16[768,256]{1,0:T(8,128)(2,1)} %pad_maximum_fusion.8), channel_id=1, source_target_pairs={{0,4},{4,0},{8,12},{12,8},{16,20},{20,16},{24,28},{28,24},{1,5},{5... | collective-permute-start | bytes 1179656 | tf_op jit(solution)/shard_map/ppermute | solution.py:141
  27.8 6.5 %collective-permute-done.1 = f32[2,768]{0,1:T(8,128)} collective-permute-done((f32[2,768]{0,1:T(8,128)}, f32[2,768]{0,1:T(8,128)}, u32[]{:S(2)}, u32[]{:S(2)}) %collective-permute-start.1) | collective-permute-done | bytes 6176 | tf_op jit(solution)/shard_map/ppermute | solution.py:141
  34.3 2.2 %bitcast_select_fusion.1 = (f32[2,768]{0,1:T(8,128)}, f32[2,768]{0,1:T(8,128)}) fusion(f32[2,768]{0,1:T(8,128)} %collective-permute-done.1, f32[768,4]{1,0:T(8,128)} %copy-done.1, s32[]{:T(128)S(6)} %select_n.171, pred[]{:T(512)S(6)} %eq.11), kind=kLoop, calls=%fused_computation.54 | loop fusion | flops 3072 | bytes 24581 | tf_op jit(solution)/shard_map/jit(_where)/select_n | solution.py:210
  36.5 1.7 %copy.16 = f32[2,768]{1,0:T(2,128)} copy(f32[2,768]{0,1:T(8,128)} %get-tuple-element.80) | data formatting | bytes 12288 | tf_op jit(solution)/shard_map/jit(_where)/select_n | solution.py:210
  38.2 1.7 %copy.17 = f32[2,768]{1,0:T(2,128)} copy(f32[2,768]{0,1:T(8,128)} %get-tuple-element.81) | data formatting | bytes 12288 | tf_op jit(solution)/shard_map/jit(_where)/select_n | solution.py:210
  40.7 1.9 %collective-permute-done.5.refs_3_ = bf16[768,256]{1,0:T(8,128)(2,1)S(1)} collective-permute-done((bf16[768,256]{1,0:T(8,128)(2,1)}, bf16[768,256]{1,0:T(8,128)(2,1)S(1)}, u32[]{:S(2)}, u32[]{:S(2)}) %collective-permute-start.5) | collective-permute-done | bytes 393248 | tf_op jit(solution)/shard_map/ppermute | solution.py:141
  43.0 1.6 %collective-permute-start.8 = (bf16[768,256]{1,0:T(8,128)(2,1)S(1)}, bf16[768,256]{1,0:T(8,128)(2,1)S(1)}, u32[]{:S(2)}, u32[]{:S(2)}) collective-permute-start(bf16[768,256]{1,0:T(8,128)(2,1)S(1)} %collective-permute-done.5.refs_3_), channel_id=1, source_target_pairs={{0,8},{4,28},{8,16},{12,4},{16,24},{20,12},{24,0},{28,20},{1,9},{5... | collective-permute-start | bytes 1179656 | tf_op jit(solution)/shard_map/ppermute | solution.py:223
  44.6 6.5 %collective-permute-done.2.refs_1_ = bf16[768,256]{1,0:T(8,128)(2,1)S(1)} collective-permute-done((bf16[768,256]{1,0:T(8,128)(2,1)}, bf16[768,256]{1,0:T(8,128)(2,1)S(1)}, u32[]{:S(2)}, u32[]{:S(2)}) %collective-permute-start.2) | collective-permute-done | bytes 393248 | tf_op jit(solution)/shard_map/ppermute | solution.py:141
  51.0 9.7 %shard_map.82 = (bf16[2,384,128]{2,1,0:T(8,128)(2,1)S(1)}, bf16[2,384,128]{2,1,0:T(8,128)(2,1)S(1)}, f32[2,384,256]{2,1,0:T(8,128)S(1)}, f32[2,384,256]{2,1,0:T(...) custom-call(s32[16]{0:T(128)S(1)} %and_select_fusion.slots_ref, s32[4]{0:T(128)S(1)} %gather_fusion.1, ...), custom_call_target="tpu_custom_call" | custom-call | flops 6039797760 | bytes 5898240 | tf_op jit(solution)/shard_map/pallas_call | solution.py:111
  61.2 1.6 %collective-permute-start.10 = (bf16[2,384,256]{2,1,0:T(8,128)(2,1)S(1)}, bf16[2,384,256]{2,1,0:T(8,128)(2,1)S(1)}, u32[]{:S(2)}, u32[]{:S(2)}) collective-permute-start(bf16[2,384,256]{2,1,0:T(8,128)(2,1)S(1)} %get-tuple-element.42), channel_id=1, source_target_pairs={{0,8},{4,28},{8,16},{12,4},{16,24},{20,12},{24,0},{28,20},{1,9},{5... | collective-permute-start | bytes 1179656 | tf_op jit(solution)/shard_map/ppermute | solution.py:223
  62.8 9.2 %shard_map.83 = (bf16[2,384,128]{2,1,0:T(8,128)(2,1)S(1)}, bf16[2,384,128]{2,1,0:T(8,128)(2,1)S(1)}, f32[2,384,256]{2,1,0:T(8,128)S(1)}, f32[2,384,256]{2,1,0:T(...) custom-call(s32[16]{0:T(128)S(1)} %and_select_fusion.slots_ref, s32[4]{0:T(128)S(1)} %gather_fusion.1, ...), custom_call_target="tpu_custom_call" | custom-call | flops 6039797760 | bytes 5898240 | tf_op jit(solution)/shard_map/pallas_call | solution.py:111
  72.1 2.3 %collective-permute-start.14 = (bf16[384,256]{1,0:T(8,128)(2,1)S(1)}, bf16[384,256]{1,0:T(8,128)(2,1)S(1)}, u32[]{:S(2)}, u32[]{:S(2)}) collective-permute-start(bf16[384,256]{1,0:T(8,128)(2,1)S(1)} %get-tuple-element.99), channel_id=1, source_target_pairs={{0,24},{4,12},{8,0},{12,20},{16,8},{20,28},{24,16},{28,4},{1,25},{... | collective-permute-start | bytes 589832 | tf_op jit(solution)/shard_map/ppermute | solution.py:223
  74.4 6.0 %collective-permute-done.12 = bf16[2,384,256]{2,1,0:T(8,128)(2,1)S(1)} collective-permute-done((bf16[2,384,256]{2,1,0:T(8,128)(2,1)S(1)}, bf16[2,384,256]{2,1,0:T(8,128)(2,1)S(1)}, u32[]{:S(2)}, u32[]{:S(2)}) %collective-permute-start.12) | collective-permute-done | bytes 393248 | tf_op jit(solution)/shard_map/ppermute | solution.py:223
  80.9 2.1 %collective-permute-start.9 = (bf16[2,384,256]{2,1,0:T(8,128)(2,1)S(1)}, bf16[2,384,256]{2,1,0:T(8,128)(2,1)S(1)}, u32[]{:S(2)}, u32[]{:S(2)}) collective-permute-start(bf16[2,384,256]{2,1,0:T(8,128)(2,1)S(1)} %pad_maximum_fusion.15), channel_id=1, source_target_pairs={{0,4},{4,0},{8,12},{12,8},{16,20},{20,16},{24,28},{28,24},{1,5},{5... | collective-permute-start | bytes 1179656 | tf_op jit(solution)/shard_map/ppermute | solution.py:141
  83.1 2.4 %collective-permute-start.20 = (bf16[384,256]{1,0:T(8,128)(2,1)S(1)}, bf16[384,256]{1,0:T(8,128)(2,1)S(1)}, u32[]{:S(2)}, u32[]{:S(2)}) collective-permute-start(bf16[384,256]{1,0:T(8,128)(2,1)S(1)} %get-tuple-element.52), channel_id=1, source_target_pairs={{0,24},{4,12},{8,0},{12,20},{16,8},{20,28},{24,16},{28,4},{1,25},{... | collective-permute-start | bytes 589832 | tf_op jit(solution)/shard_map/ppermute | solution.py:223
  85.6 4.6 %collective-permute-done.11 = bf16[384,256]{1,0:T(8,128)(2,1)S(1)} collective-permute-done((bf16[384,256]{1,0:T(8,128)(2,1)S(1)}, bf16[384,256]{1,0:T(8,128)(2,1)S(1)}, u32[]{:S(2)}, u32[]{:S(2)}) %collective-permute-start.11) | collective-permute-done | bytes 196640 | tf_op jit(solution)/shard_map/ppermute | solution.py:223
  90.1 2.6 %collective-permute-done.20 = bf16[384,256]{1,0:T(8,128)(2,1)S(1)} collective-permute-done((bf16[384,256]{1,0:T(8,128)(2,1)S(1)}, bf16[384,256]{1,0:T(8,128)(2,1)S(1)}, u32[]{:S(2)}, u32[]{:S(2)}) %collective-permute-start.20) | collective-permute-done | bytes 196640 | tf_op jit(solution)/shard_map/ppermute | solution.py:223
  92.8 2.1 %collective-permute-start.15 = (bf16[384,256]{1,0:T(8,128)(2,1)S(1)}, bf16[384,256]{1,0:T(8,128)(2,1)S(1)}, u32[]{:S(2)}, u32[]{:S(2)}) collective-permute-start(bf16[384,256]{1,0:T(8,128)(2,1)S(1)} %get-tuple-element.63), channel_id=1, source_target_pairs={{0,4},{4,0},{8,12},{12,8},{16,20},{20,16},{24,28},{28,24},{1,5},{5... | collective-permute-start | bytes 589832 | tf_op jit(solution)/shard_map/ppermute | solution.py:141
  95.1 2.5 %collective-permute-done.19 = bf16[384,256]{1,0:T(8,128)(2,1)S(1)} collective-permute-done((bf16[384,256]{1,0:T(8,128)(2,1)S(1)}, bf16[384,256]{1,0:T(8,128)(2,1)S(1)}, u32[]{:S(2)}, u32[]{:S(2)}) %collective-permute-start.19) | collective-permute-done | bytes 196640 | tf_op jit(solution)/shard_map/ppermute | solution.py:223
  98.0 2.0 %collective-permute-done.15 = bf16[384,256]{1,0:T(8,128)(2,1)S(1)} collective-permute-done((bf16[384,256]{1,0:T(8,128)(2,1)S(1)}, bf16[384,256]{1,0:T(8,128)(2,1)S(1)}, u32[]{:S(2)}, u32[]{:S(2)}) %collective-permute-start.15) | collective-permute-done | bytes 196640 | tf_op jit(solution)/shard_map/ppermute | solution.py:141
  100.4 2.0 %fusion.23 = bf16[384,1536]{1,0:T(8,128)(2,1)S(1)} fusion(bf16[3,512,3072]{2,1,0:T(8,128)(2,1)S(1)} %bitcast.93, s32[]{:T(128)S(6)} %select_n.190, bf16[1,384,512]{2,1,0:T(8,128)(2,1)S(1)} %maximum_bitcast_fusion.2, bf16[1,384,512]{2,1,0:T(8,128)(2,1)S(1)} %maximum_bitcast_fusion.1, bf16[1,384,512]{2,1,0:T(8,128)(2,1)S(1)} %maximum_bitcast_fusion), kind=kOutput, calls=%fused_computation.15 | convolution fusion | flops 1813708800 | bytes 7077892 | tf_op jit(solution)/shard_map/cik,ckm->im/dot_general | solution.py:158
  102.8 1.7 %collective-permute-done.17 = bf16[384,768]{1,0:T(8,128)(2,1)S(1)} collective-permute-done((bf16[384,768]{1,0:T(8,128)(2,1)S(1)}, bf16[384,768]{1,0:T(8,128)(2,1)S(1)}, u32[]{:S(2)}, u32[]{:S(2)}) %collective-permute-start.17) | collective-permute-done | bytes 589856 | tf_op jit(solution)/shard_map/ppermute | solution.py:141
  104.8 2.0 %fusion.20 = bf16[384,1536]{1,0:T(8,128)(2,1)S(1)} fusion(bf16[3,512,3072]{2,1,0:T(8,128)(2,1)S(1)} %bitcast.93, s32[]{:T(128)S(6)} %select_n.190, bf16[1,384,512]{2,1,0:T(8,128)(2,1)S(1)} %maximum_bitcast_fusion.5, bf16[1,384,512]{2,1,0:T(8,128)(2,1)S(1)} %maximum_bitcast_fusion.4, bf16[1,384,512]{2,1,0:T(8,128)(2,1)S(1)} %maximum_bitcast_fusion.3), kind=kOutput, calls=%fused_computation.14 | convolution fusion | flops 1813708800 | bytes 7077892 | tf_op jit(solution)/shard_map/cik,ckm->im/dot_general | solution.py:158
  107.1 2.0 %fusion.29 = bf16[384,1536]{1,0:T(8,128)(2,1)S(1)} fusion(bf16[3,512,3072]{2,1,0:T(8,128)(2,1)S(1)} %bitcast.93, s32[]{:T(128)S(6)} %select_n.186, bf16[1,384,512]{2,1,0:T(8,128)(2,1)S(1)} %maximum_bitcast_fusion.2, bf16[1,384,512]{2,1,0:T(8,128)(2,1)S(1)} %maximum_bitcast_fusion.1, bf16[1,384,512]{2,1,0:T(8,128)(2,1)S(1)} %maximum_bitcast_fusion), kind=kOutput, calls=%fused_computation.17 | convolution fusion | flops 1813708800 | bytes 7077892 | tf_op jit(solution)/shard_map/cik,ckm->im/dot_general | solution.py:158
  111.0 2.0 %fusion.26 = bf16[384,1536]{1,0:T(8,128)(2,1)S(1)} fusion(bf16[3,512,3072]{2,1,0:T(8,128)(2,1)S(1)} %bitcast.93, s32[]{:T(128)S(6)} %select_n.186, bf16[1,384,512]{2,1,0:T(8,128)(2,1)S(1)} %maximum_bitcast_fusion.5, bf16[1,384,512]{2,1,0:T(8,128)(2,1)S(1)} %maximum_bitcast_fusion.4, bf16[1,384,512]{2,1,0:T(8,128)(2,1)S(1)} %maximum_bitcast_fusion.3), kind=kOutput, calls=%fused_computation.16 | convolution fusion | flops 1813708800 | bytes 7077892 | tf_op jit(solution)/shard_map/cik,ckm->im/dot_general | solution.py:158
  114.1 11.7 %collective-permute-done.18 = bf16[384,768]{1,0:T(8,128)(2,1)S(1)} collective-permute-done((bf16[384,768]{1,0:T(8,128)(2,1)S(1)}, bf16[384,768]{1,0:T(8,128)(2,1)S(1)}, u32[]{:S(2)}, u32[]{:S(2)}) %collective-permute-start.18) | collective-permute-done | bytes 589856 | tf_op jit(solution)/shard_map/ppermute | solution.py:141
  125.8 11.8 %collective-permute-done.24 = bf16[384,768]{1,0:T(8,128)(2,1)S(1)} collective-permute-done((bf16[384,768]{1,0:T(8,128)(2,1)S(1)}, bf16[384,768]{1,0:T(8,128)(2,1)S(1)}, u32[]{:S(2)}, u32[]{:S(2)}) %collective-permute-start.24) | collective-permute-done | bytes 589856 | tf_op jit(solution)/shard_map/ppermute | solution.py:141
  (114 shorter events, 22.3 us)
Async XLA Ops:
  0.0 23.0 %copy-start = (s32[16]{0:T(128)S(1)}, s32[16]{0:T(128)}, u32[]{:S(2)}) copy-start(s32[16]{0:T(128)} %param.15) | copy-start | bytes 196
  1.6 7.5 %copy-start.8 = (s32[16,4]{0,1:T(4,128)S(1)}, s32[16,4]{0,1:T(4,128)}, u32[]{:S(2)}) copy-start(s32[16,4]{0,1:T(4,128)} %param.14) | copy-start | bytes 772
  1.6 8.2 %copy-start.2 = (bf16[768,512]{1,0:T(8,128)(2,1)S(1)}, bf16[768,512]{1,0:T(8,128)(2,1)}, u32[]{:S(2)}) copy-start(bf16[768,512]{1,0:T(8,128)(2,1)} %param.12) | copy-start | bytes 2359300
  1.6 8.2 %copy-start.3 = (bf16[768,512]{1,0:T(8,128)(2,1)S(1)}, bf16[768,512]{1,0:T(8,128)(2,1)}, u32[]{:S(2)}) copy-start(bf16[768,512]{1,0:T(8,128)(2,1)} %param.8) | copy-start | bytes 2359300
  2.5 19.4 %collective-permute-start = (bf16[768,256]{1,0:T(8,128)(2,1)}, bf16[768,256]{1,0:T(8,128)(2,1)S(1)}, u32[]{:S(2)}, u32[]{:S(2)}) collective-permute-start(bf16[768,256]{1,0:T(8,128)(2,1)} %pad_maximum_fusion.9), channel_id=1, source_target_pairs={{0,4},{4,0},{8,12},{12,8},{16,20},{20,16},{24,28},{28,24},{1,5},{5... | collective-permute-start | bytes 1179656 | tf_op jit(solution)/shard_map/ppermute | solution.py:141
  5.5 20.3 %collective-permute-start.3 = (bf16[768,256]{1,0:T(8,128)(2,1)S(1)}, bf16[768,256]{1,0:T(8,128)(2,1)S(1)}, u32[]{:S(2)}, u32[]{:S(2)}) collective-permute-start(bf16[768,256]{1,0:T(8,128)(2,1)S(1)} %pad_maximum_fusion.11.refs_2_), channel_id=1, source_target_pairs={{0,24},{4,12},{8,0},{12,20},{16,8},{20,28},{24,16},{28,4},{1,25},{... | collective-permute-start | bytes 1179656 | tf_op jit(solution)/shard_map/ppermute | solution.py:223
  21.8 12.4 %collective-permute-start.1 = (f32[2,768]{0,1:T(8,128)}, f32[2,768]{0,1:T(8,128)}, u32[]{:S(2)}, u32[]{:S(2)}) collective-permute-start(f32[2,768]{0,1:T(8,128)} %dynamic-slice_bitcast_fusion), channel_id=1, source_target_pairs={{0,4},{4,0},{8,12},{12,8},{16,20},{20,16},{24,28},{28,24},{1,5},{5... | collective-permute-start | bytes 18440 | tf_op jit(solution)/shard_map/ppermute | solution.py:141
  23.7 18.9 %collective-permute-start.5 = (bf16[768,256]{1,0:T(8,128)(2,1)}, bf16[768,256]{1,0:T(8,128)(2,1)S(1)}, u32[]{:S(2)}, u32[]{:S(2)}) collective-permute-start(bf16[768,256]{1,0:T(8,128)(2,1)} %pad_maximum_fusion.8), channel_id=1, source_target_pairs={{0,4},{4,0},{8,12},{12,8},{16,20},{20,16},{24,28},{28,24},{1,5},{5... | collective-permute-start | bytes 1179656 | tf_op jit(solution)/shard_map/ppermute | solution.py:141
  25.8 37.0 %collective-permute-start.7 = (bf16[768,256]{1,0:T(8,128)(2,1)S(1)}, bf16[768,256]{1,0:T(8,128)(2,1)S(1)}, u32[]{:S(2)}, u32[]{:S(2)}) collective-permute-start(bf16[768,256]{1,0:T(8,128)(2,1)S(1)} %pad_maximum_fusion.14.refs_2_), channel_id=1, source_target_pairs={{0,24},{4,12},{8,0},{12,20},{16,8},{20,28},{24,16},{28,4},{1,25},{... | collective-permute-start | bytes 1179656 | tf_op jit(solution)/shard_map/ppermute | solution.py:223
  26.2 24.8 %collective-permute-start.2 = (bf16[768,256]{1,0:T(8,128)(2,1)}, bf16[768,256]{1,0:T(8,128)(2,1)S(1)}, u32[]{:S(2)}, u32[]{:S(2)}) collective-permute-start(bf16[768,256]{1,0:T(8,128)(2,1)} %pad_maximum_fusion.7), channel_id=1, source_target_pairs={{0,4},{4,0},{8,12},{12,8},{16,20},{20,16},{24,28},{28,24},{1,5},{5... | collective-permute-start | bytes 1179656 | tf_op jit(solution)/shard_map/ppermute | solution.py:141
  26.2 16.7 %collective-permute-start.4 = (bf16[768,256]{1,0:T(8,128)(2,1)S(1)}, bf16[768,256]{1,0:T(8,128)(2,1)}, u32[]{:S(2)}, u32[]{:S(2)}) collective-permute-start(bf16[768,256]{1,0:T(8,128)(2,1)S(1)} %collective-permute-done.refs_3_), channel_id=1, source_target_pairs={{0,8},{4,28},{8,16},{12,4},{16,24},{20,12},{24,0},{28,20},{1,9},{5... | collective-permute-start | bytes 1179656 | tf_op jit(solution)/shard_map/ppermute | solution.py:223
  42.6 20.2 %collective-permute-start.6 = (bf16[768,256]{1,0:T(8,128)(2,1)}, bf16[768,256]{1,0:T(8,128)(2,1)S(1)}, u32[]{:S(2)}, u32[]{:S(2)}) collective-permute-start(bf16[768,256]{1,0:T(8,128)(2,1)} %pad_maximum_fusion.13), channel_id=1, source_target_pairs={{0,4},{4,0},{8,12},{12,8},{16,20},{20,16},{24,28},{28,24},{1,5},{5... | collective-permute-start | bytes 1179656 | tf_op jit(solution)/shard_map/ppermute | solution.py:141
  43.0 19.9 %collective-permute-start.8 = (bf16[768,256]{1,0:T(8,128)(2,1)S(1)}, bf16[768,256]{1,0:T(8,128)(2,1)S(1)}, u32[]{:S(2)}, u32[]{:S(2)}) collective-permute-start(bf16[768,256]{1,0:T(8,128)(2,1)S(1)} %collective-permute-done.5.refs_3_), channel_id=1, source_target_pairs={{0,8},{4,28},{8,16},{12,4},{16,24},{20,12},{24,0},{28,20},{1,9},{5... | collective-permute-start | bytes 1179656 | tf_op jit(solution)/shard_map/ppermute | solution.py:223
  60.7 19.7 %collective-permute-start.12 = (bf16[2,384,256]{2,1,0:T(8,128)(2,1)S(1)}, bf16[2,384,256]{2,1,0:T(8,128)(2,1)S(1)}, u32[]{:S(2)}, u32[]{:S(2)}) collective-permute-start(bf16[2,384,256]{2,1,0:T(8,128)(2,1)S(1)} %get-tuple-element.46), channel_id=1, source_target_pairs={{0,24},{4,12},{8,0},{12,20},{16,8},{20,28},{24,16},{28,4},{1,25},{... | collective-permute-start | bytes 1179656 | tf_op jit(solution)/shard_map/ppermute | solution.py:223
  61.2 19.5 %collective-permute-start.10 = (bf16[2,384,256]{2,1,0:T(8,128)(2,1)S(1)}, bf16[2,384,256]{2,1,0:T(8,128)(2,1)S(1)}, u32[]{:S(2)}, u32[]{:S(2)}) collective-permute-start(bf16[2,384,256]{2,1,0:T(8,128)(2,1)S(1)} %get-tuple-element.42), channel_id=1, source_target_pairs={{0,8},{4,28},{8,16},{12,4},{16,24},{20,12},{24,0},{28,20},{1,9},{5... | collective-permute-start | bytes 1179656 | tf_op jit(solution)/shard_map/ppermute | solution.py:223
  62.8 37.5 %slice-start = ((s8[9437184]{0:T(1024)(128)(4,1)}), s8[1048576]{0:T(1024)(128)(4,1)S(1)}, s32[]{:S(2)}) async-start(s8[9437184]{0:T(1024)(128)(4,1)} %bitcast.92), calls=%async_computation | async-start | bytes 2097152
  62.8 37.5 %slice-start.1 = ((s8[9437184]{0:T(1024)(128)(4,1)}), s8[4194304]{0:T(1024)(128)(4,1)S(1)}, s32[]{:S(2)}) async-start(s8[9437184]{0:T(1024)(128)(4,1)} %bitcast.92), calls=%async_computation.1 | async-start | bytes 8388608
  72.1 11.0 %collective-permute-start.14 = (bf16[384,256]{1,0:T(8,128)(2,1)S(1)}, bf16[384,256]{1,0:T(8,128)(2,1)S(1)}, u32[]{:S(2)}, u32[]{:S(2)}) collective-permute-start(bf16[384,256]{1,0:T(8,128)(2,1)S(1)} %get-tuple-element.99), channel_id=1, source_target_pairs={{0,24},{4,12},{8,0},{12,20},{16,8},{20,28},{24,16},{28,4},{1,25},{... | collective-permute-start | bytes 589832 | tf_op jit(solution)/shard_map/ppermute | solution.py:223
  80.5 14.6 %collective-permute-start.13 = (bf16[2,384,256]{2,1,0:T(8,128)(2,1)S(1)}, bf16[2,384,256]{2,1,0:T(8,128)(2,1)S(1)}, u32[]{:S(2)}, u32[]{:S(2)}) collective-permute-start(bf16[2,384,256]{2,1,0:T(8,128)(2,1)S(1)} %add_convert_fusion.4), channel_id=1, source_target_pairs={{0,4},{4,0},{8,12},{12,8},{16,20},{20,16},{24,28},{28,24},{1,5},{5... | collective-permute-start | bytes 1179656 | tf_op jit(solution)/shard_map/ppermute | solution.py:141
  80.6 9.5 %collective-permute-start.11 = (bf16[384,256]{1,0:T(8,128)(2,1)S(1)}, bf16[384,256]{1,0:T(8,128)(2,1)S(1)}, u32[]{:S(2)}, u32[]{:S(2)}) collective-permute-start(bf16[384,256]{1,0:T(8,128)(2,1)S(1)} %get-tuple-element.95), channel_id=1, source_target_pairs={{0,8},{4,28},{8,16},{12,4},{16,24},{20,12},{24,0},{28,20},{1,9},{5... | collective-permute-start | bytes 589832 | tf_op jit(solution)/shard_map/ppermute | solution.py:223
  80.8 19.6 %slice-start.2 = ((s8[9437184]{0:T(1024)(128)(4,1)}), s8[4194304]{0:T(1024)(128)(4,1)S(1)}, s32[]{:S(2)}) async-start(s8[9437184]{0:T(1024)(128)(4,1)} %bitcast.92), calls=%async_computation.2 | async-start | bytes 8388608
  80.9 16.8 %collective-permute-start.9 = (bf16[2,384,256]{2,1,0:T(8,128)(2,1)S(1)}, bf16[2,384,256]{2,1,0:T(8,128)(2,1)S(1)}, u32[]{:S(2)}, u32[]{:S(2)}) collective-permute-start(bf16[2,384,256]{2,1,0:T(8,128)(2,1)S(1)} %pad_maximum_fusion.15), channel_id=1, source_target_pairs={{0,4},{4,0},{8,12},{12,8},{16,20},{20,16},{24,28},{28,24},{1,5},{5... | collective-permute-start | bytes 1179656 | tf_op jit(solution)/shard_map/ppermute | solution.py:141
  83.1 9.6 %collective-permute-start.20 = (bf16[384,256]{1,0:T(8,128)(2,1)S(1)}, bf16[384,256]{1,0:T(8,128)(2,1)S(1)}, u32[]{:S(2)}, u32[]{:S(2)}) collective-permute-start(bf16[384,256]{1,0:T(8,128)(2,1)S(1)} %get-tuple-element.52), channel_id=1, source_target_pairs={{0,24},{4,12},{8,0},{12,20},{16,8},{20,28},{24,16},{28,4},{1,25},{... | collective-permute-start | bytes 589832 | tf_op jit(solution)/shard_map/ppermute | solution.py:223
  90.1 7.5 %collective-permute-start.19 = (bf16[384,256]{1,0:T(8,128)(2,1)S(1)}, bf16[384,256]{1,0:T(8,128)(2,1)S(1)}, u32[]{:S(2)}, u32[]{:S(2)}) collective-permute-start(bf16[384,256]{1,0:T(8,128)(2,1)S(1)} %get-tuple-element.51), channel_id=1, source_target_pairs={{0,8},{4,28},{8,16},{12,4},{16,24},{20,12},{24,0},{28,20},{1,9},{5... | collective-permute-start | bytes 589832 | tf_op jit(solution)/shard_map/ppermute | solution.py:223
  92.8 7.2 %collective-permute-start.15 = (bf16[384,256]{1,0:T(8,128)(2,1)S(1)}, bf16[384,256]{1,0:T(8,128)(2,1)S(1)}, u32[]{:S(2)}, u32[]{:S(2)}) collective-permute-start(bf16[384,256]{1,0:T(8,128)(2,1)S(1)} %get-tuple-element.63), channel_id=1, source_target_pairs={{0,4},{4,0},{8,12},{12,8},{16,20},{20,16},{24,28},{28,24},{1,5},{5... | collective-permute-start | bytes 589832 | tf_op jit(solution)/shard_map/ppermute | solution.py:141
  95.0 7.6 %collective-permute-start.21 = (bf16[384,256]{1,0:T(8,128)(2,1)S(1)}, bf16[384,256]{1,0:T(8,128)(2,1)S(1)}, u32[]{:S(2)}, u32[]{:S(2)}) collective-permute-start(bf16[384,256]{1,0:T(8,128)(2,1)S(1)} %get-tuple-element.62), channel_id=1, source_target_pairs={{0,4},{4,0},{8,12},{12,8},{16,20},{20,16},{24,28},{28,24},{1,5},{5... | collective-permute-start | bytes 589832 | tf_op jit(solution)/shard_map/ppermute | solution.py:141
  102.5 2.1 %collective-permute-start.17 = (bf16[384,768]{1,0:T(8,128)(2,1)S(1)}, bf16[384,768]{1,0:T(8,128)(2,1)S(1)}, u32[]{:S(2)}, u32[]{:S(2)}) collective-permute-start(bf16[384,768]{1,0:T(8,128)(2,1)S(1)} %constant_dynamic-slice_fusion.2), channel_id=1, source_target_pairs={{0,1},{1,0},{2,3},{3,2},{4,5},{5,4},{6,7},{7,6},{8,9},{9,8},{10,11... | collective-permute-start | bytes 1769480 | tf_op jit(solution)/shard_map/ppermute | solution.py:141
  106.9 6.3 %collective-permute-start.23 = (bf16[384,768]{1,0:T(8,128)(2,1)S(1)}, bf16[384,768]{1,0:T(8,128)(2,1)S(1)}, u32[]{:S(2)}, u32[]{:S(2)}) collective-permute-start(bf16[384,768]{1,0:T(8,128)(2,1)S(1)} %constant_dynamic-slice_fusion), channel_id=1, source_target_pairs={{0,1},{1,0},{2,3},{3,2},{4,5},{5,4},{6,7},{7,6},{8,9},{9,8},{10,11... | collective-permute-start | bytes 1769480 | tf_op jit(solution)/shard_map/ppermute | solution.py:141
  109.2 4.9 %collective-permute-start.16 = (bf16[384,768]{1,0:T(8,128)(2,1)S(1)}, bf16[384,768]{1,0:T(8,128)(2,1)S(1)}, u32[]{:S(2)}, u32[]{:S(2)}) collective-permute-start(bf16[384,768]{1,0:T(8,128)(2,1)S(1)} %constant_dynamic-slice_fusion.3), channel_id=1, source_target_pairs={{0,1},{1,0},{2,3},{3,2},{4,5},{5,4},{6,7},{7,6},{8,9},{9,8},{10,11... | collective-permute-start | bytes 1769480 | tf_op jit(solution)/shard_map/ppermute | solution.py:141
  109.6 16.2 %collective-permute-start.18 = (bf16[384,768]{1,0:T(8,128)(2,1)S(1)}, bf16[384,768]{1,0:T(8,128)(2,1)S(1)}, u32[]{:S(2)}, u32[]{:S(2)}) collective-permute-start(bf16[384,768]{1,0:T(8,128)(2,1)S(1)} %add_convert_fusion.3), channel_id=1, source_target_pairs={{0,2},{1,3},{2,0},{3,1},{4,6},{5,7},{6,4},{7,5},{8,10},{9,11},{10,... | collective-permute-start | bytes 1769480 | tf_op jit(solution)/shard_map/ppermute | solution.py:141
  113.1 12.7 %collective-permute-start.22 = (bf16[384,768]{1,0:T(8,128)(2,1)S(1)}, bf16[384,768]{1,0:T(8,128)(2,1)S(1)}, u32[]{:S(2)}, u32[]{:S(2)}) collective-permute-start(bf16[384,768]{1,0:T(8,128)(2,1)S(1)} %constant_dynamic-slice_fusion.1), channel_id=1, source_target_pairs={{0,1},{1,0},{2,3},{3,2},{4,5},{5,4},{6,7},{7,6},{8,9},{9,8},{10,11... | collective-permute-start | bytes 1769480 | tf_op jit(solution)/shard_map/ppermute | solution.py:141
  113.4 24.3 %collective-permute-start.24 = (bf16[384,768]{1,0:T(8,128)(2,1)S(1)}, bf16[384,768]{1,0:T(8,128)(2,1)S(1)}, u32[]{:S(2)}, u32[]{:S(2)}) collective-permute-start(bf16[384,768]{1,0:T(8,128)(2,1)S(1)} %add_convert_fusion.1), channel_id=1, source_target_pairs={{0,2},{1,3},{2,0},{3,1},{4,6},{5,7},{6,4},{7,5},{8,10},{9,11},{10,... | collective-permute-start | bytes 1769480 | tf_op jit(solution)/shard_map/ppermute | solution.py:141
  (5 other events, 10.7 us)

commit v4 on v3

--- a/solution.py
+++ b/solution.py
@@ -151,11 +151,15 @@
     return slots.astype(jnp.int32), counts[ids].astype(jnp.int32)
 
 
-def chip_sum(stack, projection, target):
-    core = lax.axis_index("head") % 2
+def chip_term(stack, projection, target):
     width = projection.shape[2] // 4
     weights = lax.dynamic_slice_in_dim(projection, target * 2 * width, 2 * width, 2)
-    term = jnp.einsum("cik,ckm->im", stack, weights, preferred_element_type=F32).astype(BF16)
+    return jnp.einsum("cik,ckm->im", stack, weights, preferred_element_type=F32).astype(BF16)
+
+
+def chip_sum(term):
+    core = lax.axis_index("head") % 2
+    width = term.shape[1] // 2
     sent = lax.dynamic_slice_in_dim(term, (1 - core) * width, width, 1)
     kept = lax.dynamic_slice_in_dim(term, core * width, width, 1)
     return kept.astype(F32) + swapped(sent, "head", 1).astype(F32)
@@ -179,9 +183,11 @@
     tiles_dev = rows_dev // TILE
     tiles_all = tiles_dev * seq_count
     heads_dev = query_rows.shape[1] // HD
-    deltas = jnp.sum(
-        (output_grad.astype(F32) * output_rows.astype(F32)).reshape(rows_dev, heads_dev, HD), axis=-1
-    ).T
+
+    def head_delta(head):
+        grad, output = head_cols(output_grad, head), head_cols(output_rows, head)
+        return jnp.sum(grad.astype(F32) * output.astype(F32), axis=1)
+
     if heads_dev % 2 or seq_count % 2 or tiles_dev != HALO:
         grads = ([], [], [])
         slots, live = tables(neighbours, counts, place * tiles_dev, tiles_dev, tiles_all)
@@ -190,7 +196,7 @@
             kv = jnp.concatenate([head_cols(key_rows, head), head_cols(value_rows, head)], 1)
             window = [kv, shifted(kv, "seq", 1), shifted(kv, "seq", -1)]
             (query_grad,), (own,), (to_prev, to_next) = attention(
-                slots, live, jnp.zeros((1,), jnp.int32), deltas[head], [qg], window
+                slots, live, jnp.zeros((1,), jnp.int32), head_delta(head), [qg], window
             )
             own = own + shifted(to_prev, "seq", -1).astype(F32) + shifted(to_next, "seq", 1).astype(F32)
             own = own.astype(BF16).reshape(rows_dev, 2 * HD)
@@ -213,33 +219,34 @@
         return jnp.concatenate([head_cols(left, head), head_cols(right, head)], 1)
 
     kept, sent = odd * half, (1 - odd) * half
-    kv_kept = [both(key_rows, value_rows, kept + step) for step in range(half)]
-    kv_sent = [both(key_rows, value_rows, sent + step) for step in range(half)]
-    qg_kept = [both(query_rows, output_grad, kept + step) for step in range(half)]
-    qg_sent = [both(query_rows, output_grad, sent + step) for step in range(half)]
 
     def outward(block, sign):
         route = [(i, (i + 2 * sign * (2 * (i % 2) - 1)) % seq_count) for i in range(seq_count)]
         return lax.ppermute(block, "seq", route)
 
-    kv_got = [swapped(kv_sent[0], "seq", 1)]
+    kv_got = [swapped(both(key_rows, value_rows, sent), "seq", 1)]
+    kv_kept = [both(key_rows, value_rows, kept)]
     halos = [(outward(kv_kept[0], 1), outward(kv_got[0], -1))]
-    delta_sent = lax.dynamic_slice_in_dim(deltas, sent, half, 0)
-    qg_got = []
+    kept, sent = after([kept, sent], kv_got)
+    qg_kept, qg_got = [], []
+    arrived = kv_got[0]
     for step in range(half):
-        wave = [qg_sent[step]] + kv_sent[step + 1 : step + 2]
+        (block,) = after([both(query_rows, output_grad, sent + step)], [arrived])
+        arrived = swapped(block, "seq", 1)
+        qg_got.append(arrived)
+        qg_kept.append(both(query_rows, output_grad, kept + step))
         if step == 0:
-            wave.append(delta_sent)
-        wave = [swapped(block, "seq", 1) for block in after(wave, [kv_got[step]])]
-        qg_got.append(wave[0])
-        if step == 0:
-            delta_got = wave[-1]
+            delta_sent = jnp.stack([head_delta(sent + at) for at in range(half)])
+            delta_got = swapped(delta_sent, "seq", 1)
         if step + 1 < half:
-            kv_got.append(wave[1])
+            (block,) = after([both(key_rows, value_rows, sent + step + 1)], [arrived])
+            arrived = swapped(block, "seq", 1)
+            kv_got.append(arrived)
+            kv_kept.append(both(key_rows, value_rows, kept + step + 1))
             (own_block,) = after([kv_kept[step + 1]], [halos[step][0]])
             (got_block,) = after([kv_got[step + 1]], [halos[step][1]])
             halos.append((outward(own_block, 1), outward(got_block, -1)))
-    delta_kept = lax.dynamic_slice_in_dim(deltas, kept, half, 0)
+    delta_kept = jnp.stack([head_delta(kept + at) for at in range(half)])
     delta_pair = jnp.concatenate(in_order(delta_kept, delta_got), 1)
     odd_ref = odd.astype(jnp.int32).reshape(1)
 
@@ -263,7 +270,7 @@
                 if near is not None:
                     pair = [after([block], [before])[0] for block, before in zip(pair, near)]
                 near = outward(pair[0], 1), outward(pair[1], -1)
-                others.append(swapped((other[at] + near[0].astype(F32)).astype(BF16), "seq", 1))
+                others.append((other[at] + near[0].astype(F32)).astype(BF16))
                 mine.append((own[at] + near[1].astype(F32)).astype(BF16))
             kv_mine.append(mine)
             kv_other.append(others)
@@ -271,29 +278,28 @@
 
     chip = lax.axis_index("head") // 2
     results = []
-    sent_sum = None
+    term = None
     for at in range(HALO):
+        others = [blocks[at] for blocks in kv_other]
+        block = others[-1] if term is None else after([others[-1]], [term])[0]
+        others[-1] = swapped(block, "seq", 1)
         parts = [in_order(jnp.concatenate([block[at] for block in query_mine], 1), query_got[at])]
         for cols in (slice(0, HD), slice(HD, 2 * HD)):
             parts.append(
                 in_order(
                     jnp.concatenate([blocks[at][:, cols] for blocks in kv_mine], 1),
-                    jnp.concatenate([blocks[at][:, cols] for blocks in kv_other], 1),
+                    jnp.concatenate([block[:, cols] for block in others], 1),
                 )
             )
-        if lax.axis_size("head") != 4:
-            stack = jnp.stack([jnp.concatenate(part, 1) for part in parts])
+        stack = jnp.stack([jnp.concatenate(part, 1) for part in parts])
+        if lax.axis_size("head") == 4:
+            term = chip_term(stack, projection, 1 - chip)
+            results.append((stack, swapped(chip_sum(term).astype(BF16), "head", 2)))
+        else:
             results.append(scattered_over_heads(stack, projection))
-            continue
-        if sent_sum is not None:
-            parts = [after(part, [sent_sum]) for part in parts]
-        stack = jnp.stack([jnp.concatenate(part, 1) for part in parts])
-        sent_sum = chip_sum(stack, projection, 1 - chip).astype(BF16)
-        far = swapped(sent_sum, "head", 2)
-        results.append((stack, far))
     if lax.axis_size("head") == 4:
         results = [
-            (chip_sum(stack, projection, chip) + far.astype(F32)).astype(BF16)
+            (chip_sum(chip_term(stack, projection, chip)) + far.astype(F32)).astype(BF16)
             for stack, far in results
         ]
     return jnp.concatenate(in_order(results[0], results[1]), 0)

time: 140 us -> 154 us (1.10)
  waiting for transfers between devices: 58.3 us -> 76.6 us
  starting transfers between devices: 26.5 us -> 41.1 us
  other arithmetic: 15.5 us -> 4.1 us
  local copies, waits for them, and re-layouts: 11.5 us -> 4 us
    ppermute x10, waiting for transfers between devices: 16.1 us -> 35.9 us  [outward(): return lax.ppermute(block, 'seq', route)]
    ppermute x15, starting transfers between devices: 12.3 us -> 25.2 us  [swapped(): return lax.ppermute(block, axis, [(i, i ^ bit) for i in range(count)])]
    concatenate x8, other arithmetic: 6.37 us -> 0.36 us  [both(): return jnp.concatenate([head_cols(left, head), head_cols(right, head)], 1)]
    select_n x2 -> x0, local copies, waits for them, and re-layouts: 3.48 us -> none  [in_order(): return (jnp.where(even, mine, other), jnp.where(even, other, mine))]
    select_n x8, other arithmetic: 3.35 us -> 1.18 us  [in_order(): return (jnp.where(even, mine, other), jnp.where(even, other, mine))]
    reshape x1 -> x0, local copies, waits for them, and re-layouts: 1.78 us -> none  [local(): (output_grad.astype(F32) * output_rows.astype(F32)).reshape(rows_dev, hea...]
    ppermute x10, starting transfers between devices: 14.2 us -> 15.9 us  [outward(): return lax.ppermute(block, 'seq', route)]
  transfers between devices with their start and end apart: 25 -> 25, of which waited for: 13 -> 14; matrix products, arithmetic and copies ran while one was open for 20% -> 7% of each run, Pallas kernels for 14% -> 12%
where the time goes in v4:
time: 154 us
  waiting for transfers between devices  76.6 us (50%)
  starting transfers between devices  41.1 us (27%)
  Pallas kernels  19.2 us (12%)
  matrix products  8.18 us (5%)
  other arithmetic  4.1 us (3%)
  local copies, waits for them, and re-layouts  4 us (3%)
    ppermute x15, waiting for transfers between devices, swapped(): return lax.ppermute(block, axis, [(i, i ^ bit) for i in range(count)])  40.7 us
    ppermute x10, waiting for transfers between devices, outward(): return lax.ppermute(block, 'seq', route)  35.9 us
    ppermute x15, starting transfers between devices, swapped(): return lax.ppermute(block, axis, [(i, i ^ bit) for i in range(count)])  25.2 us
    pallas_call x2, Pallas kernels, attention(): pl.pallas_call(functools.partial(attention_kernel, n), out_shape=blocks(n...  19.2 us
    ppermute x10, starting transfers between devices, outward(): return lax.ppermute(block, 'seq', route)  15.9 us
    dot_general x4, matrix products, chip_term(): jnp.einsum('cik,ckm->im', stack, weights, preferred_element_type=F32)  8.18 us
  transfers between devices with their start and end apart: 25, of which 14 were waited for; matrix products, arithmetic and copies ran while one was open for 7% of the time, Pallas kernels for 12%

profile of v4, /device:TPU:0, one launch (start us, length us, event | category | flops | bytes accessed | tf_op | source)
XLA Modules:
  0.0 153.7 jit_solution(15100908897847765786)
XLA Ops:
  0.0 1.3 constant_dynamic-slice_fusion.10
  1.4 3.0 %collective-permute-start = (bf16[768,256]{1,0:T(8,128)(2,1)S(1)}, bf16[768,256]{1,0:T(8,128)(2,1)S(1)}, u32[]{:S(2)}, u32[]{:S(2)}) collective-permute-start(bf16[768,256]{1,0:T(8,128)(2,1)S(1)} %pad_maximum_fusion.7), channel_id=1, source_target_pairs={{0,4},{4,0},{8,12},{12,8},{16,20},{20,16},{24,28},{28,24},{1,5},{5... | collective-permute-start | bytes 1179656 | tf_op jit(solution)/shard_map/ppermute | solution.py:141
  4.5 3.7 %collective-permute-start.3 = (bf16[768,256]{1,0:T(8,128)(2,1)S(1)}, bf16[768,256]{1,0:T(8,128)(2,1)S(1)}, u32[]{:S(2)}, u32[]{:S(2)}) collective-permute-start(bf16[768,256]{1,0:T(8,128)(2,1)S(1)} %pad_maximum_fusion.10.refs_2_), channel_id=1, source_target_pairs={{0,24},{4,12},{8,0},{12,20},{16,8},{20,28},{24,16},{28,4},{1,25},{... | collective-permute-start | bytes 1179656 | tf_op jit(solution)/shard_map/ppermute | solution.py:225
  9.5 4.0 %collective-permute-done.refs_3_ = bf16[768,256]{1,0:T(8,128)(2,1)S(1)} collective-permute-done((bf16[768,256]{1,0:T(8,128)(2,1)S(1)}, bf16[768,256]{1,0:T(8,128)(2,1)S(1)}, u32[]{:S(2)}, u32[]{:S(2)}) %collective-permute-start) | collective-permute-done | bytes 393248 | tf_op jit(solution)/shard_map/ppermute | solution.py:141
  14.2 1.8 %collective-permute-start.1 = (f32[2,768]{1,0:T(2,128)S(1)}, f32[2,768]{1,0:T(2,128)S(1)}, u32[]{:S(2)}, u32[]{:S(2)}) collective-permute-start(f32[2,768]{1,0:T(2,128)S(1)} %pad_maximum_fusion.28), channel_id=1, source_target_pairs={{0,4},{4,0},{8,12},{12,8},{16,20},{20,16},{24,28},{28,24},{1,5},{5... | collective-permute-start | bytes 18440 | tf_op jit(solution)/shard_map/ppermute | solution.py:141
  17.4 3.7 %collective-permute-start.7 = (bf16[768,256]{1,0:T(8,128)(2,1)S(1)}, bf16[768,256]{1,0:T(8,128)(2,1)S(1)}, u32[]{:S(2)}, u32[]{:S(2)}) collective-permute-start(bf16[768,256]{1,0:T(8,128)(2,1)S(1)} %pad_maximum_fusion.14.refs_2_), channel_id=1, source_target_pairs={{0,24},{4,12},{8,0},{12,20},{16,8},{20,28},{24,16},{28,4},{1,25},{... | collective-permute-start | bytes 1179656 | tf_op jit(solution)/shard_map/ppermute | solution.py:225
  21.3 4.7 %collective-permute-done.2.refs_1_ = bf16[768,256]{1,0:T(8,128)(2,1)S(1)} collective-permute-done((bf16[768,256]{1,0:T(8,128)(2,1)S(1)}, bf16[768,256]{1,0:T(8,128)(2,1)S(1)}, u32[]{:S(2)}, u32[]{:S(2)}) %collective-permute-start.2) | collective-permute-done | bytes 393248 | tf_op jit(solution)/shard_map/ppermute | solution.py:141
  26.9 10.8 %collective-permute-done.4.refs_5_ = bf16[768,256]{1,0:T(8,128)(2,1)S(1)} collective-permute-done((bf16[768,256]{1,0:T(8,128)(2,1)S(1)}, bf16[768,256]{1,0:T(8,128)(2,1)S(1)}, u32[]{:S(2)}, u32[]{:S(2)}) %collective-permute-start.4) | collective-permute-done | bytes 393248 | tf_op jit(solution)/shard_map/ppermute | solution.py:225
  37.7 9.6 %shard_map.82 = (bf16[2,384,128]{2,1,0:T(8,128)(2,1)S(1)}, bf16[2,384,128]{2,1,0:T(8,128)(2,1)S(1)}, f32[2,384,256]{2,1,0:T(8,128)S(1)}, f32[2,384,256]{2,1,0:T(...) custom-call(s32[16]{0:T(128)S(1)} %and_select_fusion.slots_ref, s32[4]{0:T(128)S(1)} %gather_fusion.1, ...), custom_call_target="tpu_custom_call" | custom-call | flops 6039797760 | bytes 5898240 | tf_op jit(solution)/shard_map/pallas_call | solution.py:111
  48.3 1.2 collective-permute-start.10
  49.5 2.1 %collective-permute-start.6 = (bf16[768,256]{1,0:T(8,128)(2,1)S(1)}, bf16[768,256]{1,0:T(8,128)(2,1)S(1)}, u32[]{:S(2)}, u32[]{:S(2)}) collective-permute-start(bf16[768,256]{1,0:T(8,128)(2,1)S(1)} %pad_maximum_fusion.12), channel_id=1, source_target_pairs={{0,4},{4,0},{8,12},{12,8},{16,20},{20,16},{24,28},{28,24},{1,5},{5... | collective-permute-start | bytes 1179656 | tf_op jit(solution)/shard_map/ppermute | solution.py:141
  51.7 6.1 %collective-permute-done.12 = bf16[2,384,256]{2,1,0:T(8,128)(2,1)S(1)} collective-permute-done((bf16[2,384,256]{2,1,0:T(8,128)(2,1)S(1)}, bf16[2,384,256]{2,1,0:T(8,128)(2,1)S(1)}, u32[]{:S(2)}, u32[]{:S(2)}) %collective-permute-start.12) | collective-permute-done | bytes 393248 | tf_op jit(solution)/shard_map/ppermute | solution.py:225
  57.8 3.8 %collective-permute-start.13 = (bf16[2,384,256]{2,1,0:T(8,128)(2,1)S(1)}, bf16[2,384,256]{2,1,0:T(8,128)(2,1)S(1)}, u32[]{:S(2)}, u32[]{:S(2)}) collective-permute-start(bf16[2,384,256]{2,1,0:T(8,128)(2,1)S(1)} %add_convert_fusion.4), channel_id=1, source_target_pairs={{0,4},{4,0},{8,12},{12,8},{16,20},{20,16},{24,28},{28,24},{1,5},{5... | collective-permute-start | bytes 1179656 | tf_op jit(solution)/shard_map/ppermute | solution.py:141
  61.6 7.5 %collective-permute-done.10 = bf16[2,384,256]{2,1,0:T(8,128)(2,1)S(1)} collective-permute-done((bf16[2,384,256]{2,1,0:T(8,128)(2,1)S(1)}, bf16[2,384,256]{2,1,0:T(8,128)(2,1)S(1)}, u32[]{:S(2)}, u32[]{:S(2)}) %collective-permute-start.10) | collective-permute-done | bytes 393248 | tf_op jit(solution)/shard_map/ppermute | solution.py:225
  69.3 5.6 %collective-permute-done.8.refs_5_ = bf16[768,256]{1,0:T(8,128)(2,1)S(1)} collective-permute-done((bf16[768,256]{1,0:T(8,128)(2,1)S(1)}, bf16[768,256]{1,0:T(8,128)(2,1)S(1)}, u32[]{:S(2)}, u32[]{:S(2)}) %collective-permute-start.8) | collective-permute-done | bytes 393248 | tf_op jit(solution)/shard_map/ppermute | solution.py:225
  74.9 9.6 %shard_map.83 = (bf16[2,384,128]{2,1,0:T(8,128)(2,1)S(1)}, bf16[2,384,128]{2,1,0:T(8,128)(2,1)S(1)}, f32[2,384,256]{2,1,0:T(8,128)S(1)}, f32[2,384,256]{2,1,0:T(...) custom-call(s32[16]{0:T(128)S(1)} %and_select_fusion.slots_ref, s32[4]{0:T(128)S(1)} %gather_fusion.1, ...), custom_call_target="tpu_custom_call" | custom-call | flops 6039797760 | bytes 5898240 | tf_op jit(solution)/shard_map/pallas_call | solution.py:111
  85.1 1.7 %collective-permute-start.11 = (bf16[384,256]{1,0:T(8,128)(2,1)S(1)}, bf16[384,256]{1,0:T(8,128)(2,1)S(1)}, u32[]{:S(2)}, u32[]{:S(2)}) collective-permute-start(bf16[384,256]{1,0:T(8,128)(2,1)S(1)} %get-tuple-element.89), channel_id=1, source_target_pairs={{0,8},{4,28},{8,16},{12,4},{16,24},{20,12},{24,0},{28,20},{1,9},{5... | collective-permute-start | bytes 589832 | tf_op jit(solution)/shard_map/ppermute | solution.py:225
  86.8 3.3 %collective-permute-start.9 = (bf16[2,384,256]{2,1,0:T(8,128)(2,1)S(1)}, bf16[2,384,256]{2,1,0:T(8,128)(2,1)S(1)}, u32[]{:S(2)}, u32[]{:S(2)}) collective-permute-start(bf16[2,384,256]{2,1,0:T(8,128)(2,1)S(1)} %pad_maximum_fusion.15), channel_id=1, source_target_pairs={{0,4},{4,0},{8,12},{12,8},{16,20},{20,16},{24,28},{28,24},{1,5},{5... | collective-permute-start | bytes 1179656 | tf_op jit(solution)/shard_map/ppermute | solution.py:141
  90.3 4.3 %collective-permute-start.20 = (bf16[384,256]{1,0:T(8,128)(2,1)S(1)}, bf16[384,256]{1,0:T(8,128)(2,1)S(1)}, u32[]{:S(2)}, u32[]{:S(2)}) collective-permute-start(bf16[384,256]{1,0:T(8,128)(2,1)S(1)} %get-tuple-element.47), channel_id=1, source_target_pairs={{0,24},{4,12},{8,0},{12,20},{16,8},{20,28},{24,16},{28,4},{1,25},{... | collective-permute-start | bytes 589832 | tf_op jit(solution)/shard_map/ppermute | solution.py:225
  94.6 3.0 %collective-permute-done.11 = bf16[384,256]{1,0:T(8,128)(2,1)S(1)} collective-permute-done((bf16[384,256]{1,0:T(8,128)(2,1)S(1)}, bf16[384,256]{1,0:T(8,128)(2,1)S(1)}, u32[]{:S(2)}, u32[]{:S(2)}) %collective-permute-start.11) | collective-permute-done | bytes 196640 | tf_op jit(solution)/shard_map/ppermute | solution.py:225
  97.5 2.7 %collective-permute-done.20 = bf16[384,256]{1,0:T(8,128)(2,1)S(1)} collective-permute-done((bf16[384,256]{1,0:T(8,128)(2,1)S(1)}, bf16[384,256]{1,0:T(8,128)(2,1)S(1)}, u32[]{:S(2)}, u32[]{:S(2)}) %collective-permute-start.20) | collective-permute-done | bytes 196640 | tf_op jit(solution)/shard_map/ppermute | solution.py:225
  100.3 4.6 %collective-permute-start.15 = (bf16[384,256]{1,0:T(8,128)(2,1)S(1)}, bf16[384,256]{1,0:T(8,128)(2,1)S(1)}, u32[]{:S(2)}, u32[]{:S(2)}) collective-permute-start(bf16[384,256]{1,0:T(8,128)(2,1)S(1)} %get-tuple-element.59), channel_id=1, source_target_pairs={{0,4},{4,0},{8,12},{12,8},{16,20},{20,16},{24,28},{28,24},{1,5},{5... | collective-permute-start | bytes 589832 | tf_op jit(solution)/shard_map/ppermute | solution.py:141
  105.5 3.1 %collective-permute-done.15 = bf16[384,256]{1,0:T(8,128)(2,1)S(1)} collective-permute-done((bf16[384,256]{1,0:T(8,128)(2,1)S(1)}, bf16[384,256]{1,0:T(8,128)(2,1)S(1)}, u32[]{:S(2)}, u32[]{:S(2)}) %collective-permute-start.15) | collective-permute-done | bytes 196640 | tf_op jit(solution)/shard_map/ppermute | solution.py:141
  108.9 2.1 %fusion.23 = bf16[384,1536]{1,0:T(8,128)(2,1)S(1)} fusion(bf16[3,512,3072]{2,1,0:T(8,128)(2,1)S(1)} %bitcast.88, s32[]{:T(128)S(6)} %select_n.196, bf16[1,384,512]{2,1,0:T(8,128)(2,1)S(1)} %maximum_bitcast_fusion.2, bf16[1,384,512]{2,1,0:T(8,128)(2,1)S(1)} %maximum_bitcast_fusion.1, bf16[1,384,512]{2,1,0:T(8,128)(2,1)S(1)} %maximum_bitcast_fusion), kind=kOutput, calls=%fused_computation.15 | convolution fusion | flops 1813708800 | bytes 7077892 | tf_op jit(solution)/shard_map/cik,ckm->im/dot_general | solution.py:157
  111.1 2.1 %collective-permute-start.21 = (bf16[384,256]{1,0:T(8,128)(2,1)S(1)}, bf16[384,256]{1,0:T(8,128)(2,1)S(1)}, u32[]{:S(2)}, u32[]{:S(2)}) collective-permute-start(bf16[384,256]{1,0:T(8,128)(2,1)S(1)} %get-tuple-element.48), channel_id=1, source_target_pairs={{0,4},{4,0},{8,12},{12,8},{16,20},{20,16},{24,28},{28,24},{1,5},{5... | collective-permute-start | bytes 589832 | tf_op jit(solution)/shard_map/ppermute | solution.py:141
  113.2 2.0 %fusion.29 = bf16[384,1536]{1,0:T(8,128)(2,1)S(1)} fusion(bf16[3,512,3072]{2,1,0:T(8,128)(2,1)S(1)} %bitcast.88, s32[]{:T(128)S(6)} %select_n.192, bf16[1,384,512]{2,1,0:T(8,128)(2,1)S(1)} %maximum_bitcast_fusion.2, bf16[1,384,512]{2,1,0:T(8,128)(2,1)S(1)} %maximum_bitcast_fusion.1, bf16[1,384,512]{2,1,0:T(8,128)(2,1)S(1)} %maximum_bitcast_fusion), kind=kOutput, calls=%fused_computation.17 | convolution fusion | flops 1813708800 | bytes 7077892 | tf_op jit(solution)/shard_map/cik,ckm->im/dot_general | solution.py:157
  115.5 3.2 %collective-permute-done.21 = bf16[384,256]{1,0:T(8,128)(2,1)S(1)} collective-permute-done((bf16[384,256]{1,0:T(8,128)(2,1)S(1)}, bf16[384,256]{1,0:T(8,128)(2,1)S(1)}, u32[]{:S(2)}, u32[]{:S(2)}) %collective-permute-start.21) | collective-permute-done | bytes 196640 | tf_op jit(solution)/shard_map/ppermute | solution.py:141
  119.0 2.1 %fusion.20 = bf16[384,1536]{1,0:T(8,128)(2,1)S(1)} fusion(bf16[3,512,3072]{2,1,0:T(8,128)(2,1)S(1)} %bitcast.88, s32[]{:T(128)S(6)} %select_n.196, bf16[1,384,512]{2,1,0:T(8,128)(2,1)S(1)} %maximum_bitcast_fusion.5, bf16[1,384,512]{2,1,0:T(8,128)(2,1)S(1)} %maximum_bitcast_fusion.4, bf16[1,384,512]{2,1,0:T(8,128)(2,1)S(1)} %maximum_bitcast_fusion.3), kind=kOutput, calls=%fused_computation.14 | convolution fusion | flops 1813708800 | bytes 7077892 | tf_op jit(solution)/shard_map/cik,ckm->im/dot_general | solution.py:157
  121.2 2.0 %fusion.26 = bf16[384,1536]{1,0:T(8,128)(2,1)S(1)} fusion(bf16[3,512,3072]{2,1,0:T(8,128)(2,1)S(1)} %bitcast.88, s32[]{:T(128)S(6)} %select_n.192, bf16[1,384,512]{2,1,0:T(8,128)(2,1)S(1)} %maximum_bitcast_fusion.5, bf16[1,384,512]{2,1,0:T(8,128)(2,1)S(1)} %maximum_bitcast_fusion.4, bf16[1,384,512]{2,1,0:T(8,128)(2,1)S(1)} %maximum_bitcast_fusion.3), kind=kOutput, calls=%fused_computation.16 | convolution fusion | flops 1813708800 | bytes 7077892 | tf_op jit(solution)/shard_map/cik,ckm->im/dot_general | solution.py:157
  124.0 1.6 %collective-permute-start.18 = (bf16[384,768]{1,0:T(8,128)(2,1)S(1)}, bf16[384,768]{1,0:T(8,128)(2,1)S(1)}, u32[]{:S(2)}, u32[]{:S(2)}) collective-permute-start(bf16[384,768]{1,0:T(8,128)(2,1)S(1)} %add_convert_fusion.3), channel_id=1, source_target_pairs={{0,2},{1,3},{2,0},{3,1},{4,6},{5,7},{6,4},{7,5},{8,10},{9,11},{10,... | collective-permute-start | bytes 1769480 | tf_op jit(solution)/shard_map/ppermute | solution.py:141
  126.3 13.9 %collective-permute-done.18 = bf16[384,768]{1,0:T(8,128)(2,1)S(1)} collective-permute-done((bf16[384,768]{1,0:T(8,128)(2,1)S(1)}, bf16[384,768]{1,0:T(8,128)(2,1)S(1)}, u32[]{:S(2)}, u32[]{:S(2)}) %collective-permute-start.18) | collective-permute-done | bytes 589856 | tf_op jit(solution)/shard_map/ppermute | solution.py:141
  140.3 11.7 %collective-permute-done.24 = bf16[384,768]{1,0:T(8,128)(2,1)S(1)} collective-permute-done((bf16[384,768]{1,0:T(8,128)(2,1)S(1)}, bf16[384,768]{1,0:T(8,128)(2,1)S(1)}, u32[]{:S(2)}, u32[]{:S(2)}) %collective-permute-start.24) | collective-permute-done | bytes 589856 | tf_op jit(solution)/shard_map/ppermute | solution.py:141
  (113 shorter events, 11.4 us)
Async XLA Ops:
  0.0 8.9 %copy-start = (s32[16]{0:T(128)S(1)}, s32[16]{0:T(128)}, u32[]{:S(2)}) copy-start(s32[16]{0:T(128)} %param.15) | copy-start | bytes 196
  1.3 6.8 %copy-start.6 = (s32[16,4]{0,1:T(4,128)S(1)}, s32[16,4]{0,1:T(4,128)}, u32[]{:S(2)}) copy-start(s32[16,4]{0,1:T(4,128)} %param.14) | copy-start | bytes 772
  1.3 12.2 %copy-start.1 = (bf16[768,512]{1,0:T(8,128)(2,1)S(1)}, bf16[768,512]{1,0:T(8,128)(2,1)}, u32[]{:S(2)}) copy-start(bf16[768,512]{1,0:T(8,128)(2,1)} %param.12) | copy-start | bytes 2359300
  1.4 12.1 %collective-permute-start = (bf16[768,256]{1,0:T(8,128)(2,1)S(1)}, bf16[768,256]{1,0:T(8,128)(2,1)S(1)}, u32[]{:S(2)}, u32[]{:S(2)}) collective-permute-start(bf16[768,256]{1,0:T(8,128)(2,1)S(1)} %pad_maximum_fusion.7), channel_id=1, source_target_pairs={{0,4},{4,0},{8,12},{12,8},{16,20},{20,16},{24,28},{28,24},{1,5},{5... | collective-permute-start | bytes 1179656 | tf_op jit(solution)/shard_map/ppermute | solution.py:141
  4.5 9.2 %copy-start.2 = (bf16[768,512]{1,0:T(8,128)(2,1)S(1)}, bf16[768,512]{1,0:T(8,128)(2,1)}, u32[]{:S(2)}) copy-start(bf16[768,512]{1,0:T(8,128)(2,1)} %param.11) | copy-start | bytes 2359300
  4.5 13.0 %collective-permute-start.3 = (bf16[768,256]{1,0:T(8,128)(2,1)S(1)}, bf16[768,256]{1,0:T(8,128)(2,1)S(1)}, u32[]{:S(2)}, u32[]{:S(2)}) collective-permute-start(bf16[768,256]{1,0:T(8,128)(2,1)S(1)} %pad_maximum_fusion.10.refs_2_), channel_id=1, source_target_pairs={{0,24},{4,12},{8,0},{12,20},{16,8},{20,28},{24,16},{28,4},{1,25},{... | collective-permute-start | bytes 1179656 | tf_op jit(solution)/shard_map/ppermute | solution.py:225
  14.2 7.1 %collective-permute-start.1 = (f32[2,768]{1,0:T(2,128)S(1)}, f32[2,768]{1,0:T(2,128)S(1)}, u32[]{:S(2)}, u32[]{:S(2)}) collective-permute-start(f32[2,768]{1,0:T(2,128)S(1)} %pad_maximum_fusion.28), channel_id=1, source_target_pairs={{0,4},{4,0},{8,12},{12,8},{16,20},{20,16},{24,28},{28,24},{1,5},{5... | collective-permute-start | bytes 18440 | tf_op jit(solution)/shard_map/ppermute | solution.py:141
  16.3 9.8 %collective-permute-start.2 = (bf16[768,256]{1,0:T(8,128)(2,1)S(1)}, bf16[768,256]{1,0:T(8,128)(2,1)S(1)}, u32[]{:S(2)}, u32[]{:S(2)}) collective-permute-start(bf16[768,256]{1,0:T(8,128)(2,1)S(1)} %pad_maximum_fusion.9), channel_id=1, source_target_pairs={{0,4},{4,0},{8,12},{12,8},{16,20},{20,16},{24,28},{28,24},{1,5},{5... | collective-permute-start | bytes 1179656 | tf_op jit(solution)/shard_map/ppermute | solution.py:141
  17.4 51.8 %collective-permute-start.7 = (bf16[768,256]{1,0:T(8,128)(2,1)S(1)}, bf16[768,256]{1,0:T(8,128)(2,1)S(1)}, u32[]{:S(2)}, u32[]{:S(2)}) collective-permute-start(bf16[768,256]{1,0:T(8,128)(2,1)S(1)} %pad_maximum_fusion.14.refs_2_), channel_id=1, source_target_pairs={{0,24},{4,12},{8,0},{12,20},{16,8},{20,28},{24,16},{28,4},{1,25},{... | collective-permute-start | bytes 1179656 | tf_op jit(solution)/shard_map/ppermute | solution.py:225
  21.2 16.4 %collective-permute-start.4 = (bf16[768,256]{1,0:T(8,128)(2,1)S(1)}, bf16[768,256]{1,0:T(8,128)(2,1)S(1)}, u32[]{:S(2)}, u32[]{:S(2)}) collective-permute-start(bf16[768,256]{1,0:T(8,128)(2,1)S(1)} %collective-permute-done.refs_3_), channel_id=1, source_target_pairs={{0,8},{4,28},{8,16},{12,4},{16,24},{20,12},{24,0},{28,20},{1,9},{5... | collective-permute-start | bytes 1179656 | tf_op jit(solution)/shard_map/ppermute | solution.py:225
  26.1 23.4 %collective-permute-start.5 = (bf16[768,256]{1,0:T(8,128)(2,1)S(1)}, bf16[768,256]{1,0:T(8,128)(2,1)S(1)}, u32[]{:S(2)}, u32[]{:S(2)}) collective-permute-start(bf16[768,256]{1,0:T(8,128)(2,1)S(1)} %pad_maximum_fusion.13), channel_id=1, source_target_pairs={{0,4},{4,0},{8,12},{12,8},{16,20},{20,16},{24,28},{28,24},{1,5},{5... | collective-permute-start | bytes 1179656 | tf_op jit(solution)/shard_map/ppermute | solution.py:141
  47.2 10.5 %collective-permute-start.12 = (bf16[2,384,256]{2,1,0:T(8,128)(2,1)S(1)}, bf16[2,384,256]{2,1,0:T(8,128)(2,1)S(1)}, u32[]{:S(2)}, u32[]{:S(2)}) collective-permute-start(bf16[2,384,256]{2,1,0:T(8,128)(2,1)S(1)} %get-tuple-element.43), channel_id=1, source_target_pairs={{0,24},{4,12},{8,0},{12,20},{16,8},{20,28},{24,16},{28,4},{1,25},{... | collective-permute-start | bytes 1179656 | tf_op jit(solution)/shard_map/ppermute | solution.py:225
  48.3 20.8 %collective-permute-start.10 = (bf16[2,384,256]{2,1,0:T(8,128)(2,1)S(1)}, bf16[2,384,256]{2,1,0:T(8,128)(2,1)S(1)}, u32[]{:S(2)}, u32[]{:S(2)}) collective-permute-start(bf16[2,384,256]{2,1,0:T(8,128)(2,1)S(1)} %get-tuple-element.39), channel_id=1, source_target_pairs={{0,8},{4,28},{8,16},{12,4},{16,24},{20,12},{24,0},{28,20},{1,9},{5... | collective-permute-start | bytes 1179656 | tf_op jit(solution)/shard_map/ppermute | solution.py:225
  49.5 19.8 %collective-permute-start.6 = (bf16[768,256]{1,0:T(8,128)(2,1)S(1)}, bf16[768,256]{1,0:T(8,128)(2,1)S(1)}, u32[]{:S(2)}, u32[]{:S(2)}) collective-permute-start(bf16[768,256]{1,0:T(8,128)(2,1)S(1)} %pad_maximum_fusion.12), channel_id=1, source_target_pairs={{0,4},{4,0},{8,12},{12,8},{16,20},{20,16},{24,28},{28,24},{1,5},{5... | collective-permute-start | bytes 1179656 | tf_op jit(solution)/shard_map/ppermute | solution.py:141
  51.7 23.2 %collective-permute-start.8 = (bf16[768,256]{1,0:T(8,128)(2,1)S(1)}, bf16[768,256]{1,0:T(8,128)(2,1)S(1)}, u32[]{:S(2)}, u32[]{:S(2)}) collective-permute-start(bf16[768,256]{1,0:T(8,128)(2,1)S(1)} %collective-permute-done.5.refs_3_), channel_id=1, source_target_pairs={{0,8},{4,28},{8,16},{12,4},{16,24},{20,12},{24,0},{28,20},{1,9},{5... | collective-permute-start | bytes 1179656 | tf_op jit(solution)/shard_map/ppermute | solution.py:225
  57.8 27.1 %collective-permute-start.13 = (bf16[2,384,256]{2,1,0:T(8,128)(2,1)S(1)}, bf16[2,384,256]{2,1,0:T(8,128)(2,1)S(1)}, u32[]{:S(2)}, u32[]{:S(2)}) collective-permute-start(bf16[2,384,256]{2,1,0:T(8,128)(2,1)S(1)} %add_convert_fusion.4), channel_id=1, source_target_pairs={{0,4},{4,0},{8,12},{12,8},{16,20},{20,16},{24,28},{28,24},{1,5},{5... | collective-permute-start | bytes 1179656 | tf_op jit(solution)/shard_map/ppermute | solution.py:141
  74.9 34.0 %slice-start = ((s8[9437184]{0:T(1024)(128)(4,1)}), s8[1048576]{0:T(1024)(128)(4,1)S(1)}, s32[]{:S(2)}) async-start(s8[9437184]{0:T(1024)(128)(4,1)} %bitcast.87), calls=%async_computation | async-start | bytes 2097152
  74.9 34.0 %slice-start.1 = ((s8[9437184]{0:T(1024)(128)(4,1)}), s8[4194304]{0:T(1024)(128)(4,1)S(1)}, s32[]{:S(2)}) async-start(s8[9437184]{0:T(1024)(128)(4,1)} %bitcast.87), calls=%async_computation.1 | async-start | bytes 8388608
  84.5 5.8 %collective-permute-start.14 = (bf16[384,256]{1,0:T(8,128)(2,1)S(1)}, bf16[384,256]{1,0:T(8,128)(2,1)S(1)}, u32[]{:S(2)}, u32[]{:S(2)}) collective-permute-start(bf16[384,256]{1,0:T(8,128)(2,1)S(1)} %get-tuple-element.93), channel_id=1, source_target_pairs={{0,24},{4,12},{8,0},{12,20},{16,8},{20,28},{24,16},{28,4},{1,25},{... | collective-permute-start | bytes 589832 | tf_op jit(solution)/shard_map/ppermute | solution.py:225
  85.0 23.9 %slice-start.2 = ((s8[9437184]{0:T(1024)(128)(4,1)}), s8[4194304]{0:T(1024)(128)(4,1)S(1)}, s32[]{:S(2)}) async-start(s8[9437184]{0:T(1024)(128)(4,1)} %bitcast.87), calls=%async_computation.2 | async-start | bytes 8388608
  85.1 12.5 %collective-permute-start.11 = (bf16[384,256]{1,0:T(8,128)(2,1)S(1)}, bf16[384,256]{1,0:T(8,128)(2,1)S(1)}, u32[]{:S(2)}, u32[]{:S(2)}) collective-permute-start(bf16[384,256]{1,0:T(8,128)(2,1)S(1)} %get-tuple-element.89), channel_id=1, source_target_pairs={{0,8},{4,28},{8,16},{12,4},{16,24},{20,12},{24,0},{28,20},{1,9},{5... | collective-permute-start | bytes 589832 | tf_op jit(solution)/shard_map/ppermute | solution.py:225
  86.8 18.4 %collective-permute-start.9 = (bf16[2,384,256]{2,1,0:T(8,128)(2,1)S(1)}, bf16[2,384,256]{2,1,0:T(8,128)(2,1)S(1)}, u32[]{:S(2)}, u32[]{:S(2)}) collective-permute-start(bf16[2,384,256]{2,1,0:T(8,128)(2,1)S(1)} %pad_maximum_fusion.15), channel_id=1, source_target_pairs={{0,4},{4,0},{8,12},{12,8},{16,20},{20,16},{24,28},{28,24},{1,5},{5... | collective-permute-start | bytes 1179656 | tf_op jit(solution)/shard_map/ppermute | solution.py:141
  90.3 9.9 %collective-permute-start.20 = (bf16[384,256]{1,0:T(8,128)(2,1)S(1)}, bf16[384,256]{1,0:T(8,128)(2,1)S(1)}, u32[]{:S(2)}, u32[]{:S(2)}) collective-permute-start(bf16[384,256]{1,0:T(8,128)(2,1)S(1)} %get-tuple-element.47), channel_id=1, source_target_pairs={{0,24},{4,12},{8,0},{12,20},{16,8},{20,28},{24,16},{28,4},{1,25},{... | collective-permute-start | bytes 589832 | tf_op jit(solution)/shard_map/ppermute | solution.py:225
  97.5 7.5 %collective-permute-start.19 = (bf16[384,256]{1,0:T(8,128)(2,1)S(1)}, bf16[384,256]{1,0:T(8,128)(2,1)S(1)}, u32[]{:S(2)}, u32[]{:S(2)}) collective-permute-start(bf16[384,256]{1,0:T(8,128)(2,1)S(1)} %get-tuple-element.46), channel_id=1, source_target_pairs={{0,8},{4,28},{8,16},{12,4},{16,24},{20,12},{24,0},{28,20},{1,9},{5... | collective-permute-start | bytes 589832 | tf_op jit(solution)/shard_map/ppermute | solution.py:225
  100.3 8.3 %collective-permute-start.15 = (bf16[384,256]{1,0:T(8,128)(2,1)S(1)}, bf16[384,256]{1,0:T(8,128)(2,1)S(1)}, u32[]{:S(2)}, u32[]{:S(2)}) collective-permute-start(bf16[384,256]{1,0:T(8,128)(2,1)S(1)} %get-tuple-element.59), channel_id=1, source_target_pairs={{0,4},{4,0},{8,12},{12,8},{16,20},{20,16},{24,28},{28,24},{1,5},{5... | collective-permute-start | bytes 589832 | tf_op jit(solution)/shard_map/ppermute | solution.py:141
  111.0 12.8 %collective-permute-start.17 = (bf16[384,768]{1,0:T(8,128)(2,1)S(1)}, bf16[384,768]{1,0:T(8,128)(2,1)S(1)}, u32[]{:S(2)}, u32[]{:S(2)}) collective-permute-start(bf16[384,768]{1,0:T(8,128)(2,1)S(1)} %constant_dynamic-slice_fusion.2), channel_id=1, source_target_pairs={{0,1},{1,0},{2,3},{3,2},{4,5},{5,4},{6,7},{7,6},{8,9},{9,8},{10,11... | collective-permute-start | bytes 1769480 | tf_op jit(solution)/shard_map/ppermute | solution.py:141
  111.1 7.6 %collective-permute-start.21 = (bf16[384,256]{1,0:T(8,128)(2,1)S(1)}, bf16[384,256]{1,0:T(8,128)(2,1)S(1)}, u32[]{:S(2)}, u32[]{:S(2)}) collective-permute-start(bf16[384,256]{1,0:T(8,128)(2,1)S(1)} %get-tuple-element.48), channel_id=1, source_target_pairs={{0,4},{4,0},{8,12},{12,8},{16,20},{20,16},{24,28},{28,24},{1,5},{5... | collective-permute-start | bytes 589832 | tf_op jit(solution)/shard_map/ppermute | solution.py:141
  115.3 11.0 %collective-permute-start.16 = (bf16[384,768]{1,0:T(8,128)(2,1)S(1)}, bf16[384,768]{1,0:T(8,128)(2,1)S(1)}, u32[]{:S(2)}, u32[]{:S(2)}) collective-permute-start(bf16[384,768]{1,0:T(8,128)(2,1)S(1)} %constant_dynamic-slice_fusion.3), channel_id=1, source_target_pairs={{0,1},{1,0},{2,3},{3,2},{4,5},{5,4},{6,7},{7,6},{8,9},{9,8},{10,11... | collective-permute-start | bytes 1769480 | tf_op jit(solution)/shard_map/ppermute | solution.py:141
  121.1 4.5 %collective-permute-start.23 = (bf16[384,768]{1,0:T(8,128)(2,1)S(1)}, bf16[384,768]{1,0:T(8,128)(2,1)S(1)}, u32[]{:S(2)}, u32[]{:S(2)}) collective-permute-start(bf16[384,768]{1,0:T(8,128)(2,1)S(1)} %constant_dynamic-slice_fusion), channel_id=1, source_target_pairs={{0,1},{1,0},{2,3},{3,2},{4,5},{5,4},{6,7},{7,6},{8,9},{9,8},{10,11... | collective-permute-start | bytes 1769480 | tf_op jit(solution)/shard_map/ppermute | solution.py:141
  123.3 3.0 %collective-permute-start.22 = (bf16[384,768]{1,0:T(8,128)(2,1)S(1)}, bf16[384,768]{1,0:T(8,128)(2,1)S(1)}, u32[]{:S(2)}, u32[]{:S(2)}) collective-permute-start(bf16[384,768]{1,0:T(8,128)(2,1)S(1)} %constant_dynamic-slice_fusion.1), channel_id=1, source_target_pairs={{0,1},{1,0},{2,3},{3,2},{4,5},{5,4},{6,7},{7,6},{8,9},{9,8},{10,11... | collective-permute-start | bytes 1769480 | tf_op jit(solution)/shard_map/ppermute | solution.py:141
  124.0 16.3 %collective-permute-start.18 = (bf16[384,768]{1,0:T(8,128)(2,1)S(1)}, bf16[384,768]{1,0:T(8,128)(2,1)S(1)}, u32[]{:S(2)}, u32[]{:S(2)}) collective-permute-start(bf16[384,768]{1,0:T(8,128)(2,1)S(1)} %add_convert_fusion.3), channel_id=1, source_target_pairs={{0,2},{1,3},{2,0},{3,1},{4,6},{5,7},{6,4},{7,5},{8,10},{9,11},{10,... | collective-permute-start | bytes 1769480 | tf_op jit(solution)/shard_map/ppermute | solution.py:141
  125.7 26.2 %collective-permute-start.24 = (bf16[384,768]{1,0:T(8,128)(2,1)S(1)}, bf16[384,768]{1,0:T(8,128)(2,1)S(1)}, u32[]{:S(2)}, u32[]{:S(2)}) collective-permute-start(bf16[384,768]{1,0:T(8,128)(2,1)S(1)} %add_convert_fusion.1), channel_id=1, source_target_pairs={{0,2},{1,3},{2,0},{3,1},{4,6},{5,7},{6,4},{7,5},{8,10},{9,11},{10,... | collective-permute-start | bytes 1769480 | tf_op jit(solution)/shard_map/ppermute | solution.py:141
  (3 other events, 6.1 us)

commit v5 on v3

--- a/solution.py
+++ b/solution.py
@@ -151,11 +151,15 @@
     return slots.astype(jnp.int32), counts[ids].astype(jnp.int32)
 
 
-def chip_sum(stack, projection, target):
-    core = lax.axis_index("head") % 2
+def chip_term(stack, projection, target):
     width = projection.shape[2] // 4
     weights = lax.dynamic_slice_in_dim(projection, target * 2 * width, 2 * width, 2)
-    term = jnp.einsum("cik,ckm->im", stack, weights, preferred_element_type=F32).astype(BF16)
+    return jnp.einsum("cik,ckm->im", stack, weights, preferred_element_type=F32).astype(BF16)
+
+
+def chip_sum(term):
+    core = lax.axis_index("head") % 2
+    width = term.shape[1] // 2
     sent = lax.dynamic_slice_in_dim(term, (1 - core) * width, width, 1)
     kept = lax.dynamic_slice_in_dim(term, core * width, width, 1)
     return kept.astype(F32) + swapped(sent, "head", 1).astype(F32)
@@ -263,7 +267,7 @@
                 if near is not None:
                     pair = [after([block], [before])[0] for block, before in zip(pair, near)]
                 near = outward(pair[0], 1), outward(pair[1], -1)
-                others.append(swapped((other[at] + near[0].astype(F32)).astype(BF16), "seq", 1))
+                others.append((other[at] + near[0].astype(F32)).astype(BF16))
                 mine.append((own[at] + near[1].astype(F32)).astype(BF16))
             kv_mine.append(mine)
             kv_other.append(others)
@@ -271,29 +275,28 @@
 
     chip = lax.axis_index("head") // 2
     results = []
-    sent_sum = None
     for at in range(HALO):
+        others = [blocks[at] for blocks in kv_other]
+        others[-1] = swapped(others[-1], "seq", 1)
         parts = [in_order(jnp.concatenate([block[at] for block in query_mine], 1), query_got[at])]
         for cols in (slice(0, HD), slice(HD, 2 * HD)):
             parts.append(
                 in_order(
                     jnp.concatenate([blocks[at][:, cols] for blocks in kv_mine], 1),
-                    jnp.concatenate([blocks[at][:, cols] for blocks in kv_other], 1),
+                    jnp.concatenate([block[:, cols] for block in others], 1),
                 )
             )
-        if lax.axis_size("head") != 4:
-            stack = jnp.stack([jnp.concatenate(part, 1) for part in parts])
+        stack = jnp.stack([jnp.concatenate(part, 1) for part in parts])
+        if lax.axis_size("head") == 4:
+            term = chip_sum(chip_term(stack, projection, 1 - chip)).astype(BF16)
+            if results:
+                (term,) = after([term], [results[-1][1]])
+            results.append((stack, swapped(term, "head", 2)))
+        else:
             results.append(scattered_over_heads(stack, projection))
-            continue
-        if sent_sum is not None:
-            parts = [after(part, [sent_sum]) for part in parts]
-        stack = jnp.stack([jnp.concatenate(part, 1) for part in parts])
-        sent_sum = chip_sum(stack, projection, 1 - chip).astype(BF16)
-        far = swapped(sent_sum, "head", 2)
-        results.append((stack, far))
     if lax.axis_size("head") == 4:
         results = [
-            (chip_sum(stack, projection, chip) + far.astype(F32)).astype(BF16)
+            (chip_sum(chip_term(stack, projection, chip)) + far.astype(F32)).astype(BF16)
             for stack, far in results
         ]
     return jnp.concatenate(in_order(results[0], results[1]), 0)

time: 140 us -> 142 us (1.014)
  starting transfers between devices: 26.5 us -> 31.1 us
  waiting for transfers between devices: 58.3 us -> 54.5 us
    ppermute x10, waiting for transfers between devices: 16.1 us -> 9.75 us  [outward(): return lax.ppermute(block, 'seq', route)]
    ppermute x10, starting transfers between devices: 14.2 us -> 18.2 us  [outward(): return lax.ppermute(block, 'seq', route)]
    ppermute x15, waiting for transfers between devices: 42.2 us -> 44.7 us  [swapped(): return lax.ppermute(block, axis, [(i, i ^ bit) for i in range(count)])]
  transfers between devices with their start and end apart: 25 -> 25, of which waited for: 13 -> 12; matrix products, arithmetic and copies ran while one was open for 20% -> 22% of each run, Pallas kernels for 14% -> 14%
where the time goes in v5:
time: 142 us; the launch traced here: 141 us
  waiting for transfers between devices  54.5 us (38%)
  starting transfers between devices  31.1 us (22%)
  Pallas kernels  19.9 us (14%)
  other arithmetic  15.5 us (11%)
  local copies, waits for them, and re-layouts  11.5 us (8%)
  matrix products  8.1 us (6%)
    ppermute x15, waiting for transfers between devices, swapped(): return lax.ppermute(block, axis, [(i, i ^ bit) for i in range(count)])  44.7 us
    pallas_call x2, Pallas kernels, attention(): pl.pallas_call(functools.partial(attention_kernel, n), out_shape=blocks(n...  19.9 us
    ppermute x10, starting transfers between devices, outward(): return lax.ppermute(block, 'seq', route)  18.2 us
    ppermute x15, starting transfers between devices, swapped(): return lax.ppermute(block, axis, [(i, i ^ bit) for i in range(count)])  12.9 us
    ppermute x10, waiting for transfers between devices, outward(): return lax.ppermute(block, 'seq', route)  9.75 us
    dot_general x4, matrix products, chip_term(): jnp.einsum('cik,ckm->im', stack, weights, preferred_element_type=F32)  8.1 us
    concatenate x8, other arithmetic, both(): return jnp.concatenate([head_cols(left, head), head_cols(right, head)], 1)  6.37 us
    select_n x2, local copies, waits for them, and re-layouts, in_order(): return (jnp.where(even, mine, other), jnp.where(even, other, mine))  3.48 us
  transfers between devices with their start and end apart: 25, of which 12 were waited for; matrix products, arithmetic and copies ran while one was open for 22% of the time, Pallas kernels for 14%

profile of v5, /device:TPU:0, one launch (start us, length us, event | category | flops | bytes accessed | tf_op | source)
XLA Modules:
  0.0 141.2 jit_solution(6533110342405714844)
XLA Ops:
  0.0 1.6 %constant_dynamic-slice_fusion.10 = (bf16[768,128]{1,0:T(8,128)(2,1)S(1)}, bf16[768,128]{1,0:T(8,128)(2,1)S(1)}, bf16[768,128]{1,0:T(8,128)(2,1)S(1)}, bf16[768,...) fusion(bf16[768,512]{1,0:T(8,128)(2,1)} %param.10, ...), kind=kLoop, calls=%fused_computation.108 | loop fusion | bytes 3145744 | tf_op jit(solution)/shard_map/dynamic_slice | solution.py:145
  2.5 3.0 %collective-permute-start = (bf16[768,256]{1,0:T(8,128)(2,1)}, bf16[768,256]{1,0:T(8,128)(2,1)S(1)}, u32[]{:S(2)}, u32[]{:S(2)}) collective-permute-start(bf16[768,256]{1,0:T(8,128)(2,1)} %pad_maximum_fusion.9), channel_id=1, source_target_pairs={{0,4},{4,0},{8,12},{12,8},{16,20},{20,16},{24,28},{28,24},{1,5},{5... | collective-permute-start | bytes 1179656 | tf_op jit(solution)/shard_map/ppermute | solution.py:141
  5.5 3.7 %collective-permute-start.3 = (bf16[768,256]{1,0:T(8,128)(2,1)S(1)}, bf16[768,256]{1,0:T(8,128)(2,1)S(1)}, u32[]{:S(2)}, u32[]{:S(2)}) collective-permute-start(bf16[768,256]{1,0:T(8,128)(2,1)S(1)} %pad_maximum_fusion.11.refs_2_), channel_id=1, source_target_pairs={{0,24},{4,12},{8,0},{12,20},{16,8},{20,28},{24,16},{28,4},{1,25},{... | collective-permute-start | bytes 1179656 | tf_op jit(solution)/shard_map/ppermute | solution.py:227
  12.8 1.8 %reshape.28 = f32[768,4,128]{2,1,0:T(4,128)S(1)} reshape(f32[768,512]{1,0:T(8,128)} %convert_multiply_fusion) | data formatting | bytes 3145728 | tf_op jit(solution)/shard_map/reshape | solution.py:187
  15.3 1.8 %pad_maximum_fusion.7 = bf16[768,256]{1,0:T(8,128)(2,1)} fusion(bf16[768,128]{1,0:T(8,128)(2,1)} %get-tuple-element.59, bf16[768,128]{1,0:T(8,128)(2,1)} %get-tuple-element.122), kind=kLoop, calls=%fused_computation.30 | loop fusion | flops 786432 | bytes 786432 | tf_op jit(solution)/shard_map/concatenate | solution.py:217
  23.7 2.0 %collective-permute-start.5 = (bf16[768,256]{1,0:T(8,128)(2,1)}, bf16[768,256]{1,0:T(8,128)(2,1)S(1)}, u32[]{:S(2)}, u32[]{:S(2)}) collective-permute-start(bf16[768,256]{1,0:T(8,128)(2,1)} %pad_maximum_fusion.8), channel_id=1, source_target_pairs={{0,4},{4,0},{8,12},{12,8},{16,20},{20,16},{24,28},{28,24},{1,5},{5... | collective-permute-start | bytes 1179656 | tf_op jit(solution)/shard_map/ppermute | solution.py:141
  26.2 1.6 %collective-permute-start.4 = (bf16[768,256]{1,0:T(8,128)(2,1)S(1)}, bf16[768,256]{1,0:T(8,128)(2,1)}, u32[]{:S(2)}, u32[]{:S(2)}) collective-permute-start(bf16[768,256]{1,0:T(8,128)(2,1)S(1)} %collective-permute-done.refs_3_), channel_id=1, source_target_pairs={{0,8},{4,28},{8,16},{12,4},{16,24},{20,12},{24,0},{28,20},{1,9},{5... | collective-permute-start | bytes 1179656 | tf_op jit(solution)/shard_map/ppermute | solution.py:227
  27.8 6.5 %collective-permute-done.1 = f32[2,768]{0,1:T(8,128)} collective-permute-done((f32[2,768]{0,1:T(8,128)}, f32[2,768]{0,1:T(8,128)}, u32[]{:S(2)}, u32[]{:S(2)}) %collective-permute-start.1) | collective-permute-done | bytes 6176 | tf_op jit(solution)/shard_map/ppermute | solution.py:141
  34.3 2.2 %bitcast_select_fusion.1 = (f32[2,768]{0,1:T(8,128)}, f32[2,768]{0,1:T(8,128)}) fusion(f32[2,768]{0,1:T(8,128)} %collective-permute-done.1, f32[768,4]{1,0:T(8,128)} %copy-done.1, s32[]{:T(128)S(6)} %select_n.171, pred[]{:T(512)S(6)} %eq.11), kind=kLoop, calls=%fused_computation.54 | loop fusion | flops 3072 | bytes 24581 | tf_op jit(solution)/shard_map/jit(_where)/select_n | solution.py:214
  36.5 1.7 %copy.16 = f32[2,768]{1,0:T(2,128)} copy(f32[2,768]{0,1:T(8,128)} %get-tuple-element.70) | data formatting | bytes 12288 | tf_op jit(solution)/shard_map/jit(_where)/select_n | solution.py:214
  38.2 1.7 %copy.17 = f32[2,768]{1,0:T(2,128)} copy(f32[2,768]{0,1:T(8,128)} %get-tuple-element.71) | data formatting | bytes 12288 | tf_op jit(solution)/shard_map/jit(_where)/select_n | solution.py:214
  40.7 1.9 %collective-permute-done.5.refs_3_ = bf16[768,256]{1,0:T(8,128)(2,1)S(1)} collective-permute-done((bf16[768,256]{1,0:T(8,128)(2,1)}, bf16[768,256]{1,0:T(8,128)(2,1)S(1)}, u32[]{:S(2)}, u32[]{:S(2)}) %collective-permute-start.5) | collective-permute-done | bytes 393248 | tf_op jit(solution)/shard_map/ppermute | solution.py:141
  43.0 1.6 %collective-permute-start.8 = (bf16[768,256]{1,0:T(8,128)(2,1)S(1)}, bf16[768,256]{1,0:T(8,128)(2,1)S(1)}, u32[]{:S(2)}, u32[]{:S(2)}) collective-permute-start(bf16[768,256]{1,0:T(8,128)(2,1)S(1)} %collective-permute-done.5.refs_3_), channel_id=1, source_target_pairs={{0,8},{4,28},{8,16},{12,4},{16,24},{20,12},{24,0},{28,20},{1,9},{5... | collective-permute-start | bytes 1179656 | tf_op jit(solution)/shard_map/ppermute | solution.py:227
  44.6 6.5 %collective-permute-done.2.refs_1_ = bf16[768,256]{1,0:T(8,128)(2,1)S(1)} collective-permute-done((bf16[768,256]{1,0:T(8,128)(2,1)}, bf16[768,256]{1,0:T(8,128)(2,1)S(1)}, u32[]{:S(2)}, u32[]{:S(2)}) %collective-permute-start.2) | collective-permute-done | bytes 393248 | tf_op jit(solution)/shard_map/ppermute | solution.py:141
  51.0 10.2 %shard_map.82 = (bf16[2,384,128]{2,1,0:T(8,128)(2,1)S(1)}, bf16[2,384,128]{2,1,0:T(8,128)(2,1)S(1)}, f32[2,384,256]{2,1,0:T(8,128)S(1)}, f32[2,384,256]{2,1,0:T(...) custom-call(s32[16]{0:T(128)S(1)} %and_select_fusion.slots_ref, s32[4]{0:T(128)S(1)} %gather_fusion.1, ...), custom_call_target="tpu_custom_call" | custom-call | flops 6039797760 | bytes 5898240 | tf_op jit(solution)/shard_map/pallas_call | solution.py:111
  61.2 1.5 %collective-permute-start.12 = (bf16[2,384,256]{2,1,0:T(8,128)(2,1)S(1)}, bf16[2,384,256]{2,1,0:T(8,128)(2,1)S(1)}, u32[]{:S(2)}, u32[]{:S(2)}) collective-permute-start(bf16[2,384,256]{2,1,0:T(8,128)(2,1)S(1)} %get-tuple-element.41), channel_id=1, source_target_pairs={{0,24},{4,12},{8,0},{12,20},{16,8},{20,28},{24,16},{28,4},{1,25},{... | collective-permute-start | bytes 1179656 | tf_op jit(solution)/shard_map/ppermute | solution.py:227
  63.4 9.7 %shard_map.83 = (bf16[2,384,128]{2,1,0:T(8,128)(2,1)S(1)}, bf16[2,384,128]{2,1,0:T(8,128)(2,1)S(1)}, f32[2,384,256]{2,1,0:T(8,128)S(1)}, f32[2,384,256]{2,1,0:T(...) custom-call(s32[16]{0:T(128)S(1)} %and_select_fusion.slots_ref, s32[4]{0:T(128)S(1)} %gather_fusion.1, ...), custom_call_target="tpu_custom_call" | custom-call | flops 6039797760 | bytes 5898240 | tf_op jit(solution)/shard_map/pallas_call | solution.py:111
  73.1 4.4 %collective-permute-start.14 = (bf16[384,256]{1,0:T(8,128)(2,1)S(1)}, bf16[384,256]{1,0:T(8,128)(2,1)S(1)}, u32[]{:S(2)}, u32[]{:S(2)}) collective-permute-start(bf16[384,256]{1,0:T(8,128)(2,1)S(1)} %get-tuple-element.89), channel_id=1, source_target_pairs={{0,24},{4,12},{8,0},{12,20},{16,8},{20,28},{24,16},{28,4},{1,25},{... | collective-permute-start | bytes 589832 | tf_op jit(solution)/shard_map/ppermute | solution.py:227
  77.8 2.1 %collective-permute-done.10 = bf16[2,384,256]{2,1,0:T(8,128)(2,1)S(1)} collective-permute-done((bf16[2,384,256]{2,1,0:T(8,128)(2,1)S(1)}, bf16[2,384,256]{2,1,0:T(8,128)(2,1)S(1)}, u32[]{:S(2)}, u32[]{:S(2)}) %collective-permute-start.10) | collective-permute-done | bytes 393248 | tf_op jit(solution)/shard_map/ppermute | solution.py:227
  80.1 1.5 %collective-permute-start.9 = (bf16[2,384,256]{2,1,0:T(8,128)(2,1)S(1)}, bf16[2,384,256]{2,1,0:T(8,128)(2,1)S(1)}, u32[]{:S(2)}, u32[]{:S(2)}) collective-permute-start(bf16[2,384,256]{2,1,0:T(8,128)(2,1)S(1)} %pad_maximum_fusion.15), channel_id=1, source_target_pairs={{0,4},{4,0},{8,12},{12,8},{16,20},{20,16},{24,28},{28,24},{1,5},{5... | collective-permute-start | bytes 1179656 | tf_op jit(solution)/shard_map/ppermute | solution.py:141
  81.6 2.0 %collective-permute-done.14 = bf16[384,256]{1,0:T(8,128)(2,1)S(1)} collective-permute-done((bf16[384,256]{1,0:T(8,128)(2,1)S(1)}, bf16[384,256]{1,0:T(8,128)(2,1)S(1)}, u32[]{:S(2)}, u32[]{:S(2)}) %collective-permute-start.14) | collective-permute-done | bytes 196640 | tf_op jit(solution)/shard_map/ppermute | solution.py:227
  83.6 3.5 %collective-permute-start.20 = (bf16[384,256]{1,0:T(8,128)(2,1)S(1)}, bf16[384,256]{1,0:T(8,128)(2,1)S(1)}, u32[]{:S(2)}, u32[]{:S(2)}) collective-permute-start(bf16[384,256]{1,0:T(8,128)(2,1)S(1)} %get-tuple-element.45), channel_id=1, source_target_pairs={{0,24},{4,12},{8,0},{12,20},{16,8},{20,28},{24,16},{28,4},{1,25},{... | collective-permute-start | bytes 589832 | tf_op jit(solution)/shard_map/ppermute | solution.py:227
  89.2 3.7 %collective-permute-done.20 = bf16[384,256]{1,0:T(8,128)(2,1)S(1)} collective-permute-done((bf16[384,256]{1,0:T(8,128)(2,1)S(1)}, bf16[384,256]{1,0:T(8,128)(2,1)S(1)}, u32[]{:S(2)}, u32[]{:S(2)}) %collective-permute-start.20) | collective-permute-done | bytes 196640 | tf_op jit(solution)/shard_map/ppermute | solution.py:227
  93.0 1.8 %collective-permute-start.15 = (bf16[384,256]{1,0:T(8,128)(2,1)S(1)}, bf16[384,256]{1,0:T(8,128)(2,1)S(1)}, u32[]{:S(2)}, u32[]{:S(2)}) collective-permute-start(bf16[384,256]{1,0:T(8,128)(2,1)S(1)} %get-tuple-element.53), channel_id=1, source_target_pairs={{0,4},{4,0},{8,12},{12,8},{16,20},{20,16},{24,28},{28,24},{1,5},{5... | collective-permute-start | bytes 589832 | tf_op jit(solution)/shard_map/ppermute | solution.py:141
  96.1 4.8 %collective-permute-done.15 = bf16[384,256]{1,0:T(8,128)(2,1)S(1)} collective-permute-done((bf16[384,256]{1,0:T(8,128)(2,1)S(1)}, bf16[384,256]{1,0:T(8,128)(2,1)S(1)}, u32[]{:S(2)}, u32[]{:S(2)}) %collective-permute-start.15) | collective-permute-done | bytes 196640 | tf_op jit(solution)/shard_map/ppermute | solution.py:141
  101.2 2.0 %fusion.23 = bf16[384,1536]{1,0:T(8,128)(2,1)S(1)} fusion(bf16[3,512,3072]{2,1,0:T(8,128)(2,1)S(1)} %bitcast.93, s32[]{:T(128)S(6)} %select_n.190, bf16[1,384,512]{2,1,0:T(8,128)(2,1)S(1)} %maximum_bitcast_fusion.2, bf16[1,384,512]{2,1,0:T(8,128)(2,1)S(1)} %maximum_bitcast_fusion.1, bf16[1,384,512]{2,1,0:T(8,128)(2,1)S(1)} %maximum_bitcast_fusion), kind=kOutput, calls=%fused_computation.15 | convolution fusion | flops 1813708800 | bytes 7077892 | tf_op jit(solution)/shard_map/cik,ckm->im/dot_general | solution.py:157
  103.4 2.0 %fusion.29 = bf16[384,1536]{1,0:T(8,128)(2,1)S(1)} fusion(bf16[3,512,3072]{2,1,0:T(8,128)(2,1)S(1)} %bitcast.93, s32[]{:T(128)S(6)} %select_n.186, bf16[1,384,512]{2,1,0:T(8,128)(2,1)S(1)} %maximum_bitcast_fusion.2, bf16[1,384,512]{2,1,0:T(8,128)(2,1)S(1)} %maximum_bitcast_fusion.1, bf16[1,384,512]{2,1,0:T(8,128)(2,1)S(1)} %maximum_bitcast_fusion), kind=kOutput, calls=%fused_computation.17 | convolution fusion | flops 1813708800 | bytes 7077892 | tf_op jit(solution)/shard_map/cik,ckm->im/dot_general | solution.py:157
  106.3 2.0 %fusion.20 = bf16[384,1536]{1,0:T(8,128)(2,1)S(1)} fusion(bf16[3,512,3072]{2,1,0:T(8,128)(2,1)S(1)} %bitcast.93, s32[]{:T(128)S(6)} %select_n.190, bf16[1,384,512]{2,1,0:T(8,128)(2,1)S(1)} %maximum_bitcast_fusion.5, bf16[1,384,512]{2,1,0:T(8,128)(2,1)S(1)} %maximum_bitcast_fusion.4, bf16[1,384,512]{2,1,0:T(8,128)(2,1)S(1)} %maximum_bitcast_fusion.3), kind=kOutput, calls=%fused_computation.14 | convolution fusion | flops 1813708800 | bytes 7077892 | tf_op jit(solution)/shard_map/cik,ckm->im/dot_general | solution.py:157
  108.7 1.6 %collective-permute-start.18 = (bf16[384,768]{1,0:T(8,128)(2,1)S(1)}, bf16[384,768]{1,0:T(8,128)(2,1)S(1)}, u32[]{:S(2)}, u32[]{:S(2)}) collective-permute-start(bf16[384,768]{1,0:T(8,128)(2,1)S(1)} %add_convert_fusion.3), channel_id=1, source_target_pairs={{0,2},{1,3},{2,0},{3,1},{4,6},{5,7},{6,4},{7,5},{8,10},{9,11},{10,... | collective-permute-start | bytes 1769480 | tf_op jit(solution)/shard_map/ppermute | solution.py:141
  110.3 2.0 %fusion.26 = bf16[384,1536]{1,0:T(8,128)(2,1)S(1)} fusion(bf16[3,512,3072]{2,1,0:T(8,128)(2,1)S(1)} %bitcast.93, s32[]{:T(128)S(6)} %select_n.186, bf16[1,384,512]{2,1,0:T(8,128)(2,1)S(1)} %maximum_bitcast_fusion.5, bf16[1,384,512]{2,1,0:T(8,128)(2,1)S(1)} %maximum_bitcast_fusion.4, bf16[1,384,512]{2,1,0:T(8,128)(2,1)S(1)} %maximum_bitcast_fusion.3), kind=kOutput, calls=%fused_computation.16 | convolution fusion | flops 1813708800 | bytes 7077892 | tf_op jit(solution)/shard_map/cik,ckm->im/dot_general | solution.py:157
  112.8 11.7 %collective-permute-done.18 = bf16[384,768]{1,0:T(8,128)(2,1)S(1)} collective-permute-done((bf16[384,768]{1,0:T(8,128)(2,1)S(1)}, bf16[384,768]{1,0:T(8,128)(2,1)S(1)}, u32[]{:S(2)}, u32[]{:S(2)}) %collective-permute-start.18) | collective-permute-done | bytes 589856 | tf_op jit(solution)/shard_map/ppermute | solution.py:141
  126.0 13.4 %collective-permute-done.24 = bf16[384,768]{1,0:T(8,128)(2,1)S(1)} collective-permute-done((bf16[384,768]{1,0:T(8,128)(2,1)S(1)}, bf16[384,768]{1,0:T(8,128)(2,1)S(1)}, u32[]{:S(2)}, u32[]{:S(2)}) %collective-permute-start.24) | collective-permute-done | bytes 589856 | tf_op jit(solution)/shard_map/ppermute | solution.py:141
  (114 shorter events, 23.1 us)
Async XLA Ops:
  0.0 23.0 %copy-start = (s32[16]{0:T(128)S(1)}, s32[16]{0:T(128)}, u32[]{:S(2)}) copy-start(s32[16]{0:T(128)} %param.15) | copy-start | bytes 196
  1.6 7.5 %copy-start.8 = (s32[16,4]{0,1:T(4,128)S(1)}, s32[16,4]{0,1:T(4,128)}, u32[]{:S(2)}) copy-start(s32[16,4]{0,1:T(4,128)} %param.14) | copy-start | bytes 772
  1.6 8.2 %copy-start.2 = (bf16[768,512]{1,0:T(8,128)(2,1)S(1)}, bf16[768,512]{1,0:T(8,128)(2,1)}, u32[]{:S(2)}) copy-start(bf16[768,512]{1,0:T(8,128)(2,1)} %param.12) | copy-start | bytes 2359300
  1.6 8.2 %copy-start.3 = (bf16[768,512]{1,0:T(8,128)(2,1)S(1)}, bf16[768,512]{1,0:T(8,128)(2,1)}, u32[]{:S(2)}) copy-start(bf16[768,512]{1,0:T(8,128)(2,1)} %param.8) | copy-start | bytes 2359300
  2.5 19.4 %collective-permute-start = (bf16[768,256]{1,0:T(8,128)(2,1)}, bf16[768,256]{1,0:T(8,128)(2,1)S(1)}, u32[]{:S(2)}, u32[]{:S(2)}) collective-permute-start(bf16[768,256]{1,0:T(8,128)(2,1)} %pad_maximum_fusion.9), channel_id=1, source_target_pairs={{0,4},{4,0},{8,12},{12,8},{16,20},{20,16},{24,28},{28,24},{1,5},{5... | collective-permute-start | bytes 1179656 | tf_op jit(solution)/shard_map/ppermute | solution.py:141
  5.5 20.3 %collective-permute-start.3 = (bf16[768,256]{1,0:T(8,128)(2,1)S(1)}, bf16[768,256]{1,0:T(8,128)(2,1)S(1)}, u32[]{:S(2)}, u32[]{:S(2)}) collective-permute-start(bf16[768,256]{1,0:T(8,128)(2,1)S(1)} %pad_maximum_fusion.11.refs_2_), channel_id=1, source_target_pairs={{0,24},{4,12},{8,0},{12,20},{16,8},{20,28},{24,16},{28,4},{1,25},{... | collective-permute-start | bytes 1179656 | tf_op jit(solution)/shard_map/ppermute | solution.py:227
  21.8 12.4 %collective-permute-start.1 = (f32[2,768]{0,1:T(8,128)}, f32[2,768]{0,1:T(8,128)}, u32[]{:S(2)}, u32[]{:S(2)}) collective-permute-start(f32[2,768]{0,1:T(8,128)} %dynamic-slice_bitcast_fusion), channel_id=1, source_target_pairs={{0,4},{4,0},{8,12},{12,8},{16,20},{20,16},{24,28},{28,24},{1,5},{5... | collective-permute-start | bytes 18440 | tf_op jit(solution)/shard_map/ppermute | solution.py:141
  23.7 18.9 %collective-permute-start.5 = (bf16[768,256]{1,0:T(8,128)(2,1)}, bf16[768,256]{1,0:T(8,128)(2,1)S(1)}, u32[]{:S(2)}, u32[]{:S(2)}) collective-permute-start(bf16[768,256]{1,0:T(8,128)(2,1)} %pad_maximum_fusion.8), channel_id=1, source_target_pairs={{0,4},{4,0},{8,12},{12,8},{16,20},{20,16},{24,28},{28,24},{1,5},{5... | collective-permute-start | bytes 1179656 | tf_op jit(solution)/shard_map/ppermute | solution.py:141
  25.8 37.6 %collective-permute-start.7 = (bf16[768,256]{1,0:T(8,128)(2,1)S(1)}, bf16[768,256]{1,0:T(8,128)(2,1)S(1)}, u32[]{:S(2)}, u32[]{:S(2)}) collective-permute-start(bf16[768,256]{1,0:T(8,128)(2,1)S(1)} %pad_maximum_fusion.14.refs_2_), channel_id=1, source_target_pairs={{0,24},{4,12},{8,0},{12,20},{16,8},{20,28},{24,16},{28,4},{1,25},{... | collective-permute-start | bytes 1179656 | tf_op jit(solution)/shard_map/ppermute | solution.py:227
  26.2 24.8 %collective-permute-start.2 = (bf16[768,256]{1,0:T(8,128)(2,1)}, bf16[768,256]{1,0:T(8,128)(2,1)S(1)}, u32[]{:S(2)}, u32[]{:S(2)}) collective-permute-start(bf16[768,256]{1,0:T(8,128)(2,1)} %pad_maximum_fusion.7), channel_id=1, source_target_pairs={{0,4},{4,0},{8,12},{12,8},{16,20},{20,16},{24,28},{28,24},{1,5},{5... | collective-permute-start | bytes 1179656 | tf_op jit(solution)/shard_map/ppermute | solution.py:141
  26.2 16.7 %collective-permute-start.4 = (bf16[768,256]{1,0:T(8,128)(2,1)S(1)}, bf16[768,256]{1,0:T(8,128)(2,1)}, u32[]{:S(2)}, u32[]{:S(2)}) collective-permute-start(bf16[768,256]{1,0:T(8,128)(2,1)S(1)} %collective-permute-done.refs_3_), channel_id=1, source_target_pairs={{0,8},{4,28},{8,16},{12,4},{16,24},{20,12},{24,0},{28,20},{1,9},{5... | collective-permute-start | bytes 1179656 | tf_op jit(solution)/shard_map/ppermute | solution.py:227
  42.6 20.7 %collective-permute-start.6 = (bf16[768,256]{1,0:T(8,128)(2,1)}, bf16[768,256]{1,0:T(8,128)(2,1)S(1)}, u32[]{:S(2)}, u32[]{:S(2)}) collective-permute-start(bf16[768,256]{1,0:T(8,128)(2,1)} %pad_maximum_fusion.13), channel_id=1, source_target_pairs={{0,4},{4,0},{8,12},{12,8},{16,20},{20,16},{24,28},{28,24},{1,5},{5... | collective-permute-start | bytes 1179656 | tf_op jit(solution)/shard_map/ppermute | solution.py:141
  43.0 20.4 %collective-permute-start.8 = (bf16[768,256]{1,0:T(8,128)(2,1)S(1)}, bf16[768,256]{1,0:T(8,128)(2,1)S(1)}, u32[]{:S(2)}, u32[]{:S(2)}) collective-permute-start(bf16[768,256]{1,0:T(8,128)(2,1)S(1)} %collective-permute-done.5.refs_3_), channel_id=1, source_target_pairs={{0,8},{4,28},{8,16},{12,4},{16,24},{20,12},{24,0},{28,20},{1,9},{5... | collective-permute-start | bytes 1179656 | tf_op jit(solution)/shard_map/ppermute | solution.py:227
  61.2 16.3 %collective-permute-start.12 = (bf16[2,384,256]{2,1,0:T(8,128)(2,1)S(1)}, bf16[2,384,256]{2,1,0:T(8,128)(2,1)S(1)}, u32[]{:S(2)}, u32[]{:S(2)}) collective-permute-start(bf16[2,384,256]{2,1,0:T(8,128)(2,1)S(1)} %get-tuple-element.41), channel_id=1, source_target_pairs={{0,24},{4,12},{8,0},{12,20},{16,8},{20,28},{24,16},{28,4},{1,25},{... | collective-permute-start | bytes 1179656 | tf_op jit(solution)/shard_map/ppermute | solution.py:227
  62.7 17.1 %collective-permute-start.10 = (bf16[2,384,256]{2,1,0:T(8,128)(2,1)S(1)}, bf16[2,384,256]{2,1,0:T(8,128)(2,1)S(1)}, u32[]{:S(2)}, u32[]{:S(2)}) collective-permute-start(bf16[2,384,256]{2,1,0:T(8,128)(2,1)S(1)} %get-tuple-element.37), channel_id=1, source_target_pairs={{0,8},{4,28},{8,16},{12,4},{16,24},{20,12},{24,0},{28,20},{1,9},{5... | collective-permute-start | bytes 1179656 | tf_op jit(solution)/shard_map/ppermute | solution.py:227
  63.3 37.8 %slice-start = ((s8[9437184]{0:T(1024)(128)(4,1)}), s8[1048576]{0:T(1024)(128)(4,1)S(1)}, s32[]{:S(2)}) async-start(s8[9437184]{0:T(1024)(128)(4,1)} %bitcast.92), calls=%async_computation | async-start | bytes 2097152
  63.4 37.8 %slice-start.1 = ((s8[9437184]{0:T(1024)(128)(4,1)}), s8[4194304]{0:T(1024)(128)(4,1)S(1)}, s32[]{:S(2)}) async-start(s8[9437184]{0:T(1024)(128)(4,1)} %bitcast.92), calls=%async_computation.1 | async-start | bytes 8388608
  73.1 10.5 %collective-permute-start.14 = (bf16[384,256]{1,0:T(8,128)(2,1)S(1)}, bf16[384,256]{1,0:T(8,128)(2,1)S(1)}, u32[]{:S(2)}, u32[]{:S(2)}) collective-permute-start(bf16[384,256]{1,0:T(8,128)(2,1)S(1)} %get-tuple-element.89), channel_id=1, source_target_pairs={{0,24},{4,12},{8,0},{12,20},{16,8},{20,28},{24,16},{28,4},{1,25},{... | collective-permute-start | bytes 589832 | tf_op jit(solution)/shard_map/ppermute | solution.py:227
  77.6 17.5 %collective-permute-start.13 = (bf16[2,384,256]{2,1,0:T(8,128)(2,1)S(1)}, bf16[2,384,256]{2,1,0:T(8,128)(2,1)S(1)}, u32[]{:S(2)}, u32[]{:S(2)}) collective-permute-start(bf16[2,384,256]{2,1,0:T(8,128)(2,1)S(1)} %add_convert_fusion.4), channel_id=1, source_target_pairs={{0,4},{4,0},{8,12},{12,8},{16,20},{20,16},{24,28},{28,24},{1,5},{5... | collective-permute-start | bytes 1179656 | tf_op jit(solution)/shard_map/ppermute | solution.py:141
  77.7 10.5 %collective-permute-start.11 = (bf16[384,256]{1,0:T(8,128)(2,1)S(1)}, bf16[384,256]{1,0:T(8,128)(2,1)S(1)}, u32[]{:S(2)}, u32[]{:S(2)}) collective-permute-start(bf16[384,256]{1,0:T(8,128)(2,1)S(1)} %get-tuple-element.85), channel_id=1, source_target_pairs={{0,8},{4,28},{8,16},{12,4},{16,24},{20,12},{24,0},{28,20},{1,9},{5... | collective-permute-start | bytes 589832 | tf_op jit(solution)/shard_map/ppermute | solution.py:227
  80.0 21.2 %slice-start.2 = ((s8[9437184]{0:T(1024)(128)(4,1)}), s8[4194304]{0:T(1024)(128)(4,1)S(1)}, s32[]{:S(2)}) async-start(s8[9437184]{0:T(1024)(128)(4,1)} %bitcast.92), calls=%async_computation.2 | async-start | bytes 8388608
  80.1 15.8 %collective-permute-start.9 = (bf16[2,384,256]{2,1,0:T(8,128)(2,1)S(1)}, bf16[2,384,256]{2,1,0:T(8,128)(2,1)S(1)}, u32[]{:S(2)}, u32[]{:S(2)}) collective-permute-start(bf16[2,384,256]{2,1,0:T(8,128)(2,1)S(1)} %pad_maximum_fusion.15), channel_id=1, source_target_pairs={{0,4},{4,0},{8,12},{12,8},{16,20},{20,16},{24,28},{28,24},{1,5},{5... | collective-permute-start | bytes 1179656 | tf_op jit(solution)/shard_map/ppermute | solution.py:141
  83.6 9.3 %collective-permute-start.20 = (bf16[384,256]{1,0:T(8,128)(2,1)S(1)}, bf16[384,256]{1,0:T(8,128)(2,1)S(1)}, u32[]{:S(2)}, u32[]{:S(2)}) collective-permute-start(bf16[384,256]{1,0:T(8,128)(2,1)S(1)} %get-tuple-element.45), channel_id=1, source_target_pairs={{0,24},{4,12},{8,0},{12,20},{16,8},{20,28},{24,16},{28,4},{1,25},{... | collective-permute-start | bytes 589832 | tf_op jit(solution)/shard_map/ppermute | solution.py:227
  88.2 7.5 %collective-permute-start.19 = (bf16[384,256]{1,0:T(8,128)(2,1)S(1)}, bf16[384,256]{1,0:T(8,128)(2,1)S(1)}, u32[]{:S(2)}, u32[]{:S(2)}) collective-permute-start(bf16[384,256]{1,0:T(8,128)(2,1)S(1)} %get-tuple-element.44), channel_id=1, source_target_pairs={{0,8},{4,28},{8,16},{12,4},{16,24},{20,12},{24,0},{28,20},{1,9},{5... | collective-permute-start | bytes 589832 | tf_op jit(solution)/shard_map/ppermute | solution.py:227
  93.0 7.9 %collective-permute-start.15 = (bf16[384,256]{1,0:T(8,128)(2,1)S(1)}, bf16[384,256]{1,0:T(8,128)(2,1)S(1)}, u32[]{:S(2)}, u32[]{:S(2)}) collective-permute-start(bf16[384,256]{1,0:T(8,128)(2,1)S(1)} %get-tuple-element.53), channel_id=1, source_target_pairs={{0,4},{4,0},{8,12},{12,8},{16,20},{20,16},{24,28},{28,24},{1,5},{5... | collective-permute-start | bytes 589832 | tf_op jit(solution)/shard_map/ppermute | solution.py:141
  94.8 11.3 %collective-permute-start.21 = (bf16[384,256]{1,0:T(8,128)(2,1)S(1)}, bf16[384,256]{1,0:T(8,128)(2,1)S(1)}, u32[]{:S(2)}, u32[]{:S(2)}) collective-permute-start(bf16[384,256]{1,0:T(8,128)(2,1)S(1)} %get-tuple-element.52), channel_id=1, source_target_pairs={{0,4},{4,0},{8,12},{12,8},{16,20},{20,16},{24,28},{28,24},{1,5},{5... | collective-permute-start | bytes 589832 | tf_op jit(solution)/shard_map/ppermute | solution.py:141
  103.3 5.2 %collective-permute-start.17 = (bf16[384,768]{1,0:T(8,128)(2,1)S(1)}, bf16[384,768]{1,0:T(8,128)(2,1)S(1)}, u32[]{:S(2)}, u32[]{:S(2)}) collective-permute-start(bf16[384,768]{1,0:T(8,128)(2,1)S(1)} %constant_dynamic-slice_fusion.2), channel_id=1, source_target_pairs={{0,1},{1,0},{2,3},{3,2},{4,5},{5,4},{6,7},{7,6},{8,9},{9,8},{10,11... | collective-permute-start | bytes 1769480 | tf_op jit(solution)/shard_map/ppermute | solution.py:141
  105.5 20.5 %collective-permute-start.16 = (bf16[384,768]{1,0:T(8,128)(2,1)S(1)}, bf16[384,768]{1,0:T(8,128)(2,1)S(1)}, u32[]{:S(2)}, u32[]{:S(2)}) collective-permute-start(bf16[384,768]{1,0:T(8,128)(2,1)S(1)} %constant_dynamic-slice_fusion.3), channel_id=1, source_target_pairs={{0,1},{1,0},{2,3},{3,2},{4,5},{5,4},{6,7},{7,6},{8,9},{9,8},{10,11... | collective-permute-start | bytes 1769480 | tf_op jit(solution)/shard_map/ppermute | solution.py:141
  108.4 4.2 %collective-permute-start.23 = (bf16[384,768]{1,0:T(8,128)(2,1)S(1)}, bf16[384,768]{1,0:T(8,128)(2,1)S(1)}, u32[]{:S(2)}, u32[]{:S(2)}) collective-permute-start(bf16[384,768]{1,0:T(8,128)(2,1)S(1)} %constant_dynamic-slice_fusion), channel_id=1, source_target_pairs={{0,1},{1,0},{2,3},{3,2},{4,5},{5,4},{6,7},{7,6},{8,9},{9,8},{10,11... | collective-permute-start | bytes 1769480 | tf_op jit(solution)/shard_map/ppermute | solution.py:141
  108.7 15.8 %collective-permute-start.18 = (bf16[384,768]{1,0:T(8,128)(2,1)S(1)}, bf16[384,768]{1,0:T(8,128)(2,1)S(1)}, u32[]{:S(2)}, u32[]{:S(2)}) collective-permute-start(bf16[384,768]{1,0:T(8,128)(2,1)S(1)} %add_convert_fusion.3), channel_id=1, source_target_pairs={{0,2},{1,3},{2,0},{3,1},{4,6},{5,7},{6,4},{7,5},{8,10},{9,11},{10,... | collective-permute-start | bytes 1769480 | tf_op jit(solution)/shard_map/ppermute | solution.py:141
  112.3 13.7 %collective-permute-start.22 = (bf16[384,768]{1,0:T(8,128)(2,1)S(1)}, bf16[384,768]{1,0:T(8,128)(2,1)S(1)}, u32[]{:S(2)}, u32[]{:S(2)}) collective-permute-start(bf16[384,768]{1,0:T(8,128)(2,1)S(1)} %constant_dynamic-slice_fusion.1), channel_id=1, source_target_pairs={{0,1},{1,0},{2,3},{3,2},{4,5},{5,4},{6,7},{7,6},{8,9},{9,8},{10,11... | collective-permute-start | bytes 1769480 | tf_op jit(solution)/shard_map/ppermute | solution.py:141
  124.5 14.9 %collective-permute-start.24 = (bf16[384,768]{1,0:T(8,128)(2,1)S(1)}, bf16[384,768]{1,0:T(8,128)(2,1)S(1)}, u32[]{:S(2)}, u32[]{:S(2)}) collective-permute-start(bf16[384,768]{1,0:T(8,128)(2,1)S(1)} %add_convert_fusion.1), channel_id=1, source_target_pairs={{0,2},{1,3},{2,0},{3,1},{4,6},{5,7},{6,4},{7,5},{8,10},{9,11},{10,... | collective-permute-start | bytes 1769480 | tf_op jit(solution)/shard_map/ppermute | solution.py:141
  (5 other events, 10.7 us)
